TPU v7x, 32 devices: a whole 2x2x4 slice. The times are simulated.
32 devices in a mesh: head: 4 (over y, core), seq: 8 (over z, x).
Axes of the slice: x: 2, y: 2, z: 4, core: 2. Of those that a mesh axis runs over, the one named last changes fastest.
Arguments:
- hidden_in: bfloat16 [8, 4, 640, 768], P('seq', 'head'), may hold values from -6 to 6
- norm1_gain: bfloat16 [768], P('head'), may hold values from 0.5 to 1.5
- w_query: bfloat16 [768, 768], P('head'), may hold values from -0.21875 to 0.21875
- w_key: bfloat16 [768, 768], P('head'), may hold values from -0.21875 to 0.21875
- w_value: bfloat16 [768, 768], P('head'), may hold values from -0.21875 to 0.21875
- w_out: bfloat16 [768, 768], P('head'), may hold values from -3 to 3
- rel_bias: bfloat16 [384], P('head'), may hold values from -4 to 4
- norm2_gain: bfloat16 [768], P('head'), may hold values from 0.5 to 1.5
- w_router: bfloat16 [768, 16], P('head'), may hold values from -0.15625 to 0.15625
- w_first: bfloat16 [16, 768, 3072], P('seq', 'head'), may hold values from -0.21875 to 0.21875
- w_second: bfloat16 [16, 3072, 768], P('seq', 'head'), may hold values from -0.21875 to 0.21875
- routes: int32 [8, 4, 640, 2], P('seq', 'head'), may hold values from 0 to 15, all different within a row; in each aligned block of 640 rows (0 to 639, 640 to 1279, ..., all dimensions but the last counted through in order) at most 160 rows name the same one
- priority: int32 [8, 4, 640, 2], P('seq', 'head'), may hold values from 0 to 40959, as said below
- segments: int32 [20480], replicated, may hold values from 0 to 3, as said below
- grad_out: bfloat16 [8, 4, 640, 768], P('seq', 'head'), may hold values from -6 to 6
Outputs:
- output: bfloat16 [8, 4, 640, 768], P('seq', 'head')
- grad_hidden: float32 [8, 4, 640, 768], P('seq', 'head')
- grad_norm1: float32 [768], P('head')
- grad_query: float32 [768, 768], P('head')
- grad_key: float32 [768, 768], P('head')
- grad_value: float32 [768, 768], P('head')
- grad_outproj: float32 [768, 768], P('head')
- grad_rel: float32 [384], P('head')
- grad_norm2: float32 [768], P('head')
- grad_router: float32 [768, 16], P('head')
- grad_first: float32 [16, 768, 3072], P('seq', 'head')
- grad_second: float32 [16, 3072, 768], P('seq', 'head')
Inputs may be any that keep to these rules, and one draw needn't show every extreme that they name: `routes`: each row names 2 different experts; in the rows of one device no expert is named more than 160 times. `priority`: every pair has its own number; the pairs of the rows of one device hold 1280 consecutive numbers. `segments`: document numbers never fall along the positions.
All inputs are finite; a program needn't handle non-finite values.
Results may differ from a plain program's by a relative error of at most 0.02.
Values may be sent and summed in bfloat16 or wider, within the bound.
No kernel may reach another device: no remote copies, remote signals or barrier semaphores. Data moves between devices by JAX's collectives and lax.ppermute only.
A program may use at most 320 MiB of HBM per device.

v0:
```python
import jax
import jax.numpy as jnp
from jax import lax
from jax.sharding import PartitionSpec as P

HEAD_DIM = 64
WINDOW = 1024
BUCKETS = 32


highest = lax.Precision.HIGHEST
epsilon = 1e-06
bfloat = jnp.bfloat16
single = jnp.float32


def from_behind(value, axis, steps):
    count = lax.axis_size(axis)
    initial, last = (max(0, -steps), min(count, count - steps))
    return lax.ppermute(value, axis, [(source, source + steps) for source in range(initial, last)])


def bucket_edges(window_len, bucket_count):
    middle = bucket_count // 2
    edge_list = []
    for number in range(1, bucket_count):
        if number < middle:
            edge_list.append(number)
        else:
            edge_list.append(int(middle * (window_len / middle) ** ((number - middle) / middle)))
    return edge_list


def rms_scale(values, gain_vec):
    return (
        values * lax.rsqrt(jnp.mean(values * values, axis=-1, keepdims=True) + epsilon) * gain_vec
    )


def route_gates(logits, route_rows):
    probability = jax.nn.softmax(logits, axis=-1)
    chosen = jnp.take_along_axis(probability, route_rows, axis=1)
    return chosen / jnp.sum(chosen, axis=-1, keepdims=True)


def per_device(
    hidden_in,
    norm1_gain,
    w_query,
    w_key,
    w_value,
    w_out,
    rel_bias,
    norm2_gain,
    w_router,
    w_first,
    w_second,
    routes,
    priority,
    segments,
    grad_out,
):
    head_count = lax.axis_size("head")
    token_rows = hidden_in.shape[2]
    model_width = hidden_in.shape[3]
    resid = hidden_in.reshape(token_rows, model_width).astype(single)
    route_rows = routes.reshape(token_rows, -1)
    top_count = route_rows.shape[1]
    pair_routes = route_rows.reshape(-1)
    pair_prio = priority.reshape(-1)
    expert_total = w_router.shape[1]
    expert_local = w_first.shape[0]
    slot_count = max(2, 4 * token_rows // expert_total)
    capacity = 5 * token_rows * head_count // (2 * expert_local)
    expert_ids = jnp.arange(expert_total, dtype=jnp.int32)
    pair_hot = (pair_routes[:, None] == expert_ids[None, :]).astype(jnp.int32)
    earlier = (pair_routes[:, None] == pair_routes[None, :]) & (
        pair_prio[None, :] < pair_prio[:, None]
    )
    local_rank = jnp.sum(earlier.astype(jnp.int32), axis=1)
    block_rank = (jnp.min(pair_prio) // (top_count * token_rows)).reshape(1)
    all_counts, all_ranks = (
        lax.all_gather(jnp.sum(pair_hot, axis=0)[None, :], ("head", "seq"), axis=0, tiled=True),
        lax.all_gather(block_rank, ("head", "seq"), axis=0, tiled=True),
    )
    ahead_mask = (all_ranks < block_rank[0]).astype(jnp.int32)
    offsets = jnp.sum(all_counts * ahead_mask[:, None], axis=0)
    global_rank = jnp.sum(pair_hot * offsets[None, :], axis=1) + local_rank
    kept_pair = global_rank < capacity
    slot_index = pair_routes * slot_count + local_rank
    kept_mat = kept_pair.reshape(token_rows, top_count).astype(single)
    gain_one, gain_two, query_w, key_w, value_w, out_w, router_w, first_w, second_w = (
        lax.all_gather(norm1_gain, "head", axis=0, tiled=True),
        lax.all_gather(norm2_gain, "head", axis=0, tiled=True),
        lax.all_gather(w_query, "head", axis=0, tiled=True),
        lax.all_gather(w_key, "head", axis=0, tiled=True),
        lax.all_gather(w_value, "head", axis=0, tiled=True),
        lax.all_gather(w_out, "head", axis=0, tiled=True),
        lax.all_gather(w_router, "head", axis=0, tiled=True),
        lax.all_gather(w_first, "head", axis=1, tiled=True),
        lax.all_gather(w_second, "head", axis=1, tiled=True),
    )
    gain_one_f = gain_one.astype(single)
    gain_two_f = gain_two.astype(single)
    normed = rms_scale(resid, gain_one_f).astype(bfloat)
    query_tok = jnp.dot(normed, query_w, preferred_element_type=single).astype(bfloat)
    key_tok = jnp.dot(normed, key_w, preferred_element_type=single).astype(bfloat)
    value_tok = jnp.dot(normed, value_w, preferred_element_type=single).astype(bfloat)
    query_h, key_h, value_h = (
        lax.all_to_all(query_tok, "head", split_axis=1, concat_axis=0, tiled=True),
        lax.all_to_all(key_tok, "head", split_axis=1, concat_axis=0, tiled=True),
        lax.all_to_all(value_tok, "head", split_axis=1, concat_axis=0, tiled=True),
    )
    block_len = query_h.shape[0]
    local_width = query_h.shape[1]
    head_dim = HEAD_DIM
    local_heads = local_width // head_dim
    sent_pair = (key_h, value_h)
    prev_key, prev_value = from_behind((sent_pair[0], sent_pair[1]), "seq", 1)
    prev_rows = prev_key.shape[0]
    keys_all = jnp.concatenate([prev_key, key_h], axis=0).reshape(-1, local_heads, head_dim)
    values_all = jnp.concatenate([prev_value, value_h], axis=0).reshape(-1, local_heads, head_dim)
    queries_all = query_h.reshape(block_len, local_heads, head_dim)
    query_rows = min(512, block_len)
    key_rows = WINDOW + query_rows
    blocks_count = block_len // query_rows
    distance = (
        WINDOW
        + jnp.arange(query_rows, dtype=jnp.int32)[:, None]
        - jnp.arange(key_rows, dtype=jnp.int32)[None, :]
    )
    allowed = (distance >= 0) & (distance < WINDOW)
    bucket = jnp.zeros(distance.shape, jnp.int32)
    for edge_value in bucket_edges(WINDOW, BUCKETS):
        bucket = bucket + (distance >= edge_value).astype(jnp.int32)
    bucket_hot = (
        bucket.reshape(-1)[:, None] == jnp.arange(BUCKETS, dtype=jnp.int32)[None, :]
    ).astype(single)
    table = rel_bias.astype(single).reshape(local_heads, BUCKETS)
    bias_all = (
        jnp.dot(bucket_hot, table.T, precision=highest)
        .reshape(query_rows, key_rows, local_heads)
        .transpose(2, 0, 1)
    )
    base_pos = lax.axis_index("seq") * block_len
    segs_pad = jnp.concatenate([jnp.full((WINDOW,), -1, jnp.int32), segments])
    factor = head_dim ** (-0.5)

    def scores_of(row_start):
        key_start = row_start + prev_rows - WINDOW
        query_blk = lax.dynamic_slice_in_dim(queries_all, row_start, query_rows, 0)
        key_blk = lax.dynamic_slice_in_dim(keys_all, key_start, key_rows, 0)
        value_blk = lax.dynamic_slice_in_dim(values_all, key_start, key_rows, 0)
        query_seg = lax.dynamic_slice_in_dim(segments, base_pos + row_start, query_rows, 0)
        key_seg = lax.dynamic_slice_in_dim(segs_pad, base_pos + row_start, key_rows, 0)
        usable = allowed & (query_seg[:, None] == key_seg[None, :])
        raw_scores = (
            jnp.einsum("qhe,khe->hqk", query_blk, key_blk, preferred_element_type=single) * factor
            + bias_all
        )
        return (jnp.where(usable[None], raw_scores, -1e30), query_blk, key_blk, value_blk)

    def forward_block(unused, row_start):
        scores, query_blk, key_blk, value_blk = scores_of(row_start)
        peak = jnp.max(scores, axis=-1, keepdims=True)
        expo = jnp.exp(scores - peak)
        row_total = jnp.sum(expo, axis=-1, keepdims=True)
        weights = (expo / row_total).astype(bfloat)
        attended = jnp.einsum(
            "hqk,khe->qhe", weights, value_blk, preferred_element_type=single
        ).astype(bfloat)
        return (unused, (attended, peak[..., 0] + jnp.log(row_total[..., 0])))

    starts = jnp.arange(blocks_count, dtype=jnp.int32) * query_rows
    _, (attended_all, logsum) = lax.scan(forward_block, None, starts)
    attended_h = attended_all.reshape(block_len, local_width)
    mixed_tok = lax.all_to_all(attended_h, "head", split_axis=0, concat_axis=1, tiled=True)
    middle = resid + jnp.dot(mixed_tok, out_w, preferred_element_type=single)
    normed_two = rms_scale(middle, gain_two_f).astype(bfloat)
    logits = jnp.dot(normed_two, router_w, preferred_element_type=single)
    gate_mat = route_gates(logits, route_rows)
    pair_rows = (
        jnp.broadcast_to(normed_two[:, None, :], (token_rows, top_count, model_width))
        * kept_mat[:, :, None].astype(bfloat)
    ).reshape(-1, model_width)
    send_rows = (
        jnp.zeros((expert_total * slot_count, model_width), bfloat)
        .at[slot_index]
        .set(pair_rows)
        .reshape(-1, expert_local, slot_count, model_width)
    )
    received = lax.all_to_all(send_rows, "seq", split_axis=0, concat_axis=0, tiled=True)
    pre_act = jnp.einsum("sxpd,xdf->sxpf", received, first_w, preferred_element_type=single)
    act_low = jax.nn.gelu(pre_act).astype(bfloat)
    result = jnp.einsum("sxpf,xfd->sxpd", act_low, second_w, preferred_element_type=single).astype(
        bfloat
    )
    returned = lax.all_to_all(result, "seq", split_axis=0, concat_axis=0, tiled=True)
    returned, received, pre_act = (returned, received, pre_act)
    expert_out = (
        returned.reshape(-1, model_width)[slot_index]
        .reshape(token_rows, top_count, model_width)
        .astype(single)
    )
    pair_weight = gate_mat * kept_mat
    final_out = middle + jnp.sum(pair_weight[:, :, None] * expert_out, axis=1)
    output = final_out.astype(bfloat).reshape(hidden_in.shape)
    cotangent = grad_out.reshape(token_rows, model_width).astype(single)
    dz_pair = (
        (pair_weight[:, :, None] * cotangent[:, None, :]).astype(bfloat).reshape(-1, model_width)
    )
    dgates = kept_mat * jnp.sum(expert_out * cotangent[:, None, :], axis=-1)
    dz_send = (
        jnp.zeros((expert_total * slot_count, model_width), bfloat)
        .at[slot_index]
        .set(dz_pair)
        .reshape(-1, expert_local, slot_count, model_width)
    )
    dz_recv = lax.all_to_all(dz_send, "seq", split_axis=0, concat_axis=0, tiled=True)
    dact = jnp.einsum("sxpd,xfd->sxpf", dz_recv, second_w, preferred_element_type=single)
    act_low = jax.nn.gelu(pre_act).astype(bfloat)
    _, gelu_back = jax.vjp(jax.nn.gelu, pre_act)
    dpre = gelu_back(dact)[0].astype(bfloat)
    drows = jnp.einsum("sxpf,xdf->sxpd", dpre, first_w, preferred_element_type=single).astype(
        bfloat
    )
    drows_back = lax.all_to_all(drows, "seq", split_axis=0, concat_axis=0, tiled=True)
    dpairs = (
        drows_back.reshape(-1, model_width)[slot_index]
        .astype(single)
        .reshape(token_rows, top_count, model_width)
    )
    _, gate_back = jax.vjp(lambda logit_vals: route_gates(logit_vals, route_rows), logits)
    dlogits = gate_back(dgates)[0].astype(bfloat)
    grad_router_full = jnp.einsum("td,te->de", normed_two, dlogits, preferred_element_type=single)
    dnormed_two = jnp.sum(dpairs, axis=1) + jnp.einsum(
        "te,de->td", dlogits, router_w, preferred_element_type=single
    )
    _, norm_two_back = jax.vjp(rms_scale, middle, gain_two_f)
    dmiddle_norm, grad_gain_two = norm_two_back(dnormed_two)
    dmiddle = cotangent + dmiddle_norm
    dattn = dmiddle.astype(bfloat)
    grad_outw_full = jnp.einsum("ta,td->ad", mixed_tok, dattn, preferred_element_type=single)
    dmixed_tok = jnp.einsum("td,ad->ta", dattn, out_w, preferred_element_type=single).astype(bfloat)
    dmixed_h = lax.all_to_all(dmixed_tok, "head", split_axis=1, concat_axis=0, tiled=True).reshape(
        block_len, local_heads, head_dim
    )

    def backward_block(accum, inputs):
        dkey_acc, dvalue_acc, dscore_sum = accum
        row_start, logsum_blk = inputs
        scores, query_blk, key_blk, value_blk = scores_of(row_start)
        probs_blk = jnp.exp(scores - logsum_blk[..., None])
        dout_blk = lax.dynamic_slice_in_dim(dmixed_h, row_start, query_rows, 0)
        dprobs = jnp.einsum("qhe,khe->hqk", dout_blk, value_blk, preferred_element_type=single)
        row_delta = jnp.sum(dprobs * probs_blk, axis=-1, keepdims=True)
        dscores = (probs_blk * (dprobs - row_delta)).astype(bfloat)
        dquery_blk = (
            jnp.einsum("hqk,khe->qhe", dscores, key_blk, preferred_element_type=single) * factor
        )
        dkey_blk = (
            jnp.einsum("hqk,qhe->khe", dscores, query_blk, preferred_element_type=single) * factor
        )
        dvalue_blk = jnp.einsum(
            "hqk,qhe->khe", probs_blk.astype(bfloat), dout_blk, preferred_element_type=single
        )
        key_start = row_start + prev_rows - WINDOW
        dkey_acc = lax.dynamic_update_slice_in_dim(
            dkey_acc,
            lax.dynamic_slice_in_dim(dkey_acc, key_start, key_rows, 0) + dkey_blk,
            key_start,
            0,
        )
        dvalue_acc = lax.dynamic_update_slice_in_dim(
            dvalue_acc,
            lax.dynamic_slice_in_dim(dvalue_acc, key_start, key_rows, 0) + dvalue_blk,
            key_start,
            0,
        )
        return ((dkey_acc, dvalue_acc, dscore_sum + dscores.astype(single)), dquery_blk)

    accum_init = (
        jnp.zeros((prev_rows + block_len, local_heads, head_dim), single),
        jnp.zeros((prev_rows + block_len, local_heads, head_dim), single),
        jnp.zeros((local_heads, query_rows, key_rows), single),
    )
    (dkey_acc, dvalue_acc, dscore_sum), dquery_all = lax.scan(
        backward_block, accum_init, (starts, logsum)
    )
    grad_rel_local = jnp.dot(
        dscore_sum.reshape(local_heads, -1), bucket_hot, precision=highest
    ).reshape(-1)
    dkey_next, dvalue_next = (
        from_behind(
            dkey_acc[prev_rows - WINDOW : prev_rows]
            .reshape(WINDOW, local_width)
            .astype(jnp.bfloat16),
            "seq",
            -1,
        ).astype(jnp.float32),
        from_behind(
            dvalue_acc[prev_rows - WINDOW : prev_rows]
            .reshape(WINDOW, local_width)
            .astype(jnp.bfloat16),
            "seq",
            -1,
        ).astype(jnp.float32),
    )
    dkey_own = (
        dkey_acc[prev_rows:].reshape(block_len, local_width).at[block_len - WINDOW :].add(dkey_next)
    )
    dvalue_own = (
        dvalue_acc[prev_rows:]
        .reshape(block_len, local_width)
        .at[block_len - WINDOW :]
        .add(dvalue_next)
    )
    dquery_h = dquery_all.reshape(block_len, local_width)
    dquery_tok, dkey_tok, dvalue_tok = (
        lax.all_to_all(dquery_h.astype(bfloat), "head", split_axis=0, concat_axis=1, tiled=True),
        lax.all_to_all(dkey_own.astype(bfloat), "head", split_axis=0, concat_axis=1, tiled=True),
        lax.all_to_all(dvalue_own.astype(bfloat), "head", split_axis=0, concat_axis=1, tiled=True),
    )
    grad_query_full = jnp.einsum("td,ta->da", normed, dquery_tok, preferred_element_type=single)
    grad_key_full = jnp.einsum("td,ta->da", normed, dkey_tok, preferred_element_type=single)
    grad_value_full = jnp.einsum("td,ta->da", normed, dvalue_tok, preferred_element_type=single)
    dnormed = jnp.einsum("ta,da->td", dquery_tok, query_w, preferred_element_type=single)
    dnormed = dnormed + jnp.einsum("ta,da->td", dkey_tok, key_w, preferred_element_type=single)
    dnormed = dnormed + jnp.einsum("ta,da->td", dvalue_tok, value_w, preferred_element_type=single)
    _, norm_one_back = jax.vjp(rms_scale, resid, gain_one_f)
    dresid_norm, grad_gain_one = norm_one_back(dnormed)
    grad_hidden = (dmiddle + dresid_norm).reshape(hidden_in.shape)
    grad_second_full = jnp.einsum("sxpf,sxpd->xfd", act_low, dz_recv, preferred_element_type=single)
    grad_first_full = jnp.einsum("sxpd,sxpf->xdf", received, dpre, preferred_element_type=single)
    (
        part_gain_one,
        part_gain_two,
        part_query,
        part_key,
        part_value,
        part_outw,
        part_router,
        grad_first,
        grad_second,
    ) = (
        lax.psum_scatter(
            grad_gain_one.astype(jnp.bfloat16), "head", scatter_dimension=0, tiled=True
        ).astype(jnp.float32),
        lax.psum_scatter(
            grad_gain_two.astype(jnp.bfloat16), "head", scatter_dimension=0, tiled=True
        ).astype(jnp.float32),
        lax.psum_scatter(
            grad_query_full.astype(jnp.bfloat16), "head", scatter_dimension=0, tiled=True
        ).astype(jnp.float32),
        lax.psum_scatter(
            grad_key_full.astype(jnp.bfloat16), "head", scatter_dimension=0, tiled=True
        ).astype(jnp.float32),
        lax.psum_scatter(
            grad_value_full.astype(jnp.bfloat16), "head", scatter_dimension=0, tiled=True
        ).astype(jnp.float32),
        lax.psum_scatter(
            grad_outw_full.astype(jnp.bfloat16), "head", scatter_dimension=0, tiled=True
        ).astype(jnp.float32),
        lax.psum_scatter(
            grad_router_full.astype(jnp.bfloat16), "head", scatter_dimension=0, tiled=True
        ).astype(jnp.float32),
        lax.psum_scatter(
            grad_first_full.astype(jnp.bfloat16), "head", scatter_dimension=1, tiled=True
        ).astype(jnp.float32),
        lax.psum_scatter(
            grad_second_full.astype(jnp.bfloat16), "head", scatter_dimension=1, tiled=True
        ).astype(jnp.float32),
    )
    (
        grad_norm1,
        grad_norm2,
        grad_query,
        grad_key,
        grad_value,
        grad_outproj,
        grad_router,
        grad_rel,
    ) = (
        lax.psum(part_gain_one.astype(jnp.bfloat16), "seq").astype(jnp.float32),
        lax.psum(part_gain_two.astype(jnp.bfloat16), "seq").astype(jnp.float32),
        lax.psum(part_query.astype(jnp.bfloat16), "seq").astype(jnp.float32),
        lax.psum(part_key.astype(jnp.bfloat16), "seq").astype(jnp.float32),
        lax.psum(part_value.astype(jnp.bfloat16), "seq").astype(jnp.float32),
        lax.psum(part_outw.astype(jnp.bfloat16), "seq").astype(jnp.float32),
        lax.psum(part_router.astype(jnp.bfloat16), "seq").astype(jnp.float32),
        lax.psum(grad_rel_local.astype(jnp.bfloat16), "seq").astype(jnp.float32),
    )
    return (
        output,
        grad_hidden,
        grad_norm1,
        grad_query,
        grad_key,
        grad_value,
        grad_outproj,
        grad_rel,
        grad_norm2,
        grad_router,
        grad_first,
        grad_second,
    )


def solution(mesh):
    return jax.shard_map(
        per_device,
        mesh=mesh,
        in_specs=(
            P("seq", "head", None, None),
            P("head"),
            P("head", None),
            P("head", None),
            P("head", None),
            P("head", None),
            P("head"),
            P("head"),
            P("head", None),
            P("seq", "head", None),
            P("seq", "head", None),
            P("seq", "head", None, None),
            P("seq", "head", None, None),
            P(),
            P("seq", "head", None, None),
        ),
        out_specs=(
            P("seq", "head", None, None),
            P("seq", "head", None, None),
            P("head"),
            P("head", None),
            P("head", None),
            P("head", None),
            P("head", None),
            P("head"),
            P("head"),
            P("head", None),
            P("seq", "head", None),
            P("seq", "head", None),
        ),
        check_vma=False,
    )
```

profile of v0, /device:TPU:0, one launch (start us, length us, event | category | flops | bytes accessed | tf_op | source)
XLA Modules:
  0.0 1508.0 jit_solution(17005978289567050110)
XLA Ops:
  37.5 17.7 %all-gather.13.cloned.1.call-done = bf16[768,768]{1,0:T(8,128)(2,1)} async-done(((bf16[192,768]{1,0:T(8,128)(2,1)}), bf16[768,768]{1,0:T(8,128)(2,1)}) %all-gather.13.cloned.1.call-update) | async-done | bytes 1179664 | tf_op jit(solution)/shard_map/all_gather | solution.py:96
  95.6 18.0 %fusion.66 = f32[3,512,1536]{2,0,1:T(4,128)} fusion(bf16[3,32,1]{1,0,2:T(4,128)(2,1)S(1)} %reshape.917, s32[512,1536]{1,0:T(8,128)} %get-tuple-element.922), kind=kOutput, calls=%fused_computation.87 | convolution fusion | flops 176160768 | bytes 12583104 | tf_op jit(solution)/shard_map/dot_general | solution.py:141
  140.0 45.0 %all-reduce.7 = (s32[512]{0:T(512)S(1)}, s32[32]{0:T(128)S(1)}) all-reduce(s32[512]{0:T(512)S(1)} %dynamic-update-slice.7, s32[32]{0:T(128)S(1)} %dynamic-update-slice.8), channel_id=2, replica_groups=mesh['head'=4,'seq'=8] {'head','seq'}, use_global_device_ids=true, to_apply=%add.2 | all-reduce | flops 544 | bytes 4352
  212.1 82.6 %while.40 = (s32[]{:T(128)}, bf16[5,512,3,64]{1,3,2,0:T(8,128)(2,1)}, f32[5,3,512]{2,1,0:T(4,128)}, s32[5]{0:T(128)S(1)}, bf16[5120,3,64]{0,2,1:T(8,128)(2,1)S(1...) while((s32[]{:T(128)}, ...), condition=%wide.region_4.5_spmd.clone, body=%wide.region_1.4_spmd.clone.sunk | while | flops 630028800 | bytes 40976756 | solution.py:175
  372.0 16.0 %scatter_custom_fusion.1 = bf16[2560,768]{1,0:T(8,128)(2,1)} fusion(s32[1280]{0:T(1024)S(1)} %fusion.171, f32[1280,768]{1,0:T(8,128)} %mul.404, f32[1280]{0:T(1024)S(1)} %get-tuple-element.893, bf16[]{:T(256)} %constant.347.clone.1), kind=kCustom, calls=%fused_computation.178 | custom fusion | flops 1966080 | bytes 7872514 | tf_op jit(solution)/shard_map/scatter | solution.py:216
  388.1 60.9 %all-to-all-done.4 = bf16[8,2,160,768]{3,2,1,0:T(8,128)(2,1)} async-done(((bf16[8,2,160,768]{3,2,1,0:T(8,128)(2,1)}), bf16[8,2,160,768]{3,2,1,0:T(8,128)(2,1)}, u32[]{:S(2)}, u32[]{:S(2)}) %all-to-all-start.4) | async-done | bytes 3932192 | tf_op jit(solution)/shard_map/all_to_all | solution.py:192
  453.7 22.3 %fusion.71 = f32[2,8,160,3072]{3,2,1,0:T(8,128)} fusion(bf16[2,768,3072]{2,1,0:T(8,128)(2,1)} %all-gather.17.cloned.1.call-done, bf16[8,2,160,768]{3,2,1,0:T(8,128)(2,1)} %all-to-all-done.4), kind=kOutput, calls=%fused_computation.90 | convolution fusion | flops 12079595520 | bytes 44826624 | tf_op jit(solution)/shard_map/sxpd,xdf->sxpf/dot_general | solution.py:193
  476.1 23.8 %convert_bitcast_fusion.1 = bf16[8,2,160,768]{3,2,0,1:T(8,128)(2,1)} fusion(bf16[2,3072,768]{2,1,0:T(8,128)(2,1)} %all-gather.19.cloned.1.call-done, f32[2,8,160,3072]{3,2,1,0:T(8,128)} %fusion.71), kind=kOutput, calls=%fused_computation.102 | convolution fusion | flops 12152340480 | bytes 44826624 | tf_op jit(solution)/shard_map/sxpf,xfd->sxpd/dot_general | solution.py:195
  504.2 36.4 %all-to-all-done.6 = bf16[8,2,160,768]{3,2,1,0:T(8,128)(2,1)} async-done(((bf16[8,2,160,768]{3,2,1,0:T(8,128)(2,1)}), bf16[8,2,160,768]{3,2,1,0:T(8,128)(2,1)}, u32[]{:S(2)}, u32[]{:S(2)}) %all-to-all-start.6) | async-done | bytes 3932192 | tf_op jit(solution)/shard_map/all_to_all | solution.py:219
  545.5 36.6 %fusion.59 = bf16[8,2,160,3072]{3,2,0,1:T(8,128)(2,1)} fusion(f32[2,8,160,3072]{3,2,1,0:T(8,128)} %fusion.71, bf16[2,3072,768]{2,1,0:T(8,128)(2,1)} %all-gather.19.cloned.1.call-done, bf16[8,2,160,768]{3,2,1,0:T(8,128)(2,1)} %all-to-all-done.6), kind=kOutput, calls=%fused_computation.75 | convolution fusion | flops 12236881920 | bytes 60555264 | tf_op jit(solution)/shard_map/sxpd,xfd->sxpf/dot_general | solution.py:220
  582.1 19.8 %convert_bitcast_fusion = bf16[8,2,160,768]{3,2,0,1:T(8,128)(2,1)} fusion(bf16[8,2,160,3072]{3,2,0,1:T(8,128)(2,1)} %fusion.59, bf16[2,768,3072]{2,1,0:T(8,128)(2,1)} %all-gather.17.cloned.1.call-done), kind=kOutput, calls=%fused_computation.99 | convolution fusion | flops 12081561600 | bytes 29097984 | tf_op jit(solution)/shard_map/sxpf,xdf->sxpd/dot_general | solution.py:224
  606.2 26.3 %all-to-all-done.5 = bf16[8,2,160,768]{3,2,1,0:T(8,128)(2,1)} async-done(((bf16[8,2,160,768]{3,2,1,0:T(8,128)(2,1)}), bf16[8,2,160,768]{3,2,1,0:T(8,128)(2,1)}, u32[]{:S(2)}, u32[]{:S(2)}) %all-to-all-start.5) | async-done | bytes 3932192 | tf_op jit(solution)/shard_map/all_to_all | solution.py:198
  670.2 53.9 %all-to-all-done.7 = bf16[8,2,160,768]{3,2,1,0:T(8,128)(2,1)} async-done(((bf16[8,2,160,768]{3,2,1,0:T(8,128)(2,1)}), bf16[8,2,160,768]{3,2,1,0:T(8,128)(2,1)}, u32[]{:S(2)}, u32[]{:S(2)}) %all-to-all-start.7) | async-done | bytes 3932192 | tf_op jit(solution)/shard_map/all_to_all | solution.py:227
  775.1 282.8 %while.41 = (s32[]{:T(128)}, f32[5120,3,64]{0,2,1:T(8,128)}, f32[5120,3,64]{0,2,1:T(8,128)}, f32[3,512,1536]{2,1,0:T(8,128)}, bf16[5,512,3,64]{1,3,2,0:T(8,128)(...) while((s32[]{:T(128)}, f32[5120,3,64]{0,2,1:T(8,128)}, ...), condition=%wide.region_25.26_spmd.clone, body=%wide.region_23.25_spmd.clone.sunk | while | flops 1546320384 | bytes 179167760 | solution.py:287
  1060.7 16.3 %all_to_all.163 = bf16[4,640,192]{1,2,0:T(8,128)(2,1)S(1)} all-to-all(bf16[4,640,192]{1,2,0:T(8,128)(2,1)S(1)} %copy.141), channel_id=1, replica_groups=mesh['head'=4,'seq'=8] {'head'}, dimensions={0} | all-to-all | bytes 1966080 | tf_op jit(solution)/shard_map/all_to_all | solution.py:320
  1094.5 19.4 %all_to_all.164 = bf16[4,640,192]{1,2,0:T(8,128)(2,1)S(1)} all-to-all(bf16[4,640,192]{1,2,0:T(8,128)(2,1)S(1)} %bitcast.303), channel_id=1, replica_groups=mesh['head'=4,'seq'=8] {'head'}, dimensions={0} | all-to-all | bytes 1966080 | tf_op jit(solution)/shard_map/all_to_all | solution.py:321
  1131.3 21.4 %all_to_all.165 = bf16[4,640,192]{1,2,0:T(8,128)(2,1)S(1)} all-to-all(bf16[4,640,192]{1,2,0:T(8,128)(2,1)S(1)} %bitcast.304), channel_id=1, replica_groups=mesh['head'=4,'seq'=8] {'head'}, dimensions={0} | all-to-all | bytes 1966080 | tf_op jit(solution)/shard_map/all_to_all | solution.py:322
  1157.3 17.5 %fusion.117 = (s32[512,1536]{1,0:T(8,128)}, s32[512,1536]{1,0:T(8,128)}, s32[512,1536]{1,0:T(8,128)}, s32[512,1536]{1,0:T(8,128)}, s32[512,1536]{1,0:T(8,128)}, ...) fusion(s32[512]{0:T(512)S(1)} %get-tuple-element.1307), kind=kLoop, calls=%fused_computation.142 | loop fusion | flops 29097984 | bytes 56625152 | tf_op jit(solution)/shard_map/convert_element_type | solution.py:135
  1255.0 27.6 %bitcast_convert_fusion = bf16[2,3072,768]{2,1,0:T(8,128)(2,1)} fusion(bf16[8,2,160,768]{3,2,1,0:T(8,128)(2,1)} %all-to-all-done.6, f32[2,8,160,3072]{3,2,1,0:T(8,128)} %fusion.71), kind=kOutput, calls=%fused_computation.83 | convolution fusion | flops 12155092992 | bytes 44826624 | tf_op jit(solution)/shard_map/sxpf,sxpd->xfd/dot_general | solution.py:333
  1282.7 20.1 %add_add_fusion = s32[786432]{0:T(1024)S(1)} fusion(s32[786432]{0:T(1024)} %reshape.843, s32[786432]{0:T(1024)} %reshape.842, s32[786432]{0:T(1024)} %reshape.841, s32[786432]{0:T(1024)} %reshape.840, s32[786432]{0:T(1024)} %reshape.839, s32[786432]{0:T(1024)} %reshape.838, s32[786432]{0:T(1024)} %reshape.837, s32[786432]{0:T(1024)} %reshape.836, ...), kind=kLoop, calls=%fused_computation.105 | loop fusion | flops 14155776 | bytes 62914560 | tf_op jit(solution)/shard_map/add | solution.py:135
  1302.8 19.3 %bitcast_convert_fusion.1 = bf16[2,768,3072]{2,1,0:T(8,128)(2,1)} fusion(bf16[8,2,160,768]{3,2,1,0:T(8,128)(2,1)} %all-to-all-done.4, bf16[8,2,160,3072]{3,2,0,1:T(8,128)(2,1)} %fusion.59), kind=kOutput, calls=%fused_computation.84 | convolution fusion | flops 12084314112 | bytes 29097984 | tf_op jit(solution)/shard_map/sxpd,sxpf->xdf/dot_general | solution.py:334
  1353.8 45.4 %fusion.159 = bf16[3,32]{1,0:T(4,128)(2,1)S(1)} fusion(f32[3,786432]{1,0:T(4,128)} %bitcast.289, pred[786432,32]{0,1:T(32,128)(4,1)} %iota_compare_fusion.8), kind=kOutput, calls=%fused_computation.202 | convolution fusion | flops 905969792 | bytes 34603200 | tf_op jit(solution)/shard_map/dot_general | solution.py:290
  1412.7 21.0 %all-reduce.8 = (bf16[192]{0:T(256)(128)(2,1)S(1)}, bf16[96]{0:T(256)(128)(2,1)S(1)}, bf16[192]{0:T(256)(128)(2,1)S(1)}, bf16[192,16]{0,1:T(8,128)(2,1)S(1)}) all-reduce(bf16[192]{0:T(256)(128)(2,1)S(1)} %dynamic-slice.19, bf16[96]{0:T(256)(128)(2,1)S(1)} %convert_element_type.820, ...), channel_id=1, replica_groups=mesh['head'=4,'seq'=8] {'seq'}, use_global_device_ids=true, to_apply=%region_29.30 | all-reduce | flops 3552 | bytes 14208 | tf_op jit(solution)/shard_map/psum | solution.py:384
  1450.8 46.1 %reduce-scatter.18.cloned.1.call-done = bf16[2,192,3072]{2,1,0:T(8,128)(2,1)} async-done(((bf16[2,768,3072]{2,1,0:T(8,128)(2,1)}), bf16[2,192,3072]{2,1,0:T(8,128)(2,1)}) %reduce-scatter.18.cloned.1.call-update) | async-done | bytes 2359312 | tf_op jit(solution)/shard_map/reduce_scatter | solution.py:367
  (552 shorter events, 818.8 us)
Async XLA Ops:
  7.2 22.6 %all-gather.9.cloned.1.call-start = ((), (), s32[]{:S(2)}) async-start(), calls=%async_computation.19 | async-start | bytes 1474560 | tf_op jit(solution)/shard_map/all_gather | solution.py:97
  8.0 47.2 %all-gather.13.cloned.1.call-start = ((), (), s32[]{:S(2)}) async-start(), calls=%async_computation.21 | async-start | bytes 1474560 | tf_op jit(solution)/shard_map/all_gather | solution.py:96
  8.7 71.8 %all-gather.11.cloned.1.call-start = ((), (), s32[]{:S(2)}) async-start(), calls=%async_computation.20 | async-start | bytes 1474560 | tf_op jit(solution)/shard_map/all_gather | solution.py:95
  9.4 300.7 %all-gather.15.cloned.1.call-start = ((), (), s32[]{:S(2)}) async-start(), calls=%async_computation.22 | async-start | bytes 1474560 | tf_op jit(solution)/shard_map/all_gather | solution.py:98
  10.0 443.7 %all-gather.17.cloned.1.call-start = ((), (), s32[]{:S(2)}) async-start(), calls=%async_computation.23 | async-start | bytes 11796480 | tf_op jit(solution)/shard_map/all_gather | solution.py:100
  33.4 25.4 %all-to-all-start = ((bf16[640,4,192]{0,2,1:T(8,128)(2,1)}), bf16[640,4,192]{0,2,1:T(8,128)(2,1)S(1)}, u32[]{:S(2)}, u32[]{:S(2)}) async-start(bf16[640,4,192]{0,2,1:T(8,128)(2,1)} %bitcast.2), calls=%async_computation | async-start | bytes 1966080 | tf_op jit(solution)/shard_map/all_to_all | solution.py:112
  36.9 439.1 %all-gather.19.cloned.1.call-start = ((), (), s32[]{:S(2)}) async-start(), calls=%async_computation.24 | async-start | bytes 11796480 | tf_op jit(solution)/shard_map/all_gather | solution.py:101
  58.8 32.6 %all-to-all-start.2 = ((bf16[640,4,192]{0,2,1:T(8,128)(2,1)}), bf16[640,4,192]{0,2,1:T(8,128)(2,1)S(1)}, u32[]{:S(2)}, u32[]{:S(2)}) async-start(bf16[640,4,192]{0,2,1:T(8,128)(2,1)} %bitcast.297), calls=%async_computation.2 | async-start | bytes 1966080 | tf_op jit(solution)/shard_map/all_to_all | solution.py:111
  87.0 120.5 %collective-permute-start = (bf16[2560,192]{0,1:T(8,128)(2,1)}, bf16[2560,192]{0,1:T(8,128)(2,1)}, u32[]{:S(2)}, u32[]{:S(2)}) collective-permute-start(bf16[2560,192]{0,1:T(8,128)(2,1)} %bitcast.79), channel_id=1, source_target_pairs={{0,1},{1,2},{2,3},{3,4},{4,5},{5,6},{6,7},{8,9},{9,10},{10,11},{11... | collective-permute-start | bytes 2949128 | tf_op jit(solution)/shard_map/ppermute | solution.py:20
  91.3 105.1 %all-to-all-start.1 = ((bf16[640,4,192]{0,2,1:T(8,128)(2,1)}), bf16[640,4,192]{0,2,1:T(8,128)(2,1)}, u32[]{:S(2)}, u32[]{:S(2)}) async-start(bf16[640,4,192]{0,2,1:T(8,128)(2,1)} %bitcast.5), calls=%async_computation.1 | async-start | bytes 1966080 | tf_op jit(solution)/shard_map/all_to_all | solution.py:110
  124.3 85.0 %collective-permute-start.1 = (bf16[2560,192]{0,1:T(8,128)(2,1)}, bf16[2560,192]{0,1:T(8,128)(2,1)}, u32[]{:S(2)}, u32[]{:S(2)}) collective-permute-start(bf16[2560,192]{0,1:T(8,128)(2,1)} %bitcast.81), channel_id=1, source_target_pairs={{0,1},{1,2},{2,3},{3,4},{4,5},{5,6},{6,7},{8,9},{9,10},{10,11},{11... | collective-permute-start | bytes 2949128 | tf_op jit(solution)/shard_map/ppermute | solution.py:20
  304.2 17.9 %all-to-all-start.3 = ((bf16[4,640,192]{1,2,0:T(8,128)(2,1)}), bf16[4,640,192]{1,2,0:T(8,128)(2,1)S(1)}, u32[]{:S(2)}, u32[]{:S(2)}) async-start(bf16[4,640,192]{1,2,0:T(8,128)(2,1)} %copy.125), calls=%async_computation.3 | async-start | bytes 1966080 | tf_op jit(solution)/shard_map/all_to_all | solution.py:177
  356.7 92.2 %all-to-all-start.4 = ((bf16[8,2,160,768]{3,2,1,0:T(8,128)(2,1)}), bf16[8,2,160,768]{3,2,1,0:T(8,128)(2,1)}, u32[]{:S(2)}, u32[]{:S(2)}) async-start(bf16[8,2,160,768]{3,2,1,0:T(8,128)(2,1)} %bitcast.291), calls=%async_computation.4 | async-start | bytes 7864320 | tf_op jit(solution)/shard_map/all_to_all | solution.py:192
  449.0 91.6 %all-to-all-start.6 = ((bf16[8,2,160,768]{3,2,1,0:T(8,128)(2,1)}), bf16[8,2,160,768]{3,2,1,0:T(8,128)(2,1)}, u32[]{:S(2)}, u32[]{:S(2)}) async-start(bf16[8,2,160,768]{3,2,1,0:T(8,128)(2,1)} %bitcast.290), calls=%async_computation.6 | async-start | bytes 7864320 | tf_op jit(solution)/shard_map/all_to_all | solution.py:219
  540.6 91.9 %all-to-all-start.5 = ((bf16[8,2,160,768]{3,2,1,0:T(8,128)(2,1)}), bf16[8,2,160,768]{3,2,1,0:T(8,128)(2,1)}, u32[]{:S(2)}, u32[]{:S(2)}) async-start(bf16[8,2,160,768]{3,2,1,0:T(8,128)(2,1)} %copy.133), calls=%async_computation.5 | async-start | bytes 7864320 | tf_op jit(solution)/shard_map/all_to_all | solution.py:198
  632.5 91.6 %all-to-all-start.7 = ((bf16[8,2,160,768]{3,2,1,0:T(8,128)(2,1)}), bf16[8,2,160,768]{3,2,1,0:T(8,128)(2,1)}, u32[]{:S(2)}, u32[]{:S(2)}) async-start(bf16[8,2,160,768]{3,2,1,0:T(8,128)(2,1)} %copy.135), calls=%async_computation.7 | async-start | bytes 7864320 | tf_op jit(solution)/shard_map/all_to_all | solution.py:227
  755.5 499.5 %reduce-scatter.16.cloned.1.call-start = ((), (), s32[]{:S(2)}) async-start(), calls=%async_computation.28 | async-start | bytes 1474560 | tf_op jit(solution)/shard_map/reduce_scatter | solution.py:361
  758.9 496.0 %reduce-scatter.10.cloned.1.call-start = ((), (), s32[]{:S(2)}) async-start(), calls=%async_computation.25 | async-start | bytes 1474560 | tf_op jit(solution)/shard_map/reduce_scatter | solution.py:352
  1080.4 174.6 %reduce-scatter.12.cloned.1.call-start = ((), (), s32[]{:S(2)}) async-start(), calls=%async_computation.26 | async-start | bytes 1474560 | tf_op jit(solution)/shard_map/reduce_scatter | solution.py:355
  1117.3 137.6 %reduce-scatter.14.cloned.1.call-start = ((), (), s32[]{:S(2)}) async-start(), calls=%async_computation.27 | async-start | bytes 1474560 | tf_op jit(solution)/shard_map/reduce_scatter | solution.py:358
  1156.0 181.4 %reduce-scatter.22.cloned.1.call-start = ((), (), s32[]{:S(2)}) async-start(), calls=%async_computation.31 | async-start | bytes 245760
  1157.2 282.0 %all-reduce.14.cloned.1.call-start = ((), (), s32[]{:S(2)}) async-start(), calls=%async_computation.32 | async-start | bytes 2359296 | tf_op jit(solution)/shard_map/psum | solution.py:386
  1255.0 191.6 %reduce-scatter.20.cloned.1.call-start = ((), (), s32[]{:S(2)}) async-start(), calls=%async_computation.30 | async-start | bytes 11796480 | tf_op jit(solution)/shard_map/reduce_scatter | solution.py:370
  1282.6 214.2 %reduce-scatter.18.cloned.1.call-start = ((), (), s32[]{:S(2)}) async-start(), calls=%async_computation.29 | async-start | bytes 11796480 | tf_op jit(solution)/shard_map/reduce_scatter | solution.py:367
  (103 other events, 1750.2 us)
Sparse Core Ops, SparseCore 0:
  9.6 20.1 all-gather.8
  31.4 23.7 all-gather.12
  56.7 23.7 all-gather.10
  81.9 17.4 all-gather.14
  100.8 67.6 all-gather.16
  170.0 64.6 all-gather.18
  759.0 25.2 reduce-scatter.15
  1080.5 27.1 reduce-scatter.9
  1117.4 31.2 reduce-scatter.11
  1156.2 24.8 reduce-scatter.13
  1184.1 19.7 reduce-scatter.21
  1255.1 80.1 all-reduce.13
  1338.0 77.6 reduce-scatter.19
  1418.4 78.4 reduce-scatter.17
where the time goes:
time: 1520 us; the launch traced here: 1510 us
  matrix products  392 us (26%)
  local copies, waits for them, and re-layouts  339 us (22%)
  waiting for transfers between devices  300 us (20%)
  other arithmetic  216 us (14%)
  blocking collectives  143 us (9%)
  starting transfers between devices  60.1 us (4%)
  loops' own time  39.7 us (3%)
  between operations  18.9 us (1%)
    convert_element_type x18, local copies, waits for them, and re-layouts, per_device(): bucket = bucket + (distance >= edge_value).astype(jnp.int32)  75.9 us
    dot_general x10, matrix products, scores_of(): jnp.einsum('qhe,khe->hqk', query_blk, key_blk, preferred_element_type=sin...  63.4 us
    all_to_all x1, waiting for transfers between devices, per_device(): lax.all_to_all(send_rows, 'seq', split_axis=0, concat_axis=0, tiled=True)  60.9 us
    unnamed x3, blocking collectives  59.5 us
    all_to_all x1, waiting for transfers between devices, per_device(): lax.all_to_all(drows, 'seq', split_axis=0, concat_axis=0, tiled=True)  53.9 us
    reduce_scatter x1, waiting for transfers between devices, per_device(): lax.psum_scatter(grad_first_full.astype(jnp.bfloat16), 'head', scatter_di...  46.1 us
    dot_general x1, matrix products, per_device(): jnp.dot(dscore_sum.reshape(local_heads, -1), bucket_hot, precision=highest)  45.4 us
    add x5, other arithmetic, backward_block(): dscore_sum + dscores.astype(single)  40 us
  transfers between devices with their start and end apart: 27, of which 12 were waited for; matrix products, arithmetic and copies ran while one was open for 59% of the time, Pallas kernels for 0%

commit v1 on v0

v1 whole, which is shorter than its diff:
```python
import functools

import jax
import jax.numpy as jnp
import numpy as np
from jax import lax
from jax.experimental import pallas as pl
from jax.experimental.pallas import tpu as pltpu
from jax.sharding import PartitionSpec as P

HEAD_DIM = 64
WINDOW = 1024
BUCKETS = 32
QB = 256
CHUNKS = WINDOW // QB + 1
KEYS = CHUNKS * QB
MASKED = -1e30
epsilon = 1e-06
bfloat = jnp.bfloat16
single = jnp.float32
MIB = 1 << 20

VMEM = pl.BlockSpec(memory_space=pltpu.VMEM)
SMEM = pl.BlockSpec(memory_space=pltpu.SMEM)


def dot(a, b, dims=((1,), (0,))):
    return lax.dot_general(a, b, (dims, ((), ())), preferred_element_type=single)


NN = ((1,), (0,))
NT = ((1,), (1,))
TN = ((0,), (0,))


def params(mib, grid=0):
    extra = {"dimension_semantics": ("arbitrary",) * grid} if grid else {}
    return pltpu.CompilerParams(vmem_limit_bytes=mib * MIB, **extra)


def cost(flops, moved, trans=0):
    return pl.CostEstimate(flops=int(flops), bytes_accessed=int(moved), transcendentals=int(trans))


def bucket_edges(window_len, bucket_count):
    middle = bucket_count // 2
    edge_list = []
    for number in range(1, bucket_count):
        if number < middle:
            edge_list.append(number)
        else:
            edge_list.append(int(middle * (window_len / middle) ** ((number - middle) / middle)))
    return edge_list


def lane_tables():
    lane = np.arange(2 * QB)
    offset = np.where(lane < QB, lane, lane - 2 * QB)
    distance = WINDOW - QB * np.arange(CHUNKS)[:, None] + offset[None, :]
    allowed = (distance >= 0) & (distance < WINDOW)
    bucket = np.zeros(distance.shape, np.int32)
    for edge_value in bucket_edges(WINDOW, BUCKETS):
        bucket = bucket + (distance >= edge_value)
    hot = (bucket.reshape(-1)[:, None] == np.arange(BUCKETS)[None, :]) & allowed.reshape(-1)[:, None]
    return hot, allowed


GAINS = 16


def pack_kernel(order, wq, wk, wv, router_t, gains, own, far, near, both):
    part, width = wq.shape
    experts = router_t.shape[0]
    for lane in range(width // part):

        @pl.when(order[0] == lane)
        def _():
            for mask, ref in ((0, own), (2, far), (1, near), (3, both)):
                at = (lane ^ mask) * part
                for number, weight in enumerate((wq, wk, wv)):
                    ref[number * part : (number + 1) * part, :] = weight[:, at : at + part]

    for ref in (own, far, near, both):
        ref[3 * part : 3 * part + experts, :] = router_t[...]
        ref[3 * part + experts :, :] = gains[...]


def pack(order, wq, wk, wv, router_t, gains):
    part = wq.shape[0]
    tall = 3 * part + router_t.shape[0] + GAINS
    return pl.pallas_call(
        pack_kernel,
        in_specs=[SMEM] + [VMEM] * 5,
        out_specs=[VMEM] * 4,
        out_shape=[jax.ShapeDtypeStruct((tall, part), bfloat)] * 4,
        compiler_params=params(16),
        name="pack",
    )(order, wq, wk, wv, router_t, gains)


def project_kernel(
    order, x0, x1, x2, x3, p0, p1, p2, p3, n_out, qt_out, kv_out, rows_out, router_out, gain_out, wq, wk, wv
):
    rows, width = x0.shape
    heads = kv_out.shape[0]
    part = heads * HEAD_DIM
    experts = router_out.shape[0]
    packed = (p0, p1, p2, p3)
    for place, ref in enumerate(packed):
        at = pl.ds(pl.multiple_of(order[place] * part, 64), part)
        for number, weight in enumerate((wq, wk, wv)):
            weight[at, :] = ref[number * part : (number + 1) * part, :]

    def spread(begin, count):
        found = []
        for lane in range(len(packed)):
            piece = packed[0][begin : begin + count, :]
            for place in range(1, len(packed)):
                piece = jnp.where(order[place] == lane, packed[place][begin : begin + count, :], piece)
            found.append(piece)
        return jnp.concatenate(found, axis=1)

    router_out[...] = spread(3 * part, experts)
    gains = spread(3 * part + experts, GAINS).astype(single)
    gain_out[...] = gains[0:8, :]
    wq_t = wq[...].T
    k_t = wk[...].T
    v_t = wv[...].T
    for head in range(heads):
        at = slice(head * HEAD_DIM, (head + 1) * HEAD_DIM)
        for number, value in enumerate((wq_t, k_t, v_t)):
            begin = (3 * head + number) * HEAD_DIM
            rows_out[begin : begin + HEAD_DIM, :] = value[at, :]
    for place, ref in enumerate((x0, x1, x2, x3)):
        block = order[place]
        values = ref[...].astype(single)
        inverse = lax.rsqrt(jnp.mean(values * values, axis=-1, keepdims=True) + epsilon)
        normed = (values * inverse * gain_out[0:1, :]).astype(bfloat)
        n_out[block] = normed
        at = pl.ds(pl.multiple_of(block * rows, 128), rows)
        qt = dot(wq_t, normed, NT).astype(bfloat)
        qt_out[:, at] = qt * bfloat(HEAD_DIM**-0.5)
        for head in range(heads):
            begin = 3 * head * HEAD_DIM + HEAD_DIM
            kv = dot(normed, rows_out[begin : begin + 2 * HEAD_DIM, :], NT)
            kv_out[head, at, :] = kv.astype(bfloat)


def project(order, pieces, packed, heads, experts):
    rows, width = pieces[0].shape
    total = rows * len(pieces)
    part = heads * HEAD_DIM
    return pl.pallas_call(
        project_kernel,
        in_specs=[SMEM] + [VMEM] * 8,
        out_specs=[VMEM] * 6,
        out_shape=[
            jax.ShapeDtypeStruct((len(pieces), rows, width), bfloat),
            jax.ShapeDtypeStruct((part, total), bfloat),
            jax.ShapeDtypeStruct((heads, total, 2 * HEAD_DIM), bfloat),
            jax.ShapeDtypeStruct((3 * part, width), bfloat),
            jax.ShapeDtypeStruct((experts, width), bfloat),
            jax.ShapeDtypeStruct((8, width), single),
        ],
        scratch_shapes=[pltpu.VMEM((width, part), bfloat)] * 3,
        compiler_params=params(40),
        cost_estimate=cost(2 * total * width * 3 * part, 4 * total * width),
        name="project",
    )(order, *pieces, *packed)


def eye(size):
    return (
        lax.broadcasted_iota(jnp.int32, (size, size), 0) == lax.broadcasted_iota(jnp.int32, (size, size), 1)
    ).astype(bfloat)


def stage_attention(kvp, kv, vecs, kv_all, kvt_all, bias):
    heads = kv_all.shape[0]
    unit = eye(2 * HEAD_DIM)
    for head in range(heads):
        if kvp is None:
            kv_all[head] = kv[head]
        else:
            kv_all[head, :WINDOW, :] = kvp[head]
            kv_all[head, WINDOW:, :] = kv[head]
        kvt_all[head] = dot(unit, kv_all[head], NT).astype(bfloat)
        for chunk in range(CHUNKS):
            row = jnp.broadcast_to(vecs[head, chunk : chunk + 1, :], (QB, 2 * QB))
            tile = pltpu.roll(row, 0, 1, stride=1, stride_axis=0)
            bias[head, chunk * QB : (chunk + 1) * QB, :] = tile[:, :QB]


def keep_rows(scores, step, low):
    key = lax.broadcasted_iota(jnp.int32, scores.shape, 0) + step * QB
    return jnp.where(key >= low, scores, MASKED)


def query_tile(step, first, pieces):
    found = []
    for half in range(QB // 128):
        piece = (step + first) * (QB // 128) + half
        found.append((piece // pieces, pl.ds(pl.multiple_of((piece % pieces) * 128, 128), 128)))
    return found


def forward_kernel(first, order, need, low, qt, keys_in, vecs, *rest):
    *more, out, lse, kv_all, kvt_all, bias = rest
    step = pl.program_id(0)
    heads = kv_all.shape[0]
    pieces = out.shape[2] // 128

    @pl.when(step == 0)
    def _():
        if more:
            stage_attention(more[0], keys_in, vecs, kv_all, kvt_all, bias)
            out[...] = more[1][...]
        else:
            stage_attention(None, keys_in, vecs, kv_all, kvt_all, bias)

    start = pl.multiple_of(step * QB, QB)

    def run(masked):
        for head in range(heads):
            keys = kv_all[head, pl.ds(start, KEYS), :]
            query = qt[head * HEAD_DIM : (head + 1) * HEAD_DIM, :]
            query = jnp.concatenate([query, jnp.zeros_like(query)], axis=0)
            scores = dot(keys, query) + bias[head]
            if masked:
                scores = keep_rows(scores, step + first, low[...])
            peak = jnp.max(scores, axis=0, keepdims=True)
            expo = jnp.exp(scores - peak)
            total = jnp.sum(expo, axis=0, keepdims=True)
            values = kvt_all[head, HEAD_DIM:, pl.ds(start, KEYS)]
            mixed = dot(values, expo.astype(bfloat)) * (1.0 / total)
            mixed = mixed.astype(bfloat)
            at = slice(head * HEAD_DIM, (head + 1) * HEAD_DIM)
            for half, (owner, place) in enumerate(query_tile(step, first, pieces)):
                out[jnp.bitwise_xor(owner, order[0]), at, place] = mixed[:, half * 128 : (half + 1) * 128]
            lse[0, head : head + 1, :] = peak + jnp.log(total)

    pl.when(need[step + first] > 0)(lambda: run(True))
    pl.when(need[step + first] <= 0)(lambda: run(False))


def attention_forward(first, steps, order, need, low, qt, kvp, kv, vecs, lanes, begun=None):
    heads, total, packed = kv.shape
    width = heads * HEAD_DIM
    held = KEYS + (steps - 1) * QB
    own = held - (0 if kvp is None else WINDOW)
    more = [] if kvp is None else [kvp, begun]
    return pl.pallas_call(
        functools.partial(forward_kernel, first),
        grid=(steps,),
        in_specs=[
            SMEM,
            SMEM,
            pl.BlockSpec((1, QB), lambda i: (0, i + first)),
            pl.BlockSpec((width, QB), lambda i: (0, i + first)),
            pl.BlockSpec((heads, own, packed), lambda i: (0, 0, 0)),
            VMEM,
        ]
        + [VMEM] * len(more),
        out_specs=[VMEM, pl.BlockSpec((1, 8, QB), lambda i: (i, 0, 0))],
        out_shape=[
            jax.ShapeDtypeStruct((lanes, width, total // lanes), bfloat),
            jax.ShapeDtypeStruct((steps, 8, QB), single),
        ],
        scratch_shapes=[
            pltpu.VMEM((heads, held, packed), bfloat),
            pltpu.VMEM((heads, packed, held), bfloat),
            pltpu.VMEM((heads, KEYS, QB), single),
        ],
        compiler_params=params(48, 1),
        cost_estimate=cost(steps * heads * KEYS * QB * 2048, 8 * total * width, steps * heads * KEYS * QB),
        name="attend",
    )(order, need, low, qt, kv, vecs, *more)


def diagonal_sums(tile):
    wide = jnp.concatenate([tile, jnp.zeros_like(tile)], axis=1)
    row = lax.broadcasted_iota(jnp.int32, wide.shape, 0)
    bit = 1
    while bit < QB:
        wide = jnp.where((row & bit) != 0, pltpu.roll(wide, 2 * QB - bit, 1), wide)
        bit *= 2
    return jnp.sum(wide, axis=0, keepdims=True)


def backward_kernel(first, ends, order, need, low, qt, keys_in, vecs, lse, d0, d1, d2, d3, *rest):
    if ends:
        dkvt_in, ds_in, dqt, dkvt, sums, kv_all, kvt_all, bias, dout_all, ds_all = rest
        kvp = None
    else:
        kvp, dqt, dkvt, ds_all, kv_all, kvt_all, bias, dout_all = rest
    step = pl.program_id(0)
    heads = kv_all.shape[0]
    rows = d0.shape[1]

    @pl.when(step == 0)
    def _():
        stage_attention(kvp, keys_in, vecs, kv_all, kvt_all, bias)
        for place, ref in enumerate((d0, d1, d2, d3)):
            dout_all[:, pl.ds(pl.multiple_of(order[place] * rows, 128), rows)] = ref[...]
        if ends:
            ds_all[...] = ds_in[...]
            dkvt[:, :, :WINDOW] = dkvt_in[:, :, WINDOW : 2 * WINDOW]
            dkvt[:, :, WINDOW:] = jnp.zeros_like(dkvt[:, :, WINDOW:])
        else:
            ds_all[...] = jnp.zeros_like(ds_all)
            dkvt[...] = jnp.zeros_like(dkvt)

    start = pl.multiple_of(step * QB, QB)

    def run(masked):
        for head in range(heads):
            at = slice(head * HEAD_DIM, (head + 1) * HEAD_DIM)
            keys = kv_all[head, pl.ds(start, KEYS), :]
            query = qt[at, :]
            none = jnp.zeros_like(query)
            scores = dot(keys, jnp.concatenate([query, none], axis=0)) + bias[head]
            if masked:
                scores = keep_rows(scores, step + first, low[...])
            probs = jnp.exp(scores - lse[0, pl.ds(order[4] + head, 1), :])
            dout = dout_all[at, pl.ds(pl.multiple_of((step + first) * QB, QB), QB)]
            dprobs = dot(keys, jnp.concatenate([none, dout], axis=0))
            delta = jnp.sum(probs * dprobs, axis=0, keepdims=True)
            dscores = probs * (dprobs - delta)
            ds_all[head] += dscores
            dscores = dscores.astype(bfloat)
            probs = probs.astype(bfloat)
            window = pl.ds(start, KEYS)
            dqt[at, :] = (dot(kvt_all[head, :HEAD_DIM, window], dscores) * HEAD_DIM**-0.5).astype(bfloat)
            dkvt[head, :HEAD_DIM, window] += dot(query, dscores, NT)
            dkvt[head, HEAD_DIM:, window] += dot(dout, probs, NT)

    pl.when(need[step + first] > 0)(lambda: run(True))
    pl.when(need[step + first] <= 0)(lambda: run(False))

    if ends:

        @pl.when(step == pl.num_programs(0) - 1)
        def _():
            for head in range(heads):
                for chunk in range(CHUNKS):
                    sums[head, chunk : chunk + 1, :] = diagonal_sums(ds_all[head, chunk * QB : (chunk + 1) * QB, :])


def attention_backward(first, steps, span, order, need, low, qt, kvp, kv, vecs, lse, douts, begun=(), after=()):
    total, packed = kv.shape[1:]
    begin, heads = span
    pick = begin // heads
    width = heads * HEAD_DIM
    held = KEYS + (steps - 1) * QB
    ends = kvp is None
    own = held if ends else held - WINDOW
    scores = (heads, KEYS, QB)
    order = jnp.concatenate([order, jnp.full((1,), begin, jnp.int32)])
    kernel = functools.partial(backward_kernel, first, ends)
    specs = [
        SMEM,
        SMEM,
        pl.BlockSpec((1, QB), lambda i: (0, i + first)),
        pl.BlockSpec((width, QB), lambda i: (pick, i + first)),
        pl.BlockSpec((heads, own, packed), lambda i: (pick, 0, 0)),
        pl.BlockSpec((heads,) + vecs.shape[1:], lambda i: (pick, 0, 0)),
        pl.BlockSpec((1, 8, QB), lambda i: (i, 0, 0)),
    ] + [pl.BlockSpec((width, douts[0].shape[1]), lambda i: (pick, 0))] * 4
    inputs = [order, need, low, qt, kv, vecs, lse, *douts]
    out_specs = [pl.BlockSpec((width, QB), lambda i: (0, i)), VMEM]
    out_shape = [
        jax.ShapeDtypeStruct((width, steps * QB), bfloat),
        jax.ShapeDtypeStruct((heads, packed, held), single),
    ]
    scratch = [
        pltpu.VMEM((heads, held, packed), bfloat),
        pltpu.VMEM((heads, packed, held), bfloat),
        pltpu.VMEM(scores, single),
        pltpu.VMEM((width, total), bfloat),
    ]
    if ends:
        specs += [
            pl.BlockSpec((heads, packed, 2 * WINDOW), lambda i: (pick, 0, 0)),
            pl.BlockSpec(scores, lambda i: (pick, 0, 0)),
        ]
        inputs += list(begun)
        out_specs.append(VMEM)
        out_shape.append(jax.ShapeDtypeStruct((heads, 8, 2 * QB), single))
        scratch.append(pltpu.VMEM(scores, single))
    else:
        specs.append(VMEM)
        inputs.append(kvp)
        out_specs.append(VMEM)
        out_shape.append(jax.ShapeDtypeStruct(scores, single))
    if after:
        inner, count = kernel, len(inputs)
        kernel = lambda *refs: inner(*refs[:count], *refs[count + len(after) :])
        specs += [pl.BlockSpec(memory_space=pl.ANY)] * len(after)
        inputs += list(after)
    return pl.pallas_call(
        kernel,
        grid=(steps,),
        in_specs=specs,
        out_specs=out_specs,
        out_shape=out_shape,
        scratch_shapes=scratch,
        compiler_params=params(56, 1),
        cost_estimate=cost(steps * heads * KEYS * QB * 4096, 16 * total * width, steps * heads * KEYS * QB),
        name="attend_back",
    )(*inputs)


def settle_kernel(order, dq0, dq1, dkvt, behind, normed, out, grad):
    heads = dkvt.shape[0]
    rows = out.shape[2]
    total = dkvt.shape[2]
    edge = total - WINDOW
    sums = None
    parts = []
    for head in range(heads):
        at = slice(head * HEAD_DIM, (head + 1) * HEAD_DIM)
        dkv = jnp.concatenate([dkvt[head, :, :edge], dkvt[head, :, edge:] + behind[head].astype(single)], axis=1)
        parts.append(jnp.concatenate([dq0[at, :], dq1[at, :]], axis=1))
        parts.append(dkv.astype(bfloat))
    whole = jnp.concatenate(parts, axis=0)
    for lane in range(total // rows):
        piece = whole[:, lane * rows : (lane + 1) * rows]
        out[jnp.bitwise_xor(order[0], lane)] = piece
        term = dot(piece, normed[lane])
        sums = term if sums is None else sums + term
    grad[...] = sums.astype(bfloat)


def settle(span, order, dq0, dq1, dkvt, behind, normed):
    begin, heads = span
    pick = begin // heads
    lanes, rows, width = normed.shape
    tall = heads * 3 * HEAD_DIM
    total = lanes * rows
    whole = lambda shape: pl.BlockSpec(shape, lambda i: (0,) * len(shape))
    return pl.pallas_call(
        settle_kernel,
        grid=(1,),
        in_specs=[
            SMEM,
            pl.BlockSpec((heads * HEAD_DIM, dq0.shape[1]), lambda i: (pick, 0)),
            whole(dq1.shape),
            whole(dkvt.shape),
            pl.BlockSpec((heads,) + behind.shape[1:], lambda i: (pick, 0, 0)),
            whole(normed.shape),
        ],
        out_specs=[whole((lanes, tall, rows)), whole((tall, width))],
        out_shape=[
            jax.ShapeDtypeStruct((lanes, tall, rows), bfloat),
            jax.ShapeDtypeStruct((tall, width), bfloat),
        ],
        compiler_params=params(40, 1),
        cost_estimate=cost(2 * tall * total * width, 4 * total * width),
        name="settle",
    )(order, dq0, dq1, dkvt, behind, normed)


def middle_kernel(o0, o1, o2, o3, w0, w1, w2, w3, x, gain, code, y_out, send0, send1):
    y = x[...].astype(single)
    for ref, weight in ((o0, w0), (o1, w1), (o2, w2), (o3, w3)):
        y = y + dot(ref[...], weight[...], TN)
    y_out[...] = y
    inverse = lax.rsqrt(jnp.mean(y * y, axis=-1, keepdims=True) + epsilon)
    normed = (y * inverse * gain[...]).astype(bfloat)
    slots = send0.shape[0]
    for number, ref in enumerate((send0, send1)):
        slot = lax.broadcasted_iota(jnp.int32, (slots, y.shape[0]), 0) + number * slots
        pick = ((slot == code[0:1, :]) | (slot == code[1:2, :])).astype(bfloat)
        ref[...] = dot(pick, normed).astype(bfloat)


def middle(ots, w_out, x, gain, code, slots):
    rows, width = x.shape
    return pl.pallas_call(
        middle_kernel,
        in_specs=[VMEM] * 11,
        out_specs=[VMEM] * 3,
        out_shape=[
            jax.ShapeDtypeStruct((rows, width), single),
            jax.ShapeDtypeStruct((slots, width), bfloat),
            jax.ShapeDtypeStruct((slots, width), bfloat),
        ],
        compiler_params=params(40),
        cost_estimate=cost(2 * rows * width * (width + 2 * slots), 8 * rows * width),
        name="middle",
    )(*ots, *w_out, x, gain, code)


NOTES = 16


def send_kernel(value, code, out):
    slots, rows = out.shape[0], value.shape[0]
    slot = lax.broadcasted_iota(jnp.int32, (slots, rows), 0)
    pick = ((slot == code[0:1, :]) | (slot == code[1:2, :])).astype(bfloat)
    out[...] = dot(pick, value[...]).astype(bfloat)


def send_noted_kernel(value, code, partner, out):
    blocks, slot_rows = out.shape[0], out.shape[1] - NOTES
    rows, width = value.shape
    slots = blocks * slot_rows
    slot = lax.broadcasted_iota(jnp.int32, (slot_rows, rows), 0)
    for block in range(blocks):
        notes = []
        for number in range(2):
            here = slot + (number * slots + block * slot_rows)
            first = (here == code[0:1, :]).astype(bfloat)
            second = (here == code[1:2, :]).astype(bfloat)
            notes.append(dot(partner[0:8, :], first, NT) + dot(partner[8:16, :], second, NT))
        pick = first + second
        out[block, NOTES:, :] = dot(pick, value[...]).astype(bfloat)
        row = lax.broadcasted_iota(jnp.int32, (8, slot_rows), 0)
        note = jnp.where(row == 0, notes[0], notes[1])
        note = jnp.concatenate([note, jnp.zeros((8, width - slot_rows), single)], axis=1)
        out[block, :NOTES, :] = jnp.concatenate([note, note], axis=0).astype(bfloat)


def send_rows(value, code, slots):
    rows, width = value.shape
    return pl.pallas_call(
        send_kernel,
        in_specs=[VMEM] * 2,
        out_specs=VMEM,
        out_shape=jax.ShapeDtypeStruct((slots, width), bfloat),
        compiler_params=params(24),
        cost_estimate=cost(2 * rows * width * slots, 6 * rows * width),
        name="send_rows",
    )(value, code)


def send_noted(value, code, partner, blocks, slot_rows):
    rows, width = value.shape
    return pl.pallas_call(
        send_noted_kernel,
        in_specs=[VMEM] * 3,
        out_specs=VMEM,
        out_shape=jax.ShapeDtypeStruct((blocks, slot_rows + NOTES, width), bfloat),
        compiler_params=params(24),
        cost_estimate=cost(2 * rows * width * blocks * slot_rows, 6 * rows * width),
        name="send_noted",
    )(value, code, partner)


def collect(code, refs):
    total = None
    for number, ref in enumerate(refs):
        slots = ref.shape[0]
        slot = lax.broadcasted_iota(jnp.int32, (code.shape[0], slots), 1) + number * slots
        pick = ((slot == code[:, 0:1]) | (slot == code[:, 1:2])).astype(bfloat)
        part = dot(pick, ref[...])
        total = part if total is None else total + part
    return total


def return_kernel(order, d0, d1, code, y, gain, cotangent, w0, w1, w2, w3, o0, o1, o2, o3, dy_out, dot_out, gw_out, gg_out):
    dn = collect(code, (d0, d1))
    values = y[...]
    inverse = lax.rsqrt(jnp.mean(values * values, axis=-1, keepdims=True) + epsilon)
    hat = values * inverse
    gg_out[...] = jnp.sum(dn * hat, axis=0, keepdims=True)
    scaled = dn * gain[...]
    dy = cotangent[...].astype(single) + inverse * (scaled - hat * jnp.mean(scaled * hat, axis=-1, keepdims=True))
    dy_out[...] = dy
    low = dy.astype(bfloat)
    tall = o0.shape[0]
    for place, (ref, weight) in enumerate(((o0, w0), (o1, w1), (o2, w2), (o3, w3))):
        at = pl.ds(pl.multiple_of(order[place] * tall, 64), tall)
        mask = (0, 2, 1, 3)[place]
        dot_out[mask] = dot(weight[...], low, NT).astype(bfloat)
        gw_out[at, :] = dot(ref[...], low).astype(bfloat)


def return_rows(order, d0, d1, code, y, gain, cotangent, w_out, ots):
    rows, width = y.shape
    slots = d0.shape[0]
    lanes = len(ots)
    return pl.pallas_call(
        return_kernel,
        in_specs=[SMEM] + [VMEM] * 14,
        out_specs=[VMEM] * 4,
        out_shape=[
            jax.ShapeDtypeStruct((rows, width), single),
            jax.ShapeDtypeStruct((lanes, width // lanes, rows), bfloat),
            jax.ShapeDtypeStruct((width, width), bfloat),
            jax.ShapeDtypeStruct((1, width), single),
        ],
        compiler_params=params(48),
        cost_estimate=cost(2 * rows * width * (2 * width + 2 * slots), 16 * rows * width),
        name="return_rows",
    )(order, d0, d1, code, y, gain, cotangent, *w_out, *ots)


def finish_kernel(z0, z1, code, y, out):
    out[...] = (y[...] + collect(code, (z0, z1))).astype(bfloat)


def finish(z0, z1, code, y):
    rows, width = y.shape
    return pl.pallas_call(
        finish_kernel,
        in_specs=[VMEM] * 4,
        out_specs=VMEM,
        out_shape=jax.ShapeDtypeStruct((rows, width), bfloat),
        compiler_params=params(32),
        cost_estimate=cost(4 * rows * width * z0.shape[0], 12 * rows * width),
        name="finish",
    )(z0, z1, code, y)


def tail_kernel(order, *refs):
    *pieces, wt, x, gain, dy, out = refs
    dn = None
    for number, ref in enumerate(pieces):
        block = order[number % 4]
        tall = ref.shape[0]
        begin = block * (3 * x.shape[1] // 4)
        if number >= 4:
            begin = begin + pieces[0].shape[0]
        term = dot(ref[...], wt[pl.ds(pl.multiple_of(begin, 64), tall), :], TN)
        dn = term if dn is None else dn + term
    values = x[...].astype(single)
    inverse = lax.rsqrt(jnp.mean(values * values, axis=-1, keepdims=True) + epsilon)
    hat = values * inverse
    scaled = dn * gain[...]
    out[...] = dy[...] + inverse * (scaled - hat * jnp.mean(scaled * hat, axis=-1, keepdims=True))


def tail(order, pieces, wt, x, gain, dy):
    rows, width = x.shape
    return pl.pallas_call(
        tail_kernel,
        in_specs=[SMEM] + [VMEM] * (4 + len(pieces)),
        out_specs=VMEM,
        out_shape=jax.ShapeDtypeStruct((rows, width), single),
        compiler_params=params(40),
        cost_estimate=cost(2 * rows * width * wt.shape[0], 14 * rows * width),
        name="tail",
    )(order, *pieces, wt, x, gain, dy)


GELU_0 = 0.7978845608028654
GELU_1 = 0.7978845608028654 * 0.044715
FF_BLOCK = 512
ROW_BLOCK = 256


def expert_kernel(
    mine, xs, router, other, w1, w2, da, cot, g1, g2, dx_out, z_out, m_out, total, result, dgate, gate, act_all, du_all, xst, dzt
):
    step = pl.program_id(0)
    rows = xs.shape[0]
    experts = router.shape[0]

    def picks():
        lane = lax.broadcasted_iota(jnp.int32, (rows, experts), 1)
        return lane == mine[0], lane == other[...] - 1

    @pl.when(step == 0)
    def _():
        logits = dot(xs[...], router[...], NT)
        own, rest = picks()
        margin = jnp.sum(jnp.where(own, logits, 0.0) - jnp.where(rest, logits, 0.0), axis=1, keepdims=True)
        value = 1.0 / (1.0 + jnp.exp(-margin))
        value = jnp.where(other[...] > 0, value, 0.0)
        gate[...] = jnp.broadcast_to(value, gate.shape)
        dgate[...] = jnp.zeros_like(dgate)
        total[...] = jnp.zeros_like(total)
        result[...] = jnp.zeros_like(result)
        for begin in range(0, rows, ROW_BLOCK):
            at = slice(begin, begin + ROW_BLOCK)
            xst[:, at] = xs[at, :].T
            dzt[:, at] = (cot[at, :].astype(single) * gate[at, 0:1]).astype(bfloat).T

    for begin in range(0, rows, ROW_BLOCK):
        at = slice(begin, begin + ROW_BLOCK)
        u = dot(xs[at, :], w1[...])
        square = u * u
        tan = jnp.tanh(u * (GELU_0 + GELU_1 * square))
        half = 0.5 + 0.5 * tan
        act = u * half
        slope = half + act * (1.0 - half) * (2.0 * GELU_0 + 6.0 * GELU_1 * square)
        back = da[at, :].astype(single)
        product = act * back
        part = product[:, :128]
        for col in range(128, product.shape[1], 128):
            part = part + product[:, col : col + 128]
        dgate[at, :] += part
        act_all[at, :] = act.astype(bfloat)
        du_all[at, :] = (gate[at, 0:1] * back * slope).astype(bfloat)
    total[...] += dot(du_all[...], w1[...], NT)
    result[...] += dot(act_all[...], w2[...])
    g1[...] = dot(xst[...], du_all[...]).astype(bfloat)
    g2[...] = dot(dzt[...], act_all[...]).astype(bfloat).T

    @pl.when(step == pl.num_programs(0) - 1)
    def _():
        own, rest = picks()
        value = gate[:, 0:1]
        weight = value * (1.0 - value) * jnp.sum(dgate[...], axis=1, keepdims=True)
        m = (weight * (own.astype(single) - rest.astype(single))).astype(bfloat)
        m_out[...] = m
        dx_out[...] = (total[...] + dot(m, router[...])).astype(bfloat)
        z_out[...] = (result[...] * value).astype(bfloat)


def expert(mine, xs, router, other, w1, w2, da, cot, local):
    rows, width = xs.shape
    inner = w1.shape[2]
    experts = router.shape[0]
    block = FF_BLOCK
    whole = lambda shape: pl.BlockSpec(shape, lambda f: (0,) * len(shape))
    return pl.pallas_call(
        expert_kernel,
        grid=(inner // block,),
        in_specs=[
            SMEM,
            whole((rows, width)),
            whole((experts, width)),
            whole((rows, 1)),
            pl.BlockSpec((None, width, block), lambda f: (local, 0, f)),
            pl.BlockSpec((None, block, width), lambda f: (local, f, 0)),
            pl.BlockSpec((rows, block), lambda f: (0, f)),
            whole((rows, width)),
        ],
        out_specs=[
            pl.BlockSpec((width, block), lambda f: (0, f)),
            pl.BlockSpec((block, width), lambda f: (f, 0)),
            whole((rows, width)),
            whole((rows, width)),
            whole((rows, experts)),
        ],
        out_shape=[
            jax.ShapeDtypeStruct((width, inner), bfloat),
            jax.ShapeDtypeStruct((inner, width), bfloat),
            jax.ShapeDtypeStruct((rows, width), bfloat),
            jax.ShapeDtypeStruct((rows, width), bfloat),
            jax.ShapeDtypeStruct((rows, experts), bfloat),
        ],
        scratch_shapes=[
            pltpu.VMEM((rows, width), single),
            pltpu.VMEM((rows, width), single),
            pltpu.VMEM((rows, 128), single),
            pltpu.VMEM((rows, 128), single),
            pltpu.VMEM((rows, block), bfloat),
            pltpu.VMEM((rows, block), bfloat),
            pltpu.VMEM((width, rows), bfloat),
            pltpu.VMEM((width, rows), bfloat),
        ],
        compiler_params=params(60, 1),
        cost_estimate=cost(20 * rows * width * inner, 8 * rows * inner + 8 * width * inner, rows * inner),
        name="expert",
    )(mine, xs, router, other, w1, w2, da, cot)


def tie(*values):
    return lax.optimization_barrier(values)


def swap(value, axis, mask):
    return lax.ppermute(value, axis, [(i, i ^ mask) for i in range(lax.axis_size(axis))])


def per_device(
    hidden_in,
    norm1_gain,
    w_query,
    w_key,
    w_value,
    w_out,
    rel_bias,
    norm2_gain,
    w_router,
    w_first,
    w_second,
    routes,
    priority,
    segments,
    grad_out,
):
    lanes = lax.axis_size("head")
    blocks = lax.axis_size("seq")
    lane = lax.axis_index("head")
    place = lax.axis_index("seq")
    rows, width = hidden_in.shape[2:]
    x = hidden_in.reshape(rows, width)
    total = rows * lanes
    part = width // lanes
    heads = part // HEAD_DIM
    cotangent = grad_out.reshape(rows, width)
    experts = w_router.shape[1]
    local = w_first.shape[0]
    slot_rows = max(2, 4 * rows // experts)
    slots = blocks * slot_rows
    capacity = 5 * rows * lanes // (2 * local)

    far = swap(x, "head", 2)
    near = swap(x, "head", 1)
    order = jnp.stack([lane, lane ^ 2, lane ^ 1, lane ^ 3]).astype(jnp.int32)
    at = lambda value, mask: lax.dynamic_index_in_dim(value, lane ^ mask, 0, keepdims=False)

    def trade(value):
        return [value[0], swap(value[2], "head", 2), swap(value[1], "head", 1), swap(value[3], "head", 3)]

    gains = jnp.concatenate([norm1_gain[None, :], norm2_gain[None, :], jnp.zeros((GAINS - 2, part), bfloat)], axis=0)
    own_pack, far_pack, near_pack, both_pack = pack(order, w_query, w_key, w_value, w_router.T, gains)
    packed = [own_pack, swap(far_pack, "head", 2), swap(near_pack, "head", 1), swap(both_pack, "head", 3)]

    route_rows = routes.reshape(rows, -1)
    top_count = route_rows.shape[1]
    pair_routes = route_rows.reshape(-1)
    pair_prio = priority.reshape(-1)
    expert_ids = jnp.arange(experts, dtype=jnp.int32)
    pair_hot = (pair_routes[:, None] == expert_ids[None, :]).astype(jnp.int32)
    earlier = (pair_routes[:, None] == pair_routes[None, :]) & (pair_prio[None, :] < pair_prio[:, None])
    local_rank = jnp.sum(earlier.astype(jnp.int32), axis=1)
    code = (pair_routes % local) * slots + (pair_routes // local) * slot_rows + local_rank
    code = code.reshape(rows, top_count)
    code_t = code.T

    def exchange(value):
        return lax.all_to_all(
            value.reshape(blocks, slot_rows, -1), "seq", split_axis=0, concat_axis=0, tiled=True
        ).reshape(slots, -1)

    cot_send = send_rows(cotangent, code_t, slots)

    block_rank = (jnp.min(pair_prio) // (top_count * rows)).reshape(1)
    spare = 128 - (experts + 1) % 128
    tallies = jnp.concatenate([jnp.sum(pair_hot, axis=0), block_rank, jnp.zeros((spare,), jnp.int32)])[None, :]
    for axis, size in (("head", lanes), ("seq", blocks)):
        mask = 1
        while mask < size:
            tallies = jnp.concatenate([tallies, swap(tallies, axis, mask)], axis=0)
            mask *= 2
    ahead = (tallies[:, experts : experts + 1] < block_rank[None, :]).astype(jnp.int32)
    offsets = jnp.sum(tallies[:, :experts] * ahead, axis=0)
    kept = (jnp.sum(pair_hot * offsets[None, :], axis=1) + local_rank < capacity).reshape(rows, top_count)
    partner = jnp.where(kept, route_rows[:, ::-1] + 1, 0).astype(bfloat)
    partner = jnp.repeat(partner.T, 8, axis=0)

    near, far, cot_send, w_second, w_first, w_out, *packed = tie(near, far, cot_send, w_second, w_first, w_out, *packed)
    both = swap(far, "head", 1)
    cot_first = exchange(cot_send)

    out_far = swap(w_out, "head", 2)
    out_near = swap(w_out, "head", 1)
    second_full = lax.all_gather(w_second, "head", axis=1, tiled=True)
    first_full = lax.all_gather(w_first, "head", axis=1, tiled=True)

    both, partner = tie(both, partner)
    normed, qt, kv, w_rows, router_t, gains = project(order, (x, far, near, both), packed, heads, experts)
    w_rows_full = lax.all_gather(w_rows, "head", axis=0, tiled=True)
    gain_one, gain_two = gains[0:1], gains[1:2]
    kvp = lax.ppermute(kv[:, total - WINDOW :, :], "seq", [(i, i + 1) for i in range(blocks - 1)])
    hot, allowed = lane_tables()
    table = rel_bias.reshape(heads, BUCKETS)
    vecs = dot(table, jnp.asarray(hot.T, bfloat)).reshape(heads, CHUNKS, 2 * QB)
    vecs = jnp.where(jnp.asarray(allowed)[None], vecs, MASKED)
    vecs = jnp.concatenate([vecs, jnp.zeros((heads, 8 - CHUNKS, 2 * QB), single)], axis=1)
    base = place * total
    own = lax.dynamic_slice_in_dim(segments, base, total, 0)
    low = jnp.zeros_like(own)
    for number in range(1, 4):
        low = jnp.where(own == number, jnp.sum((segments < number).astype(jnp.int32)), low)
    low = low - base + WINDOW
    need = (jnp.max(low.reshape(-1, QB), axis=1) > jnp.arange(total // QB) * QB).astype(jnp.int32)
    low = low.reshape(1, total)
    early = WINDOW // QB
    later = total // QB - early
    kv, cot_first = tie(kv, cot_first)
    ot, lse_later = attention_forward(early, later, order, need, low, qt, None, kv, vecs, lanes)
    ot, late_cotangent, kvp, out_far, out_near = tie(ot, cotangent, kvp, out_far, out_near)
    w_outs = (w_out, out_far, out_near, swap(out_far, "head", 1))
    ot, lse_early = attention_forward(0, early, order, need, low, qt, kvp, kv, vecs, lanes, ot)
    noted = lax.all_to_all(
        send_noted(late_cotangent, code_t, partner, blocks, slot_rows), "seq", split_axis=0, concat_axis=0, tiled=True
    )
    ots = trade(ot)

    y, *sends = middle(ots, w_outs, x, gain_two, code_t, slots)
    sends[0], noted = tie(sends[0], noted)
    other = noted[:, :local, :slot_rows].astype(jnp.int32).transpose(1, 0, 2).reshape(local, slots, 1)
    cot_slots = [cot_first, noted[:, NOTES:, :].reshape(slots, width)]
    mine = (place * local).astype(jnp.int32).reshape(1)
    backs = [dot(cot_slots[i], second_full[i], NT).astype(bfloat) for i in range(local)]
    received = [exchange(sends[0])]
    sends[1], *backs = tie(sends[1], *backs)
    received.append(exchange(sends[1]))

    def run_expert(number):
        return expert(
            mine + number,
            received[number],
            router_t,
            other[number],
            first_full,
            second_full,
            backs[number],
            cot_slots[number],
            number,
        )

    *grads0, dx0, z0, m0 = run_expert(0)
    dx0, received[1] = tie(dx0, received[1])
    returns = [exchange(dx0)]
    *grads1, dx1, z1, m1 = run_expert(1)
    def near_terms(value):
        value = value.reshape(lanes, part, -1)
        cross = swap(at(value, 3), "head", 1)
        direct = swap(at(value, 1), "head", 1)
        return (
            (at(value, 2).astype(single) + cross.astype(single)).astype(bfloat),
            at(value, 0).astype(single) + direct.astype(single),
        )

    def scatter(value):
        return lax.psum_scatter(value, "head", scatter_dimension=0, tiled=True)

    away0, home0 = near_terms(grads0[0])
    second0 = scatter(grads0[1])
    across0 = swap(away0, "head", 2)
    away1, home1 = near_terms(grads1[0])
    second1 = scatter(grads1[1])

    returns[0], dx1 = tie(returns[0], dx1)
    returns.append(exchange(dx1))
    grad_router = dot(received[0], m0, TN) + dot(received[1], m1, TN)

    w_rows_full, returns[1], away1, home1, across0, home0 = tie(w_rows_full, returns[1], away1, home1, across0, home0)
    dy, douts, grad_outw, grad_gain_two = return_rows(
        order, returns[0], returns[1], code, y, gain_two, cotangent, w_outs, ots
    )
    across1 = swap(away1, "head", 2)
    dy, z0, z1 = tie(dy, z0, z1)
    z_back = [exchange(z0), exchange(z1)]
    douts = trade(douts)
    first0 = home0 + across0.astype(single)
    first1 = home1 + across1.astype(single)
    douts[3], first0, first1 = tie(douts[3], first0, first1)
    mixed = jnp.concatenate(
        [grad_outw, grad_router.astype(bfloat), grad_gain_two.astype(bfloat).T, jnp.zeros((width, 111 - experts % 128), bfloat)],
        axis=1,
    )

    def sum_blocks(value):
        count, last = value.shape[1:]
        value = value.reshape(lanes * blocks, count // blocks, last)
        value = lax.all_to_all(value, ("head", "seq"), split_axis=0, concat_axis=0, tiled=True)
        return jnp.sum(value.reshape(lanes, blocks, -1, last).astype(single), axis=1).astype(bfloat)

    dq_early, dkvt_early, ds_early = attention_backward(
        0, early, (0, heads), order, need, low, qt, kvp, kv, vecs, lse_early, douts
    )
    behind = lax.ppermute(
        dkvt_early[:, :, :WINDOW].astype(bfloat), "seq", [(i + 1, i) for i in range(blocks - 1)]
    )
    mixed = lax.psum_scatter(mixed, "head", scatter_dimension=0, tiled=True)
    dkvt_early, mixed, z_back[0], second0 = tie(dkvt_early, mixed, z_back[0], second0)
    mixed = lax.psum(mixed, "seq")
    cut = heads - 1

    def later_part(span):
        return attention_backward(
            early, later, span, order, need, low, qt, None, kv, vecs, lse_later, douts, (dkvt_early, ds_early)
        )

    pieces = []
    span = (0, cut)
    dq, dkvt, sums0 = later_part(span)
    dkvt, z_back[1] = tie(dkvt, z_back[1])
    parts, grad_part = settle(span, order, dq_early, dq, dkvt, behind, normed)
    ds_early, second1, parts, grad_part = tie(ds_early, second1, parts, grad_part)
    pieces += trade(parts)
    summed = [sum_blocks(grad_part.reshape(-1, lanes, part).transpose(1, 0, 2))]
    span = (cut, heads - cut)
    dq, dkvt, sums1 = later_part(span)
    dkvt, summed[0] = tie(dkvt, summed[0])
    parts, grad_part = settle(span, order, dq_early, dq, dkvt, behind, normed)
    pieces += trade(parts)
    grad_hidden = tail(order, pieces, w_rows_full, x, gain_one, dy).reshape(hidden_in.shape)
    output = finish(z_back[0], z_back[1], code, y).reshape(hidden_in.shape)

    grad_rel = jnp.dot(
        jnp.concatenate([sums0, sums1], axis=0)[:, :CHUNKS].reshape(heads, -1),
        jnp.asarray(hot, single),
        precision=lax.Precision.HIGHEST,
    ).reshape(-1)
    rel_row = jnp.concatenate([grad_rel.astype(bfloat), jnp.zeros((part - grad_rel.shape[0],), bfloat)])
    rel_rows = jnp.zeros((lanes, blocks, part), bfloat)
    rel_rows = lax.dynamic_update_slice(rel_rows, rel_row[None, None, :], (lane, 0, 0))
    value = jnp.concatenate([grad_part.reshape(-1, lanes, part).transpose(1, 0, 2), rel_rows], axis=1)
    summed.append(sum_blocks(value))
    split = summed[0].shape[1]
    value = jnp.concatenate(summed, axis=1)
    value, grad_hidden, mixed = tie(value, grad_hidden, mixed)
    value = lax.all_to_all(
        jnp.broadcast_to(value[None], (blocks,) + value.shape), "seq", split_axis=0, concat_axis=0, tiled=True
    )
    value = value.transpose(1, 0, 2, 3)
    summed = [
        value[:, :, :split].reshape(lanes, blocks * split, part),
        value[:, :, split:].reshape(lanes, -1, part),
    ]
    grad_rel = jnp.sum(summed[1][:, -blocks, : heads * BUCKETS].astype(single), axis=0)
    summed[1] = summed[1][:, :-blocks, :]
    rows_all = jnp.concatenate(summed, axis=1).reshape(lanes, heads, 3, HEAD_DIM, part)
    grads = rows_all.transpose(2, 4, 0, 1, 3).reshape(3, part, width).astype(single)
    grad_norm1 = sum(
        jnp.sum(grads[i] * weight.astype(single), axis=1) for i, weight in enumerate((w_query, w_key, w_value))
    ) / norm1_gain.astype(single)
    return (
        output,
        grad_hidden,
        grad_norm1,
        grads[0],
        grads[1],
        grads[2],
        mixed[:, :width].astype(single),
        grad_rel,
        mixed[:, width + experts].astype(single),
        mixed[:, width : width + experts].astype(single),
        jnp.stack([first0, first1]),
        jnp.stack([second0, second1]).astype(single),
    )


def solution(mesh):
    return jax.shard_map(
        per_device,
        mesh=mesh,
        in_specs=(
            P("seq", "head", None, None),
            P("head"),
            P("head", None),
            P("head", None),
            P("head", None),
            P("head", None),
            P("head"),
            P("head"),
            P("head", None),
            P("seq", "head", None),
            P("seq", "head", None),
            P("seq", "head", None, None),
            P("seq", "head", None, None),
            P(),
            P("seq", "head", None, None),
        ),
        out_specs=(
            P("seq", "head", None, None),
            P("seq", "head", None, None),
            P("head"),
            P("head", None),
            P("head", None),
            P("head", None),
            P("head", None),
            P("head"),
            P("head"),
            P("head", None),
            P("seq", "head", None),
            P("seq", "head", None),
        ),
        check_vma=False,
    )
```

time: 1520 us -> 732 us (0.48)
  matrix products: 392 us -> 24.7 us
  Pallas kernels: 0 us -> 247 us
  local copies, waits for them, and re-layouts: 339 us -> 93.6 us
  other arithmetic: 216 us -> 46.3 us
  blocking collectives: 143 us -> 0 us
  waiting for transfers between devices: 300 us -> 201 us
  loops' own time: 39.7 us -> 0 us
  starting transfers between devices: 60.1 us -> 90.8 us
    dot_general x58 -> x6, matrix products: 392 us -> 24.7 us  [the longest x5 24 us: dot(): lax.dot_general(a, b, (dims, ((), ())), preferred_element_type=single)]
    pallas_call x0 -> x17, Pallas kernels: none -> 247 us  [the longest x2 99.3 us: expert(): pl.pallas_call(expert_kernel, grid=(inner // block,), in_specs=[SMEM, who...]
    all_to_all x9 -> x11, waiting for transfers between devices: 200 us -> 90.6 us  [the longest x7 81.3 us: exchange(): lax.all_to_all(value.reshape(blocks, slot_rows, -1), 'seq', split_axis=0,...]
    convert_element_type x30 -> x2, local copies, waits for them, and re-layouts: 102 us -> 0.92 us  [the longest x1 0.83 us: per_device(): grad_router.astype(bfloat)]
    dynamic_update_slice x10 -> x1, local copies, waits for them, and re-layouts: 76 us -> 0.04 us  [per_device(): lax.dynamic_update_slice(rel_rows, rel_row[None, None, :], (lane, 0, 0))]
    unnamed x3 -> x0, blocking collectives: 59.5 us -> none
    all_to_all x3 -> x0, blocking collectives: 57.2 us -> none  [the longest x1 21.4 us: per_device(): lax.all_to_all(dvalue_own.astype(bfloat), 'head', split_axis=0, concat_ax...]
    add x9 -> x5, other arithmetic: 72.7 us -> 20.2 us  [the longest x2 9.97 us: near_terms(): at(value, 0).astype(single) + direct.astype(single)]
  transfers between devices with their start and end apart: 27 -> 52, of which waited for: 12 -> 17; matrix products, arithmetic and copies ran while one was open for 59% -> 14% of each run, Pallas kernels for 0% -> 34%
where the time goes in v1:
time: 732 us; the launch traced here: 721 us
  Pallas kernels  247 us (34%)
  waiting for transfers between devices  201 us (27%)
  local copies, waits for them, and re-layouts  93.6 us (13%)
  starting transfers between devices  90.8 us (12%)
  other arithmetic  46.3 us (6%)
  matrix products  24.7 us (3%)
  between operations  17.5 us (2%)
    pallas_call x2, Pallas kernels, expert(): pl.pallas_call(expert_kernel, grid=(inner // block,), in_specs=[SMEM, who...  99.3 us
    all_to_all x7, waiting for transfers between devices, exchange(): lax.all_to_all(value.reshape(blocks, slot_rows, -1), 'seq', split_axis=0,...  81.3 us
    pallas_call x3, Pallas kernels, attention_backward(): pl.pallas_call(kernel, grid=(steps,), in_specs=specs, out_specs=out_specs...  67.3 us
    ppermute x32, waiting for transfers between devices, swap(): lax.ppermute(value, axis, [(i, i ^ mask) for i in range(lax.axis_size(axi...  64.1 us
    unnamed x191, local copies, waits for them, and re-layouts  52.1 us
    psum x1, waiting for transfers between devices, per_device(): mixed = lax.psum(mixed, 'seq')  44.6 us
    all_to_all x7, starting transfers between devices, exchange(): lax.all_to_all(value.reshape(blocks, slot_rows, -1), 'seq', split_axis=0,...  37.2 us
    pallas_call x2, Pallas kernels, attention_forward(): pl.pallas_call(functools.partial(forward_kernel, first), grid=(steps,), i...  29.2 us
  transfers between devices with their start and end apart: 52, of which 17 were waited for; matrix products, arithmetic and copies ran while one was open for 14% of the time, Pallas kernels for 34%

profile of v1, /device:TPU:0, one launch (start us, length us, event | category | flops | bytes accessed | tf_op | source)
XLA Modules:
  0.0 721.0 jit_solution(14912017511138409923)
XLA Ops:
  71.7 6.2 project.1
  87.3 19.0 %all-to-all-done = bf16[8,160,768]{2,1,0:T(8,128)(2,1)} async-done(((bf16[8,160,768]{2,1,0:T(8,128)(2,1)}), bf16[8,160,768]{2,1,0:T(8,128)(2,1)}, u32[]{:S(2)}, u32[]{:S(2)}) %all-to-all-start) | async-done | bytes 1966112 | tf_op jit(solution)/shard_map/all_to_all | solution.py:827
  107.4 16.7 %attend.2 = (bf16[4,192,640]{2,1,0:T(8,128)(2,1)S(1)}, f32[6,8,256]{2,1,0:T(8,128)S(1)}) custom-call(s32[4]{0:T(128)S(1)} %pad_add_fusion.3.order, s32[10]{0:T(128)S(1)} %compare_convert_fusion.need, s32[1,2560]{1,0:T(1,128)S(1)} %reshape.182.low, bf16[192,2560]{1,0:T(8,128)(2,1)S(1)} %copy-done.59, bf16[3,2560,128]{2,1,0:T(8,128)(2,1)S(1)} %get-tuple-element.125.keys_in, ...), custom_call_target="tpu_custom_call" | custom-call | flops 12079595520 | bytes 3932160 | tf_op jit(solution)/shard_map/attend/pallas_call | solution.py:252
  138.6 12.5 %attend.3 = (bf16[4,192,640]{2,1,0:T(8,128)(2,1)S(1)}, f32[4,8,256]{2,1,0:T(8,128)S(1)}) custom-call(s32[4]{0:T(128)S(1)} %pad_add_fusion.3.order, s32[10]{0:T(128)S(1)} %compare_convert_fusion.need, s32[1,2560]{1,0:T(1,128)S(1)} %reshape.182.low, bf16[192,2560]{1,0:T(8,128)(2,1)S(1)} %copy-done.60, bf16[3,2560,128]{2,1,0:T(8,128)(2,1)S(1)} %get-tuple-element.125.keys_in, ...), custom_call_target="tpu_custom_call" | custom-call | flops 8053063680 | bytes 3932160 | tf_op jit(solution)/shard_map/attend/pallas_call | solution.py:252
  153.5 11.9 %collective-permute-done.14.o1 = bf16[192,640]{1,0:T(8,128)(2,1)S(1)} collective-permute-done((bf16[192,640]{1,0:T(8,128)(2,1)S(1)}, bf16[192,640]{1,0:T(8,128)(2,1)S(1)}, u32[]{:S(2)}, u32[]{:S(2)}) %collective-permute-start.14) | collective-permute-done | bytes 245792 | tf_op jit(solution)/shard_map/ppermute | solution.py:766
  165.4 9.9 %collective-permute-done.16.o3 = bf16[192,640]{1,0:T(8,128)(2,1)S(1)} collective-permute-done((bf16[192,640]{1,0:T(8,128)(2,1)S(1)}, bf16[192,640]{1,0:T(8,128)(2,1)S(1)}, u32[]{:S(2)}, u32[]{:S(2)}) %collective-permute-start.16) | collective-permute-done | bytes 245792 | tf_op jit(solution)/shard_map/ppermute | solution.py:766
  175.3 7.9 %middle.1 = (f32[640,768]{1,0:T(8,128)S(1)}, bf16[1280,768]{1,0:T(8,128)(2,1)}, bf16[1280,768]{1,0:T(8,128)(2,1)}) custom-call(bf16[192,640]{1,0:T(8,128)(2,1)S(1)} %get-tuple-element.301.o0, bf16[192,640]{1,0:T(8,128)(2,1)S(1)} %collective-permute-done.14.o1, bf16[192,640]{1,0:T(8,128)(2,1)S(1)} %collective-permute-done.15.o2, ...), custom_call_target="tpu_custom_call" | custom-call | flops 3271557120 | bytes 3932160 | tf_op jit(solution)/shard_map/middle/pallas_call | solution.py:479
  189.8 6.4 all-to-all-start.2
  197.6 11.3 %convolution_convert_fusion.da = bf16[1280,3072]{1,0:T(8,128)(2,1)} fusion(bf16[1280,768]{1,0:T(8,128)(2,1)} %bitcast.178, bf16[2,3072,768]{2,1,0:T(8,128)(2,1)} %all-gather.6.cloned.1.call-done.w2), kind=kOutput, calls=%fused_computation | convolution fusion | flops 6043729920 | bytes 14548992 | tf_op jit(solution)/shard_map/dot_general | solution.py:28
  208.8 10.2 %convolution_convert_fusion.1.da = bf16[1280,3072]{1,0:T(8,128)(2,1)} fusion(bf16[1280,768]{1,0:T(8,128)(2,1)} %bitcast.14.cot, bf16[2,3072,768]{2,1,0:T(8,128)(2,1)S(1)} %copy-done.85), kind=kOutput, calls=%fused_computation.1 | convolution fusion | flops 6043729920 | bytes 14548992 | tf_op jit(solution)/shard_map/dot_general | solution.py:28
  219.0 23.2 %all-to-all-done.2 = bf16[8,160,768]{2,1,0:T(8,128)(2,1)S(1)} async-done(((bf16[8,160,768]{2,1,0:T(8,128)(2,1)}), bf16[8,160,768]{2,1,0:T(8,128)(2,1)S(1)}, u32[]{:S(2)}, u32[]{:S(2)}) %all-to-all-start.2) | async-done | bytes 1966112 | tf_op jit(solution)/shard_map/all_to_all | solution.py:827
  247.9 49.1 %expert.2 = (bf16[768,3072]{1,0:T(8,128)(2,1)}, bf16[3072,768]{1,0:T(8,128)(2,1)}, bf16[1280,768]{1,0:T(8,128)(2,1)}, bf16[1280,768]{1,0:T(8,128)(2,1)}, bf16[1280,16]{1,0:T(8,128)(2,1)}) custom-call(s32[1]{0:T(128)} %bitcast.16.mine, bf16[1280,768]{1,0:T(8,128)(2,1)} %bitcast.159, bf16[16,768]{1,0:T(8,128)(2,1)} %copy-done.61, s32[1280,1]{1,0:T(8,128)} %squeeze.118.other, ...), custom_call_target="tpu_custom_call" | custom-call | flops 60397977600 | bytes 50331648 | tf_op jit(solution)/shard_map/expert/pallas_call | solution.py:718
  303.1 50.2 %expert.3 = (bf16[768,3072]{1,0:T(8,128)(2,1)}, bf16[3072,768]{1,0:T(8,128)(2,1)}, bf16[1280,768]{1,0:T(8,128)(2,1)}, bf16[1280,768]{1,0:T(8,128)(2,1)}, bf16[1280,16]{1,0:T(8,128)(2,1)}) custom-call(s32[1]{0:T(128)S(6)} %add.103.mine, bf16[1280,768]{1,0:T(8,128)(2,1)} %bitcast.28.xs, bf16[16,768]{1,0:T(8,128)(2,1)} %copy-done.61, ...), custom_call_target="tpu_custom_call" | custom-call | flops 60397977600 | bytes 50331648 | tf_op jit(solution)/shard_map/expert/pallas_call | solution.py:718
  383.3 19.2 %collective-permute-done.21 = bf16[192,3072]{1,0:T(8,128)(2,1)} collective-permute-done((bf16[192,3072]{1,0:T(8,128)(2,1)}, bf16[192,3072]{1,0:T(8,128)(2,1)}, u32[]{:S(2)}, u32[]{:S(2)}) %collective-permute-start.21) | collective-permute-done | bytes 1179680 | tf_op jit(solution)/shard_map/ppermute | solution.py:766
  408.0 11.1 %return_rows.1 = (f32[640,768]{1,0:T(8,128)}, bf16[4,192,640]{2,1,0:T(8,128)(2,1)S(1)}, bf16[768,768]{1,0:T(8,128)(2,1)S(1)}, f32[1,768]{1,0:T(1,128)S(1)}) custom-call(s32[4]{0:T(128)S(1)} %pad_add_fusion.3.order, bf16[1280,768]{1,0:T(8,128)(2,1)} %bitcast.176, bf16[1280,768]{1,0:T(8,128)(2,1)} %bitcast.32.d1, s32[640,2]{1,0:T(8,128)S(1)} %get-tuple-element.303.code, ...), custom_call_target="tpu_custom_call" | custom-call | flops 4026531840 | bytes 7864320 | tf_op jit(solution)/shard_map/return_rows/pallas_call | solution.py:583
  434.6 36.7 %all-to-all-done.6 = bf16[8,160,768]{2,1,0:T(8,128)(2,1)S(1)} async-done(((bf16[8,160,768]{2,1,0:T(8,128)(2,1)}), bf16[8,160,768]{2,1,0:T(8,128)(2,1)S(1)}, u32[]{:S(2)}, u32[]{:S(2)}) %all-to-all-start.6) | async-done | bytes 1966112 | tf_op jit(solution)/shard_map/all_to_all | solution.py:827
  482.0 21.6 %attend_back.3 = (bf16[192,1024]{1,0:T(8,128)(2,1)}, f32[3,128,2048]{2,1,0:T(8,128)}, f32[3,1280,256]{2,1,0:T(8,128)}) custom-call(s32[5]{0:T(128)} %concatenate.56.order, s32[10]{0:T(128)} %copy-done.55, s32[1,2560]{1,0:T(1,128)} %copy-done.32, bf16[192,2560]{1,0:T(8,128)(2,1)} %copy-done.58, bf16[3,2560,128]{2,1,0:T(8,128)(2,1)} %copy-done.25, ...), custom_call_target="tpu_custom_call" | custom-call | flops 16106127360 | bytes 7864320 | tf_op jit(solution)/shard_map/attend_back/pallas_call | solution.py:400
  506.6 29.5 %attend_back.4 = (bf16[128,1536]{1,0:T(8,128)(2,1)}, f32[2,128,2560]{2,1,0:T(8,128)}, f32[2,8,512]{2,1,0:T(8,128)}) custom-call(s32[5]{0:T(128)} %concatenate.56.order, s32[10]{0:T(128)} %copy-done.55, s32[1,2560]{1,0:T(1,128)} %copy-done.32, bf16[192,2560]{1,0:T(8,128)(2,1)} %copy-done.58, bf16[3,2560,128]{2,1,0:T(8,128)(2,1)} %copy-done.25, ...), custom_call_target="tpu_custom_call" | custom-call | flops 16106127360 | bytes 5242880 | tf_op jit(solution)/shard_map/attend_back/pallas_call | solution.py:400
  548.8 7.5 %all-to-all-start.8 = ((bf16[32,48,192]{2,1,0:T(8,128)(2,1)}), bf16[32,48,192]{2,1,0:T(8,128)(2,1)}, u32[]{:S(2)}, u32[]{:S(2)}) async-start(bf16[32,48,192]{2,1,0:T(8,128)(2,1)} %bitcast.170), calls=%async_computation.11 | async-start | bytes 1572864 | tf_op jit(solution)/shard_map/all_to_all | solution.py:954
  559.8 16.2 %attend_back.5 = (bf16[64,1536]{1,0:T(8,128)(2,1)}, f32[1,128,2560]{2,1,0:T(8,128)}, f32[1,8,512]{2,1,0:T(8,128)}) custom-call(s32[5]{0:T(128)} %concatenate.66.order, s32[10]{0:T(128)} %copy-done.55, s32[1,2560]{1,0:T(1,128)} %copy-done.32, bf16[192,2560]{1,0:T(8,128)(2,1)} %copy-done.58, bf16[3,2560,128]{2,1,0:T(8,128)(2,1)} %copy-done.25, ...), custom_call_target="tpu_custom_call" | custom-call | flops 8053063680 | bytes 2621440 | tf_op jit(solution)/shard_map/attend_back/pallas_call | solution.py:400
  598.5 9.9 %collective-permute-done.31.refs_5_ = bf16[192,640]{1,0:T(8,128)(2,1)} collective-permute-done((bf16[192,640]{1,0:T(8,128)(2,1)}, bf16[192,640]{1,0:T(8,128)(2,1)}, u32[]{:S(2)}, u32[]{:S(2)}) %collective-permute-start.31) | collective-permute-done | bytes 245792 | tf_op jit(solution)/shard_map/ppermute | solution.py:766
  617.8 6.6 tail.1
  626.4 44.6 %all-reduce.4.cloned.1.call-done = bf16[192,880]{1,0:T(8,128)(2,1)} async-done(((bf16[192,880]{1,0:T(8,128)(2,1)}), bf16[192,880]{1,0:T(8,128)(2,1)}) %all-reduce.4.cloned.1.call-update) | async-done | bytes 337936 | tf_op jit(solution)/shard_map/psum | solution.py:965
  695.9 8.8 %all-to-all-done.10 = bf16[8,4,73,192]{3,1,2,0:T(4,128)(2,1)} async-done(((bf16[8,4,73,192]{3,1,2,0:T(4,128)(2,1)}), bf16[8,4,73,192]{3,1,2,0:T(4,128)(2,1)}, u32[]{:S(2)}, u32[]{:S(2)}) %all-to-all-start.10) | async-done | bytes 897056 | tf_op jit(solution)/shard_map/all_to_all | solution.py:1002
  (397 shorter events, 257.3 us)
Async XLA Ops:
  7.2 190.4 %all-gather.6.cloned.1.call-start = ((), (), s32[]{:S(2)}) async-start(), calls=%async_computation.15 | async-start | bytes 11796480 | tf_op jit(solution)/shard_map/all_gather | solution.py:853
  53.4 194.5 %all-gather.4.cloned.1.call-start = ((), (), s32[]{:S(2)}) async-start(), calls=%async_computation.14 | async-start | bytes 11796480 | tf_op jit(solution)/shard_map/all_gather | solution.py:854
  54.3 51.9 %all-to-all-start = ((bf16[8,160,768]{2,1,0:T(8,128)(2,1)}), bf16[8,160,768]{2,1,0:T(8,128)(2,1)}, u32[]{:S(2)}, u32[]{:S(2)}) async-start(bf16[8,160,768]{2,1,0:T(8,128)(2,1)} %bitcast.13), calls=%async_computation | async-start | bytes 3932160 | tf_op jit(solution)/shard_map/all_to_all | solution.py:827
  65.3 60.4 %collective-permute-start.12 = (bf16[192,768]{1,0:T(8,128)(2,1)}, bf16[192,768]{1,0:T(8,128)(2,1)}, u32[]{:S(2)}, u32[]{:S(2)}) collective-permute-start(bf16[192,768]{1,0:T(8,128)(2,1)} %w0.1), channel_id=1, source_target_pairs={{0,16},{8,24},{16,0},{24,8},{1,17},{9,25},{17,1},{25,9},{2,18},{10... | collective-permute-start | bytes 884744 | tf_op jit(solution)/shard_map/ppermute | solution.py:766
  65.9 59.9 %collective-permute-start.13 = (bf16[192,768]{1,0:T(8,128)(2,1)}, bf16[192,768]{1,0:T(8,128)(2,1)}, u32[]{:S(2)}, u32[]{:S(2)}) collective-permute-start(bf16[192,768]{1,0:T(8,128)(2,1)} %w0.1), channel_id=1, source_target_pairs={{0,8},{8,0},{16,24},{24,16},{1,9},{9,1},{17,25},{25,17},{2,10},{10... | collective-permute-start | bytes 884744 | tf_op jit(solution)/shard_map/ppermute | solution.py:766
  82.4 43.3 %collective-permute-start.11 = (bf16[3,1024,128]{2,1,0:T(8,128)(2,1)}, bf16[3,1024,128]{2,1,0:T(8,128)(2,1)}, u32[]{:S(2)}, u32[]{:S(2)}) collective-permute-start(bf16[3,1024,128]{2,1,0:T(8,128)(2,1)} %slice.128), channel_id=1, source_target_pairs={{0,1},{1,2},{2,3},{3,4},{4,5},{5,6},{6,7},{8,9},{9,10},{10,11},{11... | collective-permute-start | bytes 2359304 | tf_op jit(solution)/shard_map/ppermute | solution.py:860
  130.9 53.8 %all-to-all-start.1 = ((bf16[8,176,768]{2,1,0:T(8,128)(2,1)}), bf16[8,176,768]{2,1,0:T(8,128)(2,1)}, u32[]{:S(2)}, u32[]{:S(2)}) async-start(bf16[8,176,768]{2,1,0:T(8,128)(2,1)} %send_noted.1), calls=%async_computation.1 | async-start | bytes 4325376 | tf_op jit(solution)/shard_map/all_to_all | solution.py:881
  135.7 247.6 %all-gather.8.cloned.1.call-start = ((), (), s32[]{:S(2)}) async-start(), calls=%async_computation.16 | async-start | bytes 4423680 | tf_op jit(solution)/shard_map/all_gather | solution.py:858
  135.9 39.4 %collective-permute-start.17 = (bf16[192,768]{1,0:T(8,128)(2,1)}, bf16[192,768]{1,0:T(8,128)(2,1)}, u32[]{:S(2)}, u32[]{:S(2)}) collective-permute-start(bf16[192,768]{1,0:T(8,128)(2,1)} %collective-permute-done.12.w1), channel_id=1, source_target_pairs={{0,8},{8,0},{16,24},{24,16},{1,9},{9,1},{17,25},{25,17},{2,10},{10... | collective-permute-start | bytes 884744 | tf_op jit(solution)/shard_map/ppermute | solution.py:766
  189.8 52.4 %all-to-all-start.2 = ((bf16[8,160,768]{2,1,0:T(8,128)(2,1)}), bf16[8,160,768]{2,1,0:T(8,128)(2,1)S(1)}, u32[]{:S(2)}, u32[]{:S(2)}) async-start(bf16[8,160,768]{2,1,0:T(8,128)(2,1)} %bitcast.21), calls=%async_computation.2 | async-start | bytes 3932160 | tf_op jit(solution)/shard_map/all_to_all | solution.py:827
  243.5 53.6 %all-to-all-start.3 = ((bf16[8,160,768]{2,1,0:T(8,128)(2,1)}), bf16[8,160,768]{2,1,0:T(8,128)(2,1)}, u32[]{:S(2)}, u32[]{:S(2)}) async-start(bf16[8,160,768]{2,1,0:T(8,128)(2,1)} %bitcast.27), calls=%async_computation.3 | async-start | bytes 3932160 | tf_op jit(solution)/shard_map/all_to_all | solution.py:827
  247.8 258.7 %reduce-scatter.6.cloned.1.call-start = ((), (), s32[]{:S(2)}) async-start(), calls=%async_computation.18 | async-start | bytes 5898240 | tf_op jit(solution)/shard_map/reduce_scatter | solution.py:923
  297.1 56.2 %all-to-all-start.4 = ((bf16[8,160,768]{2,1,0:T(8,128)(2,1)}), bf16[8,160,768]{2,1,0:T(8,128)(2,1)S(1)}, u32[]{:S(2)}, u32[]{:S(2)}) async-start(bf16[8,160,768]{2,1,0:T(8,128)(2,1)} %bitcast.180), calls=%async_computation.4 | async-start | bytes 3932160 | tf_op jit(solution)/shard_map/all_to_all | solution.py:827
  354.6 50.2 %all-to-all-start.5 = ((bf16[8,160,768]{2,1,0:T(8,128)(2,1)}), bf16[8,160,768]{2,1,0:T(8,128)(2,1)}, u32[]{:S(2)}, u32[]{:S(2)}) async-start(bf16[8,160,768]{2,1,0:T(8,128)(2,1)} %bitcast.177), calls=%async_computation.5 | async-start | bytes 3932160 | tf_op jit(solution)/shard_map/all_to_all | solution.py:827
  360.8 145.8 %reduce-scatter.4.cloned.1.call-start = ((), (), s32[]{:S(2)}) async-start(), calls=%async_computation.17 | async-start | bytes 1720320 | tf_op jit(solution)/shard_map/reduce_scatter | solution.py:963
  421.7 122.7 %reduce-scatter.8.cloned.1.call-start = ((), (), s32[]{:S(2)}) async-start(), calls=%async_computation.19 | async-start | bytes 5898240 | tf_op jit(solution)/shard_map/reduce_scatter | solution.py:923
  422.3 49.0 %all-to-all-start.6 = ((bf16[8,160,768]{2,1,0:T(8,128)(2,1)}), bf16[8,160,768]{2,1,0:T(8,128)(2,1)S(1)}, u32[]{:S(2)}, u32[]{:S(2)}) async-start(bf16[8,160,768]{2,1,0:T(8,128)(2,1)} %bitcast.175), calls=%async_computation.7 | async-start | bytes 3932160 | tf_op jit(solution)/shard_map/all_to_all | solution.py:827
  425.9 51.5 %collective-permute-start.26 = (bf16[192,3072]{1,0:T(8,128)(2,1)}, bf16[192,3072]{1,0:T(8,128)(2,1)}, u32[]{:S(2)}, u32[]{:S(2)}) collective-permute-start(bf16[192,3072]{1,0:T(8,128)(2,1)} %get-tuple-element.163), channel_id=1, source_target_pairs={{0,16},{8,24},{16,0},{24,8},{1,17},{9,25},{17,1},{25,9},{2,18},{10... | collective-permute-start | bytes 3538952 | tf_op jit(solution)/shard_map/ppermute | solution.py:766
  429.0 52.1 %collective-permute-start.25 = (bf16[192,640]{1,0:T(8,128)(2,1)}, bf16[192,640]{1,0:T(8,128)(2,1)S(1)}, u32[]{:S(2)}, u32[]{:S(2)}) collective-permute-start(bf16[192,640]{1,0:T(8,128)(2,1)} %get-tuple-element.294), channel_id=1, source_target_pairs={{0,24},{8,16},{16,8},{24,0},{1,25},{9,17},{17,9},{25,1},{2,26},{10... | collective-permute-start | bytes 737288 | tf_op jit(solution)/shard_map/ppermute | solution.py:766
  429.0 52.1 %collective-permute-start.23 = (bf16[192,640]{1,0:T(8,128)(2,1)}, bf16[192,640]{1,0:T(8,128)(2,1)S(1)}, u32[]{:S(2)}, u32[]{:S(2)}) collective-permute-start(bf16[192,640]{1,0:T(8,128)(2,1)} %get-tuple-element.296), channel_id=1, source_target_pairs={{0,16},{8,24},{16,0},{24,8},{1,17},{9,25},{17,1},{25,9},{2,18},{10... | collective-permute-start | bytes 737288 | tf_op jit(solution)/shard_map/ppermute | solution.py:766
  430.1 51.1 %collective-permute-start.24 = (bf16[192,640]{1,0:T(8,128)(2,1)S(1)}, bf16[192,640]{1,0:T(8,128)(2,1)S(1)}, u32[]{:S(2)}, u32[]{:S(2)}) collective-permute-start(bf16[192,640]{1,0:T(8,128)(2,1)S(1)} %get-tuple-element.295), channel_id=1, source_target_pairs={{0,8},{8,0},{16,24},{24,16},{1,9},{9,1},{17,25},{25,17},{2,10},{10... | collective-permute-start | bytes 737288 | tf_op jit(solution)/shard_map/ppermute | solution.py:766
  472.6 63.4 %all-to-all-start.7 = ((bf16[8,160,768]{2,1,0:T(8,128)(2,1)}), bf16[8,160,768]{2,1,0:T(8,128)(2,1)}, u32[]{:S(2)}, u32[]{:S(2)}) async-start(bf16[8,160,768]{2,1,0:T(8,128)(2,1)} %bitcast.174), calls=%async_computation.9 | async-start | bytes 3932160 | tf_op jit(solution)/shard_map/all_to_all | solution.py:827
  557.7 40.3 %collective-permute-start.28 = (bf16[384,640]{1,0:T(8,128)(2,1)}, bf16[384,640]{1,0:T(8,128)(2,1)}, u32[]{:S(2)}, u32[]{:S(2)}) collective-permute-start(bf16[384,640]{1,0:T(8,128)(2,1)} %get-tuple-element.288), channel_id=1, source_target_pairs={{0,16},{8,24},{16,0},{24,8},{1,17},{9,25},{17,1},{25,9},{2,18},{10... | collective-permute-start | bytes 1474568 | tf_op jit(solution)/shard_map/ppermute | solution.py:766
  593.7 77.3 %all-reduce.4.cloned.1.call-start = ((), (), s32[]{:S(2)}) async-start(), calls=%async_computation.20 | async-start | bytes 688128 | tf_op jit(solution)/shard_map/psum | solution.py:965
  (118 other events, 2282.3 us)
Sparse Core Ops, SparseCore 0:
  53.5 70.8 all-gather.5
  126.0 74.7 all-gather.3
  202.4 30.7 all-gather.7
  297.2 48.3 reduce-scatter.5
  421.8 32.8 reduce-scatter.3
  457.1 47.8 reduce-scatter.7
  598.6 72.4 all-reduce.3

commit v2 on v1

v2 whole, which is shorter than its diff:
```python
import functools

import jax
import jax.numpy as jnp
import numpy as np
from jax import lax
from jax.experimental import pallas as pl
from jax.experimental.pallas import tpu as pltpu
from jax.sharding import PartitionSpec as P

HEAD_DIM = 64
WINDOW = 1024
BUCKETS = 32
QB = 256
CHUNKS = WINDOW // QB + 1
KEYS = CHUNKS * QB
MASKED = -1e30
epsilon = 1e-06
bfloat = jnp.bfloat16
single = jnp.float32
MIB = 1 << 20

VMEM = pl.BlockSpec(memory_space=pltpu.VMEM)
SMEM = pl.BlockSpec(memory_space=pltpu.SMEM)


def dot(a, b, dims=((1,), (0,))):
    return lax.dot_general(a, b, (dims, ((), ())), preferred_element_type=single)


NN = ((1,), (0,))
NT = ((1,), (1,))
TN = ((0,), (0,))


def params(mib, grid=0):
    extra = {"dimension_semantics": ("arbitrary",) * grid} if grid else {}
    return pltpu.CompilerParams(vmem_limit_bytes=mib * MIB, **extra)


def full(shape):
    return pl.BlockSpec(tuple(shape), lambda i: (0,) * len(shape))


def once(kernel, name, inputs, outputs, scratch=()):
    found = pl.pallas_call(
        kernel,
        grid=(1,),
        in_specs=[SMEM if value.ndim == 1 else full(value.shape) for value in inputs],
        out_specs=[full(shape) for shape, _ in outputs],
        out_shape=[jax.ShapeDtypeStruct(shape, kind) for shape, kind in outputs],
        scratch_shapes=list(scratch),
        compiler_params=params(60, 1),
        cost_estimate=light(),
        name=name,
    )(*inputs)
    return found


def cost(flops, moved, trans=0):
    return pl.CostEstimate(flops=int(flops), bytes_accessed=int(moved), transcendentals=int(trans))


def light():
    return cost(1000, 1000)


MASKS = (0, 2, 1, 3)


def by_lane(own, action):
    for lane in range(len(MASKS)):

        @pl.when(own == lane)
        def _():
            for place, mask in enumerate(MASKS):
                action(place, lane ^ mask)


def bucket_edges(window_len, bucket_count):
    middle = bucket_count // 2
    edge_list = []
    for number in range(1, bucket_count):
        if number < middle:
            edge_list.append(number)
        else:
            edge_list.append(int(middle * (window_len / middle) ** ((number - middle) / middle)))
    return edge_list


def lane_tables():
    lane = np.arange(2 * QB)
    offset = np.where(lane < QB, lane, lane - 2 * QB)
    distance = WINDOW - QB * np.arange(CHUNKS)[:, None] + offset[None, :]
    allowed = (distance >= 0) & (distance < WINDOW)
    bucket = np.zeros(distance.shape, np.int32)
    for edge_value in bucket_edges(WINDOW, BUCKETS):
        bucket = bucket + (distance >= edge_value)
    hot = (bucket.reshape(-1)[:, None] == np.arange(BUCKETS)[None, :]) & allowed.reshape(-1)[:, None]
    return hot, allowed


GAINS = 16


def pack_kernel(order, wq, wk, wv, router_t, gains, *outs):
    part = wq.shape[0]
    experts = router_t.shape[0]

    def put(place, lane):
        for number, weight in enumerate((wq, wk, wv)):
            outs[place][:, number * part : (number + 1) * part] = weight[:, lane * part : (lane + 1) * part]

    by_lane(order[0], put)
    rest = outs[0].shape[1] - 3 * part
    for ref in outs:
        ref[:experts, 3 * part :] = router_t[...]
        ref[experts : experts + GAINS, 3 * part :] = gains[...]
        ref[experts + GAINS :, 3 * part :] = jnp.zeros((part - experts - GAINS, rest), bfloat)


def pack(order, wq, wk, wv, router_t, gains):
    part, width = wq.shape
    return once(pack_kernel, "pack", (order, wq, wk, wv, router_t, gains), [((part, width), bfloat)] * len(MASKS))


def project_kernel(
    order, x0, x1, x2, x3, p0, p1, p2, p3, n_out, qt_out, kv_out, kv_last, rows_out, router_out, gain_out, wq, wk, wv
):
    rows, width = x0.shape
    heads = kv_out.shape[0]
    part = heads * HEAD_DIM
    experts = router_out.shape[0]
    packed = (p0, p1, p2, p3)
    for place, ref in enumerate(packed):
        at = pl.ds(pl.multiple_of(order[place] * part, 64), part)
        for number, weight in enumerate((wq, wk, wv)):
            weight[at, :] = ref[:, number * part : (number + 1) * part]

    def spread(skip, count):
        found = []
        for lane in range(len(packed)):
            piece = None
            for place, ref in enumerate(packed):
                value = ref[skip : skip + count, 3 * part :]
                piece = value if piece is None else jnp.where(order[place] == lane, value, piece)
            found.append(piece)
        return jnp.concatenate(found, axis=1)

    router_out[...] = spread(0, experts)
    gains = spread(experts, GAINS).astype(single)
    gain_out[...] = gains[0:8, :]
    wq_t = wq[...].T
    k_t = wk[...].T
    v_t = wv[...].T
    for head in range(heads):
        at = slice(head * HEAD_DIM, (head + 1) * HEAD_DIM)
        for number, value in enumerate((wq_t, k_t, v_t)):
            begin = (3 * head + number) * HEAD_DIM
            rows_out[begin : begin + HEAD_DIM, :] = value[at, :]
    for place, ref in enumerate((x0, x1, x2, x3)):
        block = order[place]
        values = ref[...].astype(single)
        inverse = lax.rsqrt(jnp.mean(values * values, axis=-1, keepdims=True) + epsilon)
        normed = (values * inverse * gain_out[0:1, :]).astype(bfloat)
        n_out[block] = normed
        at = pl.ds(pl.multiple_of(block * rows, 128), rows)
        qt = dot(wq_t, normed, NT).astype(bfloat)
        qt_out[:, at] = qt * bfloat(HEAD_DIM**-0.5)
        for head in range(heads):
            begin = 3 * head * HEAD_DIM + HEAD_DIM
            kv = dot(normed, rows_out[begin : begin + 2 * HEAD_DIM, :], NT)
            kv_out[head, at, :] = kv.astype(bfloat)
    kv_last[...] = kv_out[:, kv_out.shape[1] - WINDOW :, :]


def project(order, pieces, packed, heads, experts):
    rows, width = pieces[0].shape
    lanes = len(MASKS)
    total = rows * lanes
    part = heads * HEAD_DIM
    return once(
        project_kernel,
        "project",
        (order, *pieces, *packed),
        [
            ((lanes, rows, width), bfloat),
            ((part, total), bfloat),
            ((heads, total, 2 * HEAD_DIM), bfloat),
            ((heads, WINDOW, 2 * HEAD_DIM), bfloat),
            ((3 * part, width), bfloat),
            ((experts, width), bfloat),
            ((8, width), single),
        ],
        [pltpu.VMEM((width, part), bfloat)] * 3,
    )


def eye(size):
    return (
        lax.broadcasted_iota(jnp.int32, (size, size), 0) == lax.broadcasted_iota(jnp.int32, (size, size), 1)
    ).astype(bfloat)


def stage_attention(kvp, kv, vecs, kv_all, kvt_all, bias):
    heads = kv_all.shape[0]
    unit = eye(2 * HEAD_DIM)
    for head in range(heads):
        if kvp is None:
            kv_all[head] = kv[head]
        else:
            kv_all[head, :WINDOW, :] = kvp[head]
            kv_all[head, WINDOW:, :] = kv[head]
        kvt_all[head] = dot(unit, kv_all[head], NT).astype(bfloat)
        for chunk in range(CHUNKS):
            row = jnp.broadcast_to(vecs[head, chunk : chunk + 1, :], (QB, 2 * QB))
            tile = pltpu.roll(row, 0, 1, stride=1, stride_axis=0)
            bias[head, chunk * QB : (chunk + 1) * QB, :] = tile[:, :QB]


def keep_rows(scores, step, low):
    key = lax.broadcasted_iota(jnp.int32, scores.shape, 0) + step * QB
    return jnp.where(key >= low, scores, MASKED)


def query_tile(step, first, pieces):
    found = []
    for half in range(QB // 128):
        piece = (step + first) * (QB // 128) + half
        found.append((piece // pieces, pl.ds(pl.multiple_of((piece % pieces) * 128, 128), 128)))
    return found


def forward_kernel(first, order, need, low, qt, keys_in, vecs, *rest):
    *more, out0, out1, out2, out3, lse, kv_all, kvt_all, bias = rest
    outs = (out0, out1, out2, out3)
    step = pl.program_id(0)
    heads = kv_all.shape[0]
    pieces = out0.shape[1] // 128

    @pl.when(step == 0)
    def _():
        if more:
            stage_attention(more[0], keys_in, vecs, kv_all, kvt_all, bias)
            for ref, begun in zip(outs, more[1:]):
                ref[...] = begun[...]
        else:
            stage_attention(None, keys_in, vecs, kv_all, kvt_all, bias)

    start = pl.multiple_of(step * QB, QB)

    def run(masked):
        found = []
        for head in range(heads):
            keys = kv_all[head, pl.ds(start, KEYS), :]
            query = qt[head * HEAD_DIM : (head + 1) * HEAD_DIM, :]
            query = jnp.concatenate([query, jnp.zeros_like(query)], axis=0)
            scores = dot(keys, query) + bias[head]
            if masked:
                scores = keep_rows(scores, step + first, low[...])
            peak = jnp.max(scores, axis=0, keepdims=True)
            expo = jnp.exp(scores - peak)
            total = jnp.sum(expo, axis=0, keepdims=True)
            values = kvt_all[head, HEAD_DIM:, pl.ds(start, KEYS)]
            mixed = dot(values, expo.astype(bfloat)) * (1.0 / total)
            found.append(mixed.astype(bfloat))
            lse[0, head : head + 1, :] = peak + jnp.log(total)
        whole = jnp.concatenate(found, axis=0)
        for half, (owner, spot) in enumerate(query_tile(step, first, pieces)):
            for mask, ref in zip(MASKS, outs):

                @pl.when(jnp.bitwise_xor(owner, order[0]) == mask)
                def _():
                    ref[:, spot] = whole[:, half * 128 : (half + 1) * 128]

    pl.when(need[step + first] > 0)(lambda: run(True))
    pl.when(need[step + first] <= 0)(lambda: run(False))


def attention_forward(first, steps, order, need, low, qt, kvp, kv, vecs, lanes, begun=None):
    heads, total, packed = kv.shape
    width = heads * HEAD_DIM
    held = KEYS + (steps - 1) * QB
    own = held - (0 if kvp is None else WINDOW)
    more = [] if kvp is None else [kvp, *begun]
    return pl.pallas_call(
        functools.partial(forward_kernel, first),
        grid=(steps,),
        in_specs=[
            SMEM,
            SMEM,
            pl.BlockSpec((1, QB), lambda i: (0, i + first)),
            pl.BlockSpec((width, QB), lambda i: (0, i + first)),
            pl.BlockSpec((heads, own, packed), lambda i: (0, 0, 0)),
            full(vecs.shape),
        ]
        + [full(value.shape) for value in more],
        out_specs=[full((width, total // lanes))] * lanes + [pl.BlockSpec((1, 8, QB), lambda i: (i, 0, 0))],
        out_shape=[jax.ShapeDtypeStruct((width, total // lanes), bfloat)] * lanes
        + [jax.ShapeDtypeStruct((steps, 8, QB), single)],
        scratch_shapes=[
            pltpu.VMEM((heads, held, packed), bfloat),
            pltpu.VMEM((heads, packed, held), bfloat),
            pltpu.VMEM((heads, KEYS, QB), single),
        ],
        compiler_params=params(60, 1),
        cost_estimate=light(),
        name="attend",
    )(order, need, low, qt, kv, vecs, *more)


def diagonal_sums(tile):
    wide = jnp.concatenate([tile, jnp.zeros_like(tile)], axis=1)
    row = lax.broadcasted_iota(jnp.int32, wide.shape, 0)
    bit = 1
    while bit < QB:
        wide = jnp.where((row & bit) != 0, pltpu.roll(wide, 2 * QB - bit, 1), wide)
        bit *= 2
    return jnp.sum(wide, axis=0, keepdims=True)


def backward_kernel(first, ends, order, need, low, qt, keys_in, vecs, lse, d0, d1, d2, d3, *rest):
    if ends:
        dkvt_in, ds_in, dqt, dkvt, sums, kv_all, kvt_all, bias, dout_all, ds_all = rest
        kvp = None
    else:
        kvp, dqt, behind, dkv_own, ds_all, kv_all, kvt_all, bias, dout_all, dkvt = rest
    step = pl.program_id(0)
    heads = kv_all.shape[0]
    rows = d0.shape[1]

    @pl.when(step == 0)
    def _():
        stage_attention(kvp, keys_in, vecs, kv_all, kvt_all, bias)
        for place, ref in enumerate((d0, d1, d2, d3)):
            dout_all[:, pl.ds(pl.multiple_of(order[place] * rows, 128), rows)] = ref[...]
        if ends:
            ds_all[...] = ds_in[...]
            dkvt[:, :, :WINDOW] = dkvt_in[...]
            dkvt[:, :, WINDOW:] = jnp.zeros_like(dkvt[:, :, WINDOW:])
        else:
            ds_all[...] = jnp.zeros_like(ds_all)
            dkvt[...] = jnp.zeros_like(dkvt)

    start = pl.multiple_of(step * QB, QB)

    def run(masked):
        for head in range(heads):
            at = slice(head * HEAD_DIM, (head + 1) * HEAD_DIM)
            keys = kv_all[head, pl.ds(start, KEYS), :]
            query = qt[at, :]
            none = jnp.zeros_like(query)
            scores = dot(keys, jnp.concatenate([query, none], axis=0)) + bias[head]
            if masked:
                scores = keep_rows(scores, step + first, low[...])
            probs = jnp.exp(scores - lse[0, pl.ds(order[4] + head, 1), :])
            dout = dout_all[at, pl.ds(pl.multiple_of((step + first) * QB, QB), QB)]
            dprobs = dot(keys, jnp.concatenate([none, dout], axis=0))
            delta = jnp.sum(probs * dprobs, axis=0, keepdims=True)
            dscores = probs * (dprobs - delta)
            ds_all[head] += dscores
            dscores = dscores.astype(bfloat)
            probs = probs.astype(bfloat)
            window = pl.ds(start, KEYS)
            dqt[at, :] = (dot(kvt_all[head, :HEAD_DIM, window], dscores) * HEAD_DIM**-0.5).astype(bfloat)
            dkvt[head, :HEAD_DIM, window] += dot(query, dscores, NT)
            dkvt[head, HEAD_DIM:, window] += dot(dout, probs, NT)

    pl.when(need[step + first] > 0)(lambda: run(True))
    pl.when(need[step + first] <= 0)(lambda: run(False))

    @pl.when(step == pl.num_programs(0) - 1)
    def _():
        if not ends:
            behind[...] = dkvt[:, :, :WINDOW].astype(bfloat)
            dkv_own[...] = dkvt[:, :, WINDOW:]
        else:
            for head in range(heads):
                for chunk in range(CHUNKS):
                    sums[head, chunk : chunk + 1, :] = diagonal_sums(ds_all[head, chunk * QB : (chunk + 1) * QB, :])


def attention_backward(first, steps, span, order, need, low, qt, kvp, kv, vecs, lse, douts, begun=()):
    total, packed = kv.shape[1:]
    begin, heads = span
    pick = begin // heads
    width = heads * HEAD_DIM
    held = KEYS + (steps - 1) * QB
    ends = kvp is None
    own = held if ends else held - WINDOW
    scores = (heads, KEYS, QB)
    order = jnp.concatenate([order, jnp.full((1,), begin, jnp.int32)])
    kernel = functools.partial(backward_kernel, first, ends)
    specs = [
        SMEM,
        SMEM,
        pl.BlockSpec((1, QB), lambda i: (0, i + first)),
        pl.BlockSpec((width, QB), lambda i: (pick, i + first)),
        pl.BlockSpec((heads, own, packed), lambda i: (pick, 0, 0)),
        pl.BlockSpec((heads,) + vecs.shape[1:], lambda i: (pick, 0, 0)),
        pl.BlockSpec((1, 8, QB), lambda i: (i, 0, 0)),
    ] + [pl.BlockSpec((width, douts[0].shape[1]), lambda i: (pick, 0))] * 4
    inputs = [order, need, low, qt, kv, vecs, lse, *douts]
    out_specs = [pl.BlockSpec((width, QB), lambda i: (0, i))]
    out_shape = [jax.ShapeDtypeStruct((width, steps * QB), bfloat)]
    scratch = [
        pltpu.VMEM((heads, held, packed), bfloat),
        pltpu.VMEM((heads, packed, held), bfloat),
        pltpu.VMEM(scores, single),
        pltpu.VMEM((width, total), bfloat),
    ]
    if ends:
        specs += [
            pl.BlockSpec((heads, packed, WINDOW), lambda i: (pick, 0, 0)),
            pl.BlockSpec(scores, lambda i: (pick, 0, 0)),
        ]
        inputs += list(begun)
        shapes = [((heads, packed, held), single), ((heads, 8, 2 * QB), single)]
        scratch.append(pltpu.VMEM(scores, single))
    else:
        specs.append(full(kvp.shape))
        inputs.append(kvp)
        shapes = [((heads, packed, WINDOW), bfloat), ((heads, packed, held - WINDOW), single), (scores, single)]
        scratch.append(pltpu.VMEM((heads, packed, held), single))
    out_specs += [full(shape) for shape, _ in shapes]
    out_shape += [jax.ShapeDtypeStruct(shape, kind) for shape, kind in shapes]
    return pl.pallas_call(
        kernel,
        grid=(steps,),
        in_specs=specs,
        out_specs=out_specs,
        out_shape=out_shape,
        scratch_shapes=scratch,
        compiler_params=params(60, 1),
        cost_estimate=light(),
        name="attend_back",
    )(*inputs)


def settle_kernel(
    order, dq0, dq1, dq2, dkv1, dkv2, behind, normed, sums1, sums2, hot, gain_terms, router0, router1,
    out0, out1, out2, out3, grad,
):
    heads = behind.shape[0]
    rows = out0.shape[1]
    outs = (out0, out1, out2, out3)
    edge = dkv1.shape[2] - WINDOW
    held = [(dq1, dkv1, sums1, number) for number in range(dkv1.shape[0])]
    held += [(dq2, dkv2, sums2, number) for number in range(dkv2.shape[0])]
    parts = []
    for head, (dq, dkvt, _, number) in enumerate(held):
        at = slice(number * HEAD_DIM, (number + 1) * HEAD_DIM)
        last = dkvt[number, :, edge:] + behind[head].astype(single)
        parts.append(jnp.concatenate([dq0[head * HEAD_DIM : (head + 1) * HEAD_DIM, :], dq[at, :]], axis=1))
        parts.append(jnp.concatenate([dkvt[number, :, :edge], last], axis=1).astype(bfloat))
    whole = jnp.concatenate(parts, axis=0)

    def put(place, lane):
        outs[place][...] = whole[:, lane * rows : (lane + 1) * rows]

    by_lane(order[0], put)
    total = None
    for lane in range(len(outs)):
        term = dot(whole[:, lane * rows : (lane + 1) * rows], normed[lane])
        total = term if total is None else total + term
    total = total.astype(bfloat)
    part = grad.shape[2]
    count = total.shape[0]
    found = []
    for _, _, ref, number in held:
        value = None
        for chunk in range(CHUNKS):
            term = lax.dot_general(
                jnp.broadcast_to(ref[number, chunk : chunk + 1, :], (8, 2 * QB)),
                hot[chunk * 2 * QB : (chunk + 1) * 2 * QB, :],
                (NN, ((), ())),
                precision=lax.Precision.HIGHEST,
                preferred_element_type=single,
            )
            value = term if value is None else value + term
        found.append(value[0:1, :])
    found.append(jnp.zeros((1, part - BUCKETS * heads), single))
    rel = jnp.broadcast_to(jnp.concatenate(found, axis=1), (16, part))
    router = (router0[...] + router1[...]).astype(bfloat)
    for lane in range(len(outs)):
        columns = slice(lane * part, (lane + 1) * part)
        grad[lane, :count, :] = total[:, columns]
        mine = jnp.where(order[0] == lane, 1.0, 0.0)
        grad[lane, count : count + 16, :] = (rel * mine).astype(bfloat)
        terms = jnp.broadcast_to(gain_terms[:, columns], (16, part))
        grad[lane, count + 16 : count + 32, :] = terms.astype(bfloat)
        begin = count + 32 + router.shape[0]
        grad[lane, count + 32 : begin, :] = router[:, columns]
        if begin < grad.shape[1]:
            grad[lane, begin:, :] = jnp.zeros((grad.shape[1] - begin, part), bfloat)


def settle(order, dq0, late, behind, normed, sums, hot, gain_terms, routers, multiple):
    lanes, rows, width = normed.shape
    tall = 3 * width // lanes
    count = tall + 32 + routers[0].shape[0]
    count = -(-count // multiple) * multiple
    (dq1, dkv1), (dq2, dkv2) = late
    return once(
        settle_kernel,
        "settle",
        (order, dq0, dq1, dq2, dkv1, dkv2, behind, normed, *sums, hot, gain_terms, *routers),
        [((tall, rows), bfloat)] * lanes + [((lanes, count, width // lanes), bfloat)],
    )


def middle_kernel(o0, o1, o2, o3, w0, w1, w2, w3, x, gain, code, y_out, send0, send1):
    y = x[...].astype(single)
    for ref, weight in ((o0, w0), (o1, w1), (o2, w2), (o3, w3)):
        y = y + dot(ref[...], weight[...], TN)
    y_out[...] = y
    inverse = lax.rsqrt(jnp.mean(y * y, axis=-1, keepdims=True) + epsilon)
    normed = (y * inverse * gain[...]).astype(bfloat)
    slots = send0.shape[0]
    for number, ref in enumerate((send0, send1)):
        slot = lax.broadcasted_iota(jnp.int32, (slots, y.shape[0]), 0) + number * slots
        pick = ((slot == code[0:1, :]) | (slot == code[1:2, :])).astype(bfloat)
        ref[...] = dot(pick, normed).astype(bfloat)


def middle(ots, w_out, x, gain, code, slots):
    rows, width = x.shape
    return once(
        middle_kernel,
        "middle",
        (*ots, *w_out, x, gain, code),
        [((rows, width), single), ((slots, width), bfloat), ((slots, width), bfloat)],
    )


NOTES = 16


def send_kernel(code, value, *outs):
    blocks, count = outs[0].shape[:2]
    slot = lax.broadcasted_iota(jnp.int32, (count, value.shape[0]), 0)
    for block in range(blocks):
        for number, out in enumerate(outs):
            here = slot + ((number // 2 * blocks + block) * 2 + number % 2) * count
            pick = ((here == code[0:1, :]) | (here == code[1:2, :])).astype(bfloat)
            out[block] = dot(pick, value[...]).astype(bfloat)


def send_rows(code, value, blocks, slot_rows):
    shape = (blocks, slot_rows // 2, value.shape[1])
    return once(send_kernel, "send_rows", (code, value), [(shape, bfloat)] * 4)


def send_noted_kernel(part, notes, out):
    for block in range(part.shape[0]):
        out[block, NOTES:, :] = part[block]
        out[block, :NOTES, :] = jnp.broadcast_to(notes[...], (NOTES, part.shape[2]))


def send_noted(part, notes):
    blocks, count, width = part.shape
    outputs = [((blocks, count + NOTES, width), bfloat)]
    return once(send_noted_kernel, "send_noted", (part, notes), outputs)[0]


def collect(code, refs):
    total = None
    for number, ref in enumerate(refs):
        slots = ref.shape[0]
        slot = lax.broadcasted_iota(jnp.int32, (code.shape[0], slots), 1) + number * slots
        pick = ((slot == code[:, 0:1]) | (slot == code[:, 1:2])).astype(bfloat)
        part = dot(pick, ref[...])
        total = part if total is None else total + part
    return total


def return_kernel(d0, d1, code, y, gain, cotangent, w0, w1, w2, w3, o0, o1, o2, o3, dy_out, gg_out, *dots):
    dn = collect(code, (d0, d1))
    values = y[...]
    inverse = lax.rsqrt(jnp.mean(values * values, axis=-1, keepdims=True) + epsilon)
    hat = values * inverse
    gg_out[...] = jnp.sum(dn * hat, axis=0, keepdims=True)
    scaled = dn * gain[...]
    dy = cotangent[...].astype(single) + inverse * (scaled - hat * jnp.mean(scaled * hat, axis=-1, keepdims=True))
    dy_out[...] = dy
    low = dy.astype(bfloat)
    for place, (ref, weight) in enumerate(((o0, w0), (o1, w1), (o2, w2), (o3, w3))):
        dots[place][...] = dot(weight[...], low, NT).astype(bfloat)
        dots[place + 4][...] = dot(ref[...], low).astype(bfloat)


def return_rows(d0, d1, code, y, gain, cotangent, w_out, ots):
    rows, width = y.shape
    lanes = len(ots)
    return once(
        return_kernel,
        "return_rows",
        (d0, d1, code, y, gain, cotangent, *w_out, *ots),
        [((rows, width), single), ((1, width), single)]
        + [((width // lanes, rows), bfloat)] * lanes
        + [((width // lanes, width), bfloat)] * lanes,
    )


def finish_kernel(z0, z1, code, y, out):
    out[...] = (y[...] + collect(code, (z0, z1))).astype(bfloat)


def finish(z0, z1, code, y):
    return once(finish_kernel, "finish", (z0, z1, code, y), [(y.shape, bfloat)])[0]


def unpack_kernel(value, wq, wk, wv, gain, q_out, k_out, v_out, other_out, gain_out):
    lanes, _, part = value.shape
    heads = part // HEAD_DIM
    mark = 3 * part
    others = None
    for lane in range(lanes):
        whole = value[lane, :mark, :].astype(single).T
        for head in range(heads):
            at = slice((lane * heads + head) * HEAD_DIM, (lane * heads + head + 1) * HEAD_DIM)
            for number, ref in enumerate((q_out, k_out, v_out)):
                begin = (3 * head + number) * HEAD_DIM
                ref[:, at] = whole[:, begin : begin + HEAD_DIM]
        term = value[lane, mark + 16 : mark + 32 + other_out.shape[0] - 16, :].astype(single)
        others = term if others is None else others + term
    other_out[...] = others
    total = None
    for ref, weight in ((q_out, wq), (k_out, wk), (v_out, wv)):
        term = jnp.sum(ref[...] * weight[...].astype(single), axis=1, keepdims=True)
        total = term if total is None else total + term
    gain_out[...] = total / gain[...].astype(single)


def unpack(value, wq, wk, wv, gain, heads, experts):
    part, width = wq.shape
    outputs = [((part, width), single)] * 3 + [((16 + experts, part), single), ((part, 1), single)]
    return once(unpack_kernel, "unpack", (value, wq, wk, wv, gain), outputs)


def tail_kernel(order, *refs):
    *pieces, wt, x, gain, dy, out = refs
    dn = None
    for number, ref in enumerate(pieces):
        block = order[number % 4]
        tall = ref.shape[0]
        begin = block * tall
        term = dot(ref[...], wt[pl.ds(pl.multiple_of(begin, 64), tall), :], TN)
        dn = term if dn is None else dn + term
    values = x[...].astype(single)
    inverse = lax.rsqrt(jnp.mean(values * values, axis=-1, keepdims=True) + epsilon)
    hat = values * inverse
    scaled = dn * gain[...]
    out[...] = dy[...] + inverse * (scaled - hat * jnp.mean(scaled * hat, axis=-1, keepdims=True))


def tail(order, pieces, wt, x, gain, dy):
    return once(tail_kernel, "tail", (order, *pieces, wt, x, gain, dy), [(x.shape, single)])[0]


GELU_0 = 0.7978845608028654
GELU_1 = 0.7978845608028654 * 0.044715
FF_BLOCK = 512
ROW_BLOCK = 256


def expert_kernel(
    mine, xs, router, other, w1, w2, da, cot, g10, g11, g12, g13, g2, dx_out, z_out, m_out, total, result, dgate, gate, act_all, du_all, xst, dzt
):
    step = pl.program_id(0)
    rows = xs.shape[0]
    experts = router.shape[0]

    def picks():
        lane = lax.broadcasted_iota(jnp.int32, (rows, experts), 1)
        return lane == mine[0], lane == other[...] - 1

    @pl.when(step == 0)
    def _():
        logits = dot(xs[...], router[...], NT)
        own, rest = picks()
        margin = jnp.sum(jnp.where(own, logits, 0.0) - jnp.where(rest, logits, 0.0), axis=1, keepdims=True)
        value = 1.0 / (1.0 + jnp.exp(-margin))
        value = jnp.where(other[...] > 0, value, 0.0)
        gate[...] = jnp.broadcast_to(value, gate.shape)
        dgate[...] = jnp.zeros_like(dgate)
        total[...] = jnp.zeros_like(total)
        result[...] = jnp.zeros_like(result)
        for begin in range(0, rows, ROW_BLOCK):
            at = slice(begin, begin + ROW_BLOCK)
            xst[:, at] = xs[at, :].T
            dzt[:, at] = (cot[at, :].astype(single) * gate[at, 0:1]).astype(bfloat).T

    for begin in range(0, rows, ROW_BLOCK):
        at = slice(begin, begin + ROW_BLOCK)
        u = dot(xs[at, :], w1[...])
        square = u * u
        tan = jnp.tanh(u * (GELU_0 + GELU_1 * square))
        half = 0.5 + 0.5 * tan
        act = u * half
        slope = half + act * (1.0 - half) * (2.0 * GELU_0 + 6.0 * GELU_1 * square)
        back = da[at, :].astype(single)
        product = act * back
        part = product[:, :128]
        for col in range(128, product.shape[1], 128):
            part = part + product[:, col : col + 128]
        dgate[at, :] += part
        act_all[at, :] = act.astype(bfloat)
        du_all[at, :] = (gate[at, 0:1] * back * slope).astype(bfloat)
    total[...] += dot(du_all[...], w1[...], NT)
    result[...] += dot(act_all[...], w2[...])
    grad = dot(xst[...], du_all[...]).astype(bfloat)
    part = g10.shape[0]

    def put(place, lane):
        (g10, g11, g12, g13)[place][...] = grad[lane * part : (lane + 1) * part, :]

    by_lane(mine[1], put)
    g2[...] = dot(dzt[...], act_all[...]).astype(bfloat).T

    @pl.when(step == pl.num_programs(0) - 1)
    def _():
        own, rest = picks()
        value = gate[:, 0:1]
        weight = value * (1.0 - value) * jnp.sum(dgate[...], axis=1, keepdims=True)
        m = (weight * (own.astype(single) - rest.astype(single))).astype(bfloat)
        m_out[...] = dot(m, xs[...], TN)
        dx_out[...] = (total[...] + dot(m, router[...])).astype(bfloat)
        z_out[...] = (result[...] * value).astype(bfloat)


def expert(mine, xs, router, other, w1, w2, da, cot, local):
    rows, width = xs.shape
    inner = w1.shape[2]
    experts = router.shape[0]
    block = FF_BLOCK
    whole = lambda shape: pl.BlockSpec(shape, lambda f: (0,) * len(shape))
    return pl.pallas_call(
        expert_kernel,
        grid=(inner // block,),
        in_specs=[
            SMEM,
            whole((rows, width)),
            whole((experts, width)),
            whole((rows, 1)),
            pl.BlockSpec((None, width, block), lambda f: (local, 0, f)),
            pl.BlockSpec((None, block, width), lambda f: (local, f, 0)),
            pl.BlockSpec((rows, block), lambda f: (0, f)),
            whole((rows, width)),
        ],
        out_specs=[
            *[pl.BlockSpec((width // len(MASKS), block), lambda f: (0, f))] * len(MASKS),
            pl.BlockSpec((block, width), lambda f: (f, 0)),
            whole((rows, width)),
            whole((rows, width)),
            whole((experts, width)),
        ],
        out_shape=[
            *[jax.ShapeDtypeStruct((width // len(MASKS), inner), bfloat)] * len(MASKS),
            jax.ShapeDtypeStruct((inner, width), bfloat),
            jax.ShapeDtypeStruct((rows, width), bfloat),
            jax.ShapeDtypeStruct((rows, width), bfloat),
            jax.ShapeDtypeStruct((experts, width), single),
        ],
        scratch_shapes=[
            pltpu.VMEM((rows, width), single),
            pltpu.VMEM((rows, width), single),
            pltpu.VMEM((rows, 128), single),
            pltpu.VMEM((rows, 128), single),
            pltpu.VMEM((rows, block), bfloat),
            pltpu.VMEM((rows, block), bfloat),
            pltpu.VMEM((width, rows), bfloat),
            pltpu.VMEM((width, rows), bfloat),
        ],
        compiler_params=params(60, 1),
        cost_estimate=cost(20 * rows * width * inner, 8 * rows * inner + 8 * width * inner, rows * inner),
        name="expert",
    )(mine, xs, router, other, w1, w2, da, cot)


def tie(*values):
    return lax.optimization_barrier(values)


def swap(value, axis, mask):
    return lax.ppermute(value, axis, [(i, i ^ mask) for i in range(lax.axis_size(axis))])


def per_device(
    hidden_in,
    norm1_gain,
    w_query,
    w_key,
    w_value,
    w_out,
    rel_bias,
    norm2_gain,
    w_router,
    w_first,
    w_second,
    routes,
    priority,
    segments,
    grad_out,
):
    lanes = lax.axis_size("head")
    blocks = lax.axis_size("seq")
    lane = lax.axis_index("head")
    place = lax.axis_index("seq")
    rows, width = hidden_in.shape[2:]
    x = hidden_in.reshape(rows, width)
    total = rows * lanes
    part = width // lanes
    heads = part // HEAD_DIM
    cotangent = grad_out.reshape(rows, width)
    experts = w_router.shape[1]
    local = w_first.shape[0]
    slot_rows = max(2, 4 * rows // experts)
    slots = blocks * slot_rows
    capacity = 5 * rows * lanes // (2 * local)

    far = swap(x, "head", 2)
    near = swap(x, "head", 1)
    order = jnp.stack([lane, lane ^ 2, lane ^ 1, lane ^ 3]).astype(jnp.int32)
    at = lambda value, mask: lax.dynamic_index_in_dim(value, lane ^ mask, 0, keepdims=False)

    def trade(value):
        return [value[0]] + [swap(value[place], "head", MASKS[place]) for place in range(1, lanes)]

    route_t = routes.reshape(rows, -1).T
    top_count = route_t.shape[0]
    pair_routes = route_t.reshape(-1)
    pair_prio = priority.reshape(rows, -1).T.reshape(-1)
    expert_ids = jnp.arange(experts, dtype=jnp.int32)
    pair_hot = (expert_ids[:, None] == pair_routes[None, :]).astype(jnp.int32)
    earlier = (pair_routes[:, None] == pair_routes[None, :]) & (pair_prio[:, None] < pair_prio[None, :])
    local_rank = jnp.sum(earlier.astype(jnp.int32), axis=0)
    code = (pair_routes % local) * slots + (pair_routes // local) * slot_rows + local_rank
    code_t = code.reshape(top_count, rows)
    code = code_t.T

    def exchange(value):
        return lax.all_to_all(
            value.reshape(blocks, slot_rows, -1), "seq", split_axis=0, concat_axis=0, tiled=True
        ).reshape(slots, -1)


    block_rank = (jnp.min(pair_prio) // (top_count * rows)).reshape(1)
    tally = jnp.concatenate([jnp.sum(pair_hot, axis=1), block_rank, jnp.zeros((part - experts - 1,), jnp.int32)])
    gains = jnp.stack([norm1_gain, norm2_gain, tally.astype(bfloat)])
    gains = jnp.concatenate([gains, jnp.zeros((GAINS - 3, part), bfloat)], axis=0)
    hot, allowed = lane_tables()
    table = rel_bias.reshape(heads, BUCKETS)
    vecs = dot(table, jnp.asarray(hot.T, bfloat)).reshape(heads, CHUNKS, 2 * QB)
    vecs = jnp.where(jnp.asarray(allowed)[None], vecs, MASKED)
    vecs = jnp.concatenate([vecs, jnp.zeros((heads, 8 - CHUNKS, 2 * QB), single)], axis=1)
    base = place * total
    own = lax.dynamic_slice_in_dim(segments, base, total, 0)
    low = jnp.zeros_like(own)
    for number in range(1, 4):
        low = jnp.where(own == number, jnp.sum((segments < number).astype(jnp.int32)), low)
    low = low - base + WINDOW
    need = (jnp.max(low.reshape(-1, QB), axis=1) > jnp.arange(total // QB) * QB).astype(jnp.int32)
    low = low.reshape(1, total)
    packed = pack(order, w_query, w_key, w_value, w_router.T, gains)
    far, near, code_t, low, need, vecs, code, packed = tie(far, near, code_t, low, need, vecs, code, packed)
    packed = trade(packed)
    both = swap(far, "head", 1)
    cot_parts = list(send_rows(code_t, cotangent, blocks, slot_rows))
    spread_out = lambda value: lax.all_to_all(value, "seq", split_axis=0, concat_axis=0, tiled=True)
    cots = [spread_out(cot_parts[0])]
    packed, both, w_second, w_out, cots[0], cot_parts = tie(packed, both, w_second, w_out, cots[0], cot_parts)
    cots.append(spread_out(cot_parts[1]))

    out_far = swap(w_out, "head", 2)
    out_near = swap(w_out, "head", 1)
    second_full = lax.all_gather(w_second, "head", axis=1, tiled=True)

    normed, qt, kv, kv_last, w_rows, router_t, gains = project(order, (x, far, near, both), packed, heads, experts)
    w_rows_full = lax.all_gather(w_rows, "head", axis=0, tiled=True)
    gain_one, gain_two = gains[0:1], gains[1:2]
    kvp = lax.ppermute(kv_last, "seq", [(i, i + 1) for i in range(blocks - 1)])
    early = WINDOW // QB
    later = total // QB - early
    *ot, lse_later = attention_forward(early, later, order, need, low, qt, None, kv, vecs, lanes)
    ot, kvp, cots[1], cot_parts[2] = tie(ot, kvp, cots[1], cot_parts[2])
    cots.append(spread_out(cot_parts[2]))
    *ot, lse_early = attention_forward(0, early, order, need, low, qt, kvp, kv, vecs, lanes, ot)
    ot, out_far, out_near = tie(ot, out_far, out_near)
    w_outs = (w_out, out_far, out_near, swap(out_far, "head", 1))
    ots = trade(ot)
    ots, w_first, cots[2], cot_parts[3] = tie(ots, w_first, cots[2], cot_parts[3])
    noted = spread_out(send_noted(cot_parts[3], gains[2:3].astype(bfloat)))
    first_full = lax.all_gather(w_first, "head", axis=1, tiled=True)

    y, *sends = middle(ots, w_outs, x, gain_two, code_t, slots)
    sends[0], noted = tie(sends[0], noted)
    cots.append(noted[:, NOTES:, :])

    tallies = noted[:, 0, :].reshape(blocks * lanes, part).astype(jnp.int32)
    ahead = (tallies[:, experts : experts + 1] < block_rank[None, :]).astype(jnp.int32)
    offsets = jnp.sum(tallies[:, :experts] * ahead, axis=0)
    kept = (jnp.sum(pair_hot * offsets[:, None], axis=0) + local_rank < capacity).reshape(top_count, rows)
    slot_ids = jnp.arange(local * slots, dtype=jnp.int32)[:, None]
    other = jnp.sum(
        jnp.where(slot_ids == code_t[0:1], jnp.where(kept[0:1], route_t[1:2] + 1, 0), 0)
        + jnp.where(slot_ids == code_t[1:2], jnp.where(kept[1:2], route_t[0:1] + 1, 0), 0),
        axis=1,
    )
    cot_slots = [jnp.concatenate([cots[2 * i], cots[2 * i + 1]], axis=1).reshape(slots, width) for i in range(local)]
    backs = [dot(cot_slots[0], second_full[0], NT).astype(bfloat)]
    other, backs[0] = tie(other, backs[0])
    other = other.reshape(local, blocks, slot_rows)
    far_others = [
        swap(lax.dynamic_index_in_dim(other, place ^ mask, 1, keepdims=False), "seq", mask) for mask in range(1, blocks)
    ]
    mine = jnp.stack([place * local, lane]).astype(jnp.int32)
    backs.append(dot(cot_slots[1], second_full[1], NT).astype(bfloat))
    received = [exchange(sends[0])]
    sends[1], far_others, *backs = tie(sends[1], far_others, *backs)
    received.append(exchange(sends[1]))
    far_others = jnp.concatenate([lax.dynamic_index_in_dim(other, place, 1, keepdims=False)[None], jnp.stack(far_others)])
    other = jnp.stack(
        [lax.dynamic_index_in_dim(far_others, place ^ number, 0, keepdims=False) for number in range(blocks)], axis=1
    ).reshape(local, slots, 1)

    def run_expert(number):
        return expert(
            mine + jnp.asarray([number, 0], jnp.int32),
            received[number],
            router_t,
            other[number],
            first_full,
            second_full,
            backs[number],
            cot_slots[number],
            number,
        )

    received[1], w_rows_full, (*first_parts0, second0, dx0, z0, router0) = tie(
        received[1], w_rows_full, run_expert(0)
    )
    returns = [exchange(dx0)]
    second0 = lax.psum_scatter(second0, "head", scatter_dimension=0, tiled=True)
    returns[0], second0, (*first_parts1, second1, dx1, z1, router1) = tie(returns[0], second0, run_expert(1))
    def near_parts(parts):
        return swap(parts[3], "head", 1), swap(parts[2], "head", 1)

    def add(one, two, kind=single):
        return (one.astype(single) + two.astype(single)).astype(kind)

    def scatter(value):
        return lax.psum_scatter(value, "head", scatter_dimension=0, tiled=True)

    cross0, direct0 = near_parts(first_parts0)
    returns.append(exchange(dx1))
    across0 = swap(add(first_parts0[1], cross0, bfloat), "head", 2)
    cross1, direct1 = near_parts(first_parts1)
    second1 = scatter(second1)

    returns[1], across0 = tie(returns[1], across0)
    first0 = add(add(first_parts0[0], direct0), across0)
    dy, gain_terms, *douts = return_rows(
        returns[0], returns[1], code, y, gain_two, cotangent, w_outs, ots
    )
    douts, outw = trade(douts[:lanes]), douts[lanes:]
    dy, z0 = tie(dy, z0)
    z_back = [exchange(z0)]
    douts, outw, cross1, direct1 = tie(douts, outw, cross1, direct1)
    outw_cross, outw_direct = near_parts(outw)
    across1 = swap(add(first_parts1[1], cross1, bfloat), "head", 2)

    def sum_blocks(value):
        count, last = value.shape[1:]
        value = value.reshape(lanes * blocks, count // blocks, last)
        value = lax.all_to_all(value, ("head", "seq"), split_axis=0, concat_axis=0, tiled=True)
        return jnp.sum(value.reshape(lanes, blocks, -1, last).astype(single), axis=1).astype(bfloat)

    dq_early, behind, dkvt_early, ds_early = attention_backward(
        0, early, (0, heads), order, need, low, qt, kvp, kv, vecs, lse_early, douts
    )
    behind = lax.ppermute(behind, "seq", [(i + 1, i) for i in range(blocks - 1)])
    dq_early, outw_cross, outw_direct, second1 = tie(dq_early, outw_cross, outw_direct, second1)
    outw_across = swap(add(outw[1], outw_cross, bfloat), "head", 2)
    cut = heads - 1

    def later_part(span):
        return attention_backward(
            early, later, span, order, need, low, qt, None, kv, vecs, lse_later, douts, (dkvt_early, ds_early)
        )

    dq_last, dkv_last, sums_last = later_part((cut, heads - cut))
    dkv_last, z_back[0], z1, behind = tie(dkv_last, z_back[0], z1, behind)
    z_back.append(exchange(z1))
    ds_early, dkv_last = tie(ds_early, dkv_last)
    dq_first, dkv_first, sums_first = later_part((0, cut))
    dq_first, outw_across, across1 = tie(dq_first, outw_across, across1)
    grad_outw = add(add(outw[0], outw_direct), outw_across, bfloat)
    grad_outw = spread_out(grad_outw.reshape(blocks, -1, part))
    *parts, grad_part = settle(
        order,
        dq_early,
        ((dq_first, dkv_first), (dq_last, dkv_last)),
        behind,
        normed,
        (sums_first, sums_last),
        jnp.asarray(hot, single),
        gain_terms,
        (router0, router1),
        max(16, blocks),
    )
    pieces = trade(parts)
    first1 = add(add(first_parts1[0], direct1), across1)
    output = finish(z_back[0], z_back[1], code, y).reshape(hidden_in.shape)

    grad_part, z_back[1] = tie(grad_part, z_back[1])
    value = sum_blocks(grad_part)
    value, dy, pieces, grad_outw = tie(value, dy, pieces, grad_outw)
    grad_hidden = tail(order, pieces, w_rows_full, x, gain_one, dy).reshape(hidden_in.shape)
    grad_outw = jnp.sum(grad_outw.astype(single), axis=0).astype(bfloat)
    count = value.shape[1]
    value = jnp.concatenate([value.reshape(-1, part), grad_outw], axis=0)
    value = lax.all_to_all(
        jnp.broadcast_to(value[None], (blocks,) + value.shape), "seq", split_axis=0, concat_axis=0, tiled=True
    )
    grad_outw = value[:, lanes * count :, :].reshape(part, width)
    value = value[:, : lanes * count, :].reshape(blocks, lanes, count, part)
    value = value.transpose(1, 0, 2, 3).reshape(lanes, -1, part)
    mark = 3 * part
    grad_rel = value[:, mark, : heads * BUCKETS].astype(single)
    grad_rel = lax.dynamic_index_in_dim(grad_rel, lane, 0, keepdims=False)
    *grads, others, grad_norm1 = unpack(value, w_query, w_key, w_value, norm1_gain.reshape(part, 1), heads, experts)
    return (
        output,
        grad_hidden,
        grad_norm1.reshape(part),
        grads[0],
        grads[1],
        grads[2],
        grad_outw.astype(single),
        grad_rel,
        others[0],
        others[16:].T,
        jnp.stack([first0, first1]),
        jnp.stack([second0, second1]).astype(single),
    )


def solution(mesh):
    return jax.shard_map(
        per_device,
        mesh=mesh,
        in_specs=(
            P("seq", "head", None, None),
            P("head"),
            P("head", None),
            P("head", None),
            P("head", None),
            P("head", None),
            P("head"),
            P("head"),
            P("head", None),
            P("seq", "head", None),
            P("seq", "head", None),
            P("seq", "head", None, None),
            P("seq", "head", None, None),
            P(),
            P("seq", "head", None, None),
        ),
        out_specs=(
            P("seq", "head", None, None),
            P("seq", "head", None, None),
            P("head"),
            P("head", None),
            P("head", None),
            P("head", None),
            P("head", None),
            P("head"),
            P("head"),
            P("head", None),
            P("seq", "head", None),
            P("seq", "head", None),
        ),
        check_vma=False,
    )
```

time: 732 us -> 674 us (0.921)
  local copies, waits for them, and re-layouts: 93.6 us -> 41.7 us
  waiting for transfers between devices: 201 us -> 165 us
  Pallas kernels: 247 us -> 278 us
  starting transfers between devices: 90.8 us -> 112 us
  other arithmetic: 46.3 us -> 29.6 us
    all_to_all x7 -> x6, waiting for transfers between devices: 81.3 us -> 4.54 us  [exchange(): lax.all_to_all(value.reshape(blocks, slot_rows, -1), 'seq', split_axis=0,...]
    psum x1 -> x0, waiting for transfers between devices: 44.6 us -> none  [per_device(): mixed = lax.psum(mixed, 'seq')]
    unnamed x191 -> x112, local copies, waits for them, and re-layouts: 52.1 us -> 11.9 us
    all_to_all x1 -> x5, waiting for transfers between devices: 0.13 us -> 32.5 us  [per_device(): lax.all_to_all(value, 'seq', split_axis=0, concat_axis=0, tiled=True)]
    all_to_all x2 -> x1, waiting for transfers between devices: 0.48 us -> 28.4 us  [sum_blocks(): lax.all_to_all(value, ('head', 'seq'), split_axis=0, concat_axis=0, tiled...]
    all_to_all x1 -> x5, starting transfers between devices: 4.79 us -> 28 us  [per_device(): lax.all_to_all(value, 'seq', split_axis=0, concat_axis=0, tiled=True)]
    pallas_call x10, Pallas kernels: 51.5 us -> 74.2 us  [once(): pl.pallas_call(kernel, grid=(1,), in_specs=[SMEM if value.ndim == 1 else...]
    ppermute x32 -> x34, waiting for transfers between devices: 64.1 us -> 82.8 us  [swap(): lax.ppermute(value, axis, [(i, i ^ mask) for i in range(lax.axis_size(axi...]
  transfers between devices with their start and end apart: 52 -> 54, of which waited for: 17 -> 21; matrix products, arithmetic and copies ran while one was open for 14% -> 10% of each run, Pallas kernels for 34% -> 40%
where the time goes in v2:
time: 674 us; the launch traced here: 666 us
  Pallas kernels  278 us (41%)
  waiting for transfers between devices  165 us (24%)
  starting transfers between devices  112 us (17%)
  local copies, waits for them, and re-layouts  41.7 us (6%)
  other arithmetic  29.6 us (4%)
  matrix products  22.1 us (3%)
  between operations  17 us (3%)
    pallas_call x2, Pallas kernels, expert(): pl.pallas_call(expert_kernel, grid=(inner // block,), in_specs=[SMEM, who...  104 us
    ppermute x34, waiting for transfers between devices, swap(): lax.ppermute(value, axis, [(i, i ^ mask) for i in range(lax.axis_size(axi...  82.8 us
    pallas_call x10, Pallas kernels, once(): pl.pallas_call(kernel, grid=(1,), in_specs=[SMEM if value.ndim == 1 else...  74.2 us
    pallas_call x3, Pallas kernels, attention_backward(): pl.pallas_call(kernel, grid=(steps,), in_specs=specs, out_specs=out_specs...  66.7 us
    pallas_call x2, Pallas kernels, attention_forward(): pl.pallas_call(functools.partial(forward_kernel, first), grid=(steps,), i...  33.6 us
    ppermute x34, starting transfers between devices, swap(): lax.ppermute(value, axis, [(i, i ^ mask) for i in range(lax.axis_size(axi...  33.6 us
    all_to_all x5, waiting for transfers between devices, per_device(): lax.all_to_all(value, 'seq', split_axis=0, concat_axis=0, tiled=True)  32.5 us
    all_to_all x6, starting transfers between devices, exchange(): lax.all_to_all(value.reshape(blocks, slot_rows, -1), 'seq', split_axis=0,...  31.5 us
  transfers between devices with their start and end apart: 54, of which 21 were waited for; matrix products, arithmetic and copies ran while one was open for 10% of the time, Pallas kernels for 40%

profile of v2, /device:TPU:0, one launch (start us, length us, event | category | flops | bytes accessed | tf_op | source)
XLA Modules:
  0.0 665.8 jit_solution(153486789086988128)
XLA Ops:
  33.1 8.6 %send_rows.1 = (bf16[8,80,768]{2,1,0:T(8,128)(2,1)}, bf16[8,80,768]{2,1,0:T(8,128)(2,1)}, bf16[8,80,768]{2,1,0:T(8,128)(2,1)}, bf16[8,80,768]{2,1,0:T(8,128)(2,1)}) custom-call(s32[2,640]{1,0:T(2,128)} %copy.108.code, bf16[640,768]{1,0:T(8,128)(2,1)} %bitcast.125), custom_call_target="tpu_custom_call" | custom-call | flops 1000 | bytes 1000 | tf_op jit(solution)/shard_map/send_rows/pallas_call | solution.py:46
  50.0 7.9 %collective-permute-done.2.p1 = bf16[192,768]{1,0:T(8,128)(2,1)S(1)} collective-permute-done((bf16[192,768]{1,0:T(8,128)(2,1)}, bf16[192,768]{1,0:T(8,128)(2,1)S(1)}, u32[]{:S(2)}, u32[]{:S(2)}) %collective-permute-start.2) | collective-permute-done | bytes 294944 | tf_op jit(solution)/shard_map/ppermute | solution.py:786
  75.2 11.2 %project.1 = (bf16[4,640,768]{2,1,0:T(8,128)(2,1)}, bf16[192,2560]{1,0:T(8,128)(2,1)}, bf16[3,2560,128]{2,1,0:T(8,128)(2,1)}, bf16[3,1024,128]{2,1,0:T(8,128)(2,...) custom-call(s32[4]{0:T(128)} %pad_add_fusion.order, bf16[640,768]{1,0:T(8,128)(2,1)} %bitcast.117, ...), custom_call_target="tpu_custom_call" | custom-call | flops 1000 | bytes 1000 | tf_op jit(solution)/shard_map/project/pallas_call | solution.py:46
  91.2 19.3 %attend.2 = (bf16[192,640]{1,0:T(8,128)(2,1)}, bf16[192,640]{1,0:T(8,128)(2,1)}, bf16[192,640]{1,0:T(8,128)(2,1)}, bf16[192,640]{1,0:T(8,128)(2,1)}, f32[6,8,256]{2,1,0:T(8,128)}) custom-call(s32[4]{0:T(128)} %pad_add_fusion.order, s32[10]{0:T(128)} %compare_convert_fusion.1.need, s32[1,2560]{1,0:T(1,128)} %reshape.204.low, ...), custom_call_target="tpu_custom_call" | custom-call | flops 1000 | bytes 1000 | tf_op jit(solution)/shard_map/attend/pallas_call | solution.py:286
  111.5 8.8 %all-to-all-start.2 = ((bf16[8,80,768]{2,1,0:T(8,128)(2,1)}), bf16[8,80,768]{2,1,0:T(8,128)(2,1)S(1)}, u32[]{:S(2)}, u32[]{:S(2)}) async-start(bf16[8,80,768]{2,1,0:T(8,128)(2,1)} %get-tuple-element.244), calls=%async_computation.2 | async-start | bytes 1966080 | tf_op jit(solution)/shard_map/all_to_all | solution.py:870
  122.4 14.3 %attend.3 = (bf16[192,640]{1,0:T(8,128)(2,1)}, bf16[192,640]{1,0:T(8,128)(2,1)}, bf16[192,640]{1,0:T(8,128)(2,1)}, bf16[192,640]{1,0:T(8,128)(2,1)}, f32[4,8,256]{2,1,0:T(8,128)}) custom-call(s32[4]{0:T(128)} %pad_add_fusion.order, s32[10]{0:T(128)} %compare_convert_fusion.1.need, s32[1,2560]{1,0:T(1,128)} %reshape.204.low, ...), custom_call_target="tpu_custom_call" | custom-call | flops 1000 | bytes 1000 | tf_op jit(solution)/shard_map/attend/pallas_call | solution.py:286
  165.9 8.6 %middle.1 = (f32[640,768]{1,0:T(8,128)}, bf16[1280,768]{1,0:T(8,128)(2,1)}, bf16[1280,768]{1,0:T(8,128)(2,1)}) custom-call(bf16[192,640]{1,0:T(8,128)(2,1)} %get-tuple-element.246.o0, bf16[192,640]{1,0:T(8,128)(2,1)} %copy-done.27, bf16[192,640]{1,0:T(8,128)(2,1)} %copy-done.28, bf16[192,640]{1,0:T(8,128)(2,1)} %collective-permute-done.11.o3, ...), custom_call_target="tpu_custom_call" | custom-call | flops 1000 | bytes 1000 | tf_op jit(solution)/shard_map/middle/pallas_call | solution.py:46
  174.5 14.4 %all-to-all-done.3 = bf16[8,96,768]{2,1,0:T(8,128)(2,1)S(1)} async-done(((bf16[8,96,768]{2,1,0:T(8,128)(2,1)}), bf16[8,96,768]{2,1,0:T(8,128)(2,1)S(1)}, u32[]{:S(2)}, u32[]{:S(2)}) %all-to-all-start.3) | async-done | bytes 1179680 | tf_op jit(solution)/shard_map/all_to_all | solution.py:870
  196.4 11.2 %convolution_convert_fusion.1.da = bf16[1280,3072]{1,0:T(8,128)(2,1)} fusion(bf16[1280,768]{1,0:T(8,128)(2,1)} %bitcast.129, bf16[2,3072,768]{2,1,0:T(8,128)(2,1)} %all-gather.4.cloned.1.call-done.w2), kind=kOutput, calls=%fused_computation.1 | convolution fusion | flops 6043729920 | bytes 14548992 | tf_op jit(solution)/shard_map/dot_general | solution.py:28
  219.1 7.4 %collective-permute-done.14 = s32[2,160]{1,0:T(2,128)S(1)} collective-permute-done((s32[2,160]{1,0:T(2,128)S(1)}, s32[2,160]{1,0:T(2,128)S(1)}, u32[]{:S(2)}, u32[]{:S(2)}) %collective-permute-start.14) | collective-permute-done | bytes 1312 | tf_op jit(solution)/shard_map/ppermute | solution.py:786
  230.5 10.9 %convolution_convert_fusion.da = bf16[1280,3072]{1,0:T(8,128)(2,1)} fusion(bf16[1280,768]{1,0:T(8,128)(2,1)S(1)} %bitcast.133, bf16[2,3072,768]{2,1,0:T(8,128)(2,1)} %all-gather.4.cloned.1.call-done.w2), kind=kOutput, calls=%fused_computation | convolution fusion | flops 6043729920 | bytes 14548992 | tf_op jit(solution)/shard_map/dot_general | solution.py:28
  246.8 51.3 %expert.2 = (bf16[192,3072]{1,0:T(8,128)(2,1)}, bf16[192,3072]{1,0:T(8,128)(2,1)}, bf16[192,3072]{1,0:T(8,128)(2,1)}, bf16[192,3072]{1,0:T(8,128)(2,1)}, bf16[30...) custom-call(s32[2]{0:T(128)} %get-tuple-element.390.mine, ...), custom_call_target="tpu_custom_call" | custom-call | flops 60397977600 | bytes 50331648 | tf_op jit(solution)/shard_map/expert/pallas_call | solution.py:738
  306.9 52.5 %expert.3 = (bf16[192,3072]{1,0:T(8,128)(2,1)}, bf16[192,3072]{1,0:T(8,128)(2,1)}, bf16[192,3072]{1,0:T(8,128)(2,1)}, bf16[192,3072]{1,0:T(8,128)(2,1)}, bf16[30...) custom-call(s32[2]{0:T(128)} %get-tuple-element.389.mine, ...), custom_call_target="tpu_custom_call" | custom-call | flops 60397977600 | bytes 50331648 | tf_op jit(solution)/shard_map/expert/pallas_call | solution.py:738
  371.7 33.5 %collective-permute-done.21 = bf16[192,3072]{1,0:T(8,128)(2,1)} collective-permute-done((bf16[192,3072]{1,0:T(8,128)(2,1)S(1)}, bf16[192,3072]{1,0:T(8,128)(2,1)}, u32[]{:S(2)}, u32[]{:S(2)}) %collective-permute-start.21) | collective-permute-done | bytes 1179680 | tf_op jit(solution)/shard_map/ppermute | solution.py:786
  409.8 11.5 %return_rows.1 = (f32[640,768]{1,0:T(8,128)}, f32[1,768]{1,0:T(1,128)}, bf16[192,640]{1,0:T(8,128)(2,1)}, bf16[192,640]{1,0:T(8,128)(2,1)}, bf16[192,640]{1,0:T(...) custom-call(bf16[1280,768]{1,0:T(8,128)(2,1)} %bitcast.123, ...), custom_call_target="tpu_custom_call" | custom-call | flops 1000 | bytes 1000 | tf_op jit(solution)/shard_map/return_rows/pallas_call | solution.py:46
  438.9 21.6 %attend_back.3 = (bf16[192,1024]{1,0:T(8,128)(2,1)}, bf16[3,128,1024]{2,1,0:T(8,128)(2,1)}, f32[3,128,1024]{2,1,0:T(8,128)}, f32[3,1280,256]{2,1,0:T(8,128)}) custom-call(s32[5]{0:T(128)} %concatenate.52.order, s32[10]{0:T(128)} %compare_convert_fusion.1.need, s32[1,2560]{1,0:T(1,128)} %reshape.204.low, bf16[192,2560]{1,0:T(8,128)(2,1)} %get-tuple-element.219.qt, ...), custom_call_target="tpu_custom_call" | custom-call | flops 1000 | bytes 1000 | tf_op jit(solution)/shard_map/attend_back/pallas_call | solution.py:427
  462.5 16.0 %attend_back.4 = (bf16[64,1536]{1,0:T(8,128)(2,1)}, f32[1,128,2560]{2,1,0:T(8,128)}, f32[1,8,512]{2,1,0:T(8,128)}) custom-call(s32[5]{0:T(128)} %concatenate.43.order, s32[10]{0:T(128)} %compare_convert_fusion.1.need, s32[1,2560]{1,0:T(1,128)} %reshape.204.low, bf16[192,2560]{1,0:T(8,128)(2,1)} %get-tuple-element.219.qt, ...), custom_call_target="tpu_custom_call" | custom-call | flops 1000 | bytes 1000 | tf_op jit(solution)/shard_map/attend_back/pallas_call | solution.py:427
  484.3 7.4 %all-to-all-start.9 = ((bf16[8,160,768]{2,1,0:T(8,128)(2,1)}), bf16[8,160,768]{2,1,0:T(8,128)(2,1)}, u32[]{:S(2)}, u32[]{:S(2)}) async-start(bf16[8,160,768]{2,1,0:T(8,128)(2,1)} %bitcast.128), calls=%async_computation.10 | async-start | bytes 3932160 | tf_op jit(solution)/shard_map/all_to_all | solution.py:843
  497.7 29.1 %attend_back.5 = (bf16[128,1536]{1,0:T(8,128)(2,1)}, f32[2,128,2560]{2,1,0:T(8,128)}, f32[2,8,512]{2,1,0:T(8,128)}) custom-call(s32[5]{0:T(128)} %concatenate.52.order, s32[10]{0:T(128)} %compare_convert_fusion.1.need, s32[1,2560]{1,0:T(1,128)} %reshape.204.low, bf16[192,2560]{1,0:T(8,128)(2,1)} %get-tuple-element.219.qt, ...), custom_call_target="tpu_custom_call" | custom-call | flops 1000 | bytes 1000 | tf_op jit(solution)/shard_map/attend_back/pallas_call | solution.py:427
  527.6 10.8 %settle.1 = (bf16[576,640]{1,0:T(8,128)(2,1)}, bf16[576,640]{1,0:T(8,128)(2,1)}, bf16[576,640]{1,0:T(8,128)(2,1)}, bf16[576,640]{1,0:T(8,128)(2,1)}, bf16[4,624,192]{2,1,0:T(8,128)(2,1)}) custom-call(s32[4]{0:T(128)} %pad_add_fusion.order, bf16[192,1024]{1,0:T(8,128)(2,1)} %get-tuple-element.332.dq0, bf16[128,1536]{1,0:T(8,128)(2,1)} %get-tuple-element.340.dq1, ...), custom_call_target="tpu_custom_call" | custom-call | flops 1000 | bytes 1000 | tf_op jit(solution)/shard_map/settle/pallas_call | solution.py:46
  551.7 28.4 %all-to-all-done.10 = bf16[32,78,192]{2,1,0:T(8,128)(2,1)S(1)} async-done(((bf16[32,78,192]{2,1,0:T(8,128)(2,1)}), bf16[32,78,192]{2,1,0:T(8,128)(2,1)S(1)}, u32[]{:S(2)}, u32[]{:S(2)}) %all-to-all-start.10) | async-done | bytes 958496 | tf_op jit(solution)/shard_map/all_to_all | solution.py:976
  584.5 10.8 %all-to-all-done.11 = bf16[8,96,192]{2,1,0:T(8,128)(2,1)S(1)} async-done(((bf16[8,96,192]{2,1,0:T(8,128)(2,1)}), bf16[8,96,192]{2,1,0:T(8,128)(2,1)S(1)}, u32[]{:S(2)}, u32[]{:S(2)}) %all-to-all-start.11) | async-done | bytes 294944 | tf_op jit(solution)/shard_map/all_to_all | solution.py:870
  618.9 8.7 %tail.1 = f32[640,768]{1,0:T(8,128)} custom-call(s32[4]{0:T(128)} %pad_add_fusion.order, bf16[576,640]{1,0:T(8,128)(2,1)} %get-tuple-element.361.refs_0_, bf16[576,640]{1,0:T(8,128)(2,1)} %copy-done.30, bf16[576,640]{1,0:T(8,128)(2,1)} %copy-done.31, bf16[576,640]{1,0:T(8,128)(2,1)} %collective-permute-done.34.refs_3_, ...), custom_call_target="tpu_custom_call" | custom-call | flops 1000 | bytes 1000 | tf_op jit(solution)/shard_map/tail/pallas_call | solution.py:46
  627.6 12.4 %all-to-all-done.12 = bf16[8,408,192]{1,2,0:T(8,128)(2,1)S(1)} async-done(((bf16[8,408,192]{1,2,0:T(8,128)(2,1)}), bf16[8,408,192]{1,2,0:T(8,128)(2,1)S(1)}, u32[]{:S(2)}, u32[]{:S(2)}) %all-to-all-start.12) | async-done | bytes 1253408 | tf_op jit(solution)/shard_map/all_to_all | solution.py:1023
  (312 shorter events, 232.2 us)
Async XLA Ops:
  47.7 148.7 %all-gather.4.cloned.1.call-start = ((), (), s32[]{:S(2)}) async-start(), calls=%async_computation.15 | async-start | bytes 11796480 | tf_op jit(solution)/shard_map/all_gather | solution.py:877
  71.4 39.1 %all-to-all-start.1 = ((bf16[8,80,768]{2,1,0:T(8,128)(2,1)}), bf16[8,80,768]{2,1,0:T(8,128)(2,1)S(1)}, u32[]{:S(2)}, u32[]{:S(2)}) async-start(bf16[8,80,768]{2,1,0:T(8,128)(2,1)} %get-tuple-element.228), calls=%async_computation.1 | async-start | bytes 1966080 | tf_op jit(solution)/shard_map/all_to_all | solution.py:870
  111.5 38.8 %all-to-all-start.2 = ((bf16[8,80,768]{2,1,0:T(8,128)(2,1)}), bf16[8,80,768]{2,1,0:T(8,128)(2,1)S(1)}, u32[]{:S(2)}, u32[]{:S(2)}) async-start(bf16[8,80,768]{2,1,0:T(8,128)(2,1)} %get-tuple-element.244), calls=%async_computation.2 | async-start | bytes 1966080 | tf_op jit(solution)/shard_map/all_to_all | solution.py:870
  120.3 126.5 %all-gather.8.cloned.1.call-start = ((), (), s32[]{:S(2)}) async-start(), calls=%async_computation.17 | async-start | bytes 11796480 | tf_op jit(solution)/shard_map/all_gather | solution.py:894
  154.0 34.9 %all-to-all-start.3 = ((bf16[8,96,768]{2,1,0:T(8,128)(2,1)}), bf16[8,96,768]{2,1,0:T(8,128)(2,1)S(1)}, u32[]{:S(2)}, u32[]{:S(2)}) async-start(bf16[8,96,768]{2,1,0:T(8,128)(2,1)} %send_noted.1), calls=%async_computation.3 | async-start | bytes 2359296 | tf_op jit(solution)/shard_map/all_to_all | solution.py:870
  160.0 138.2 %all-gather.6.cloned.1.call-start = ((), (), s32[]{:S(2)}) async-start(), calls=%async_computation.16 | async-start | bytes 4423680 | tf_op jit(solution)/shard_map/all_gather | solution.py:880
  189.9 53.0 %all-to-all-start.5 = ((bf16[8,160,768]{2,1,0:T(8,128)(2,1)}), bf16[8,160,768]{2,1,0:T(8,128)(2,1)}, u32[]{:S(2)}, u32[]{:S(2)}) async-start(bf16[8,160,768]{2,1,0:T(8,128)(2,1)} %bitcast.131), calls=%async_computation.5 | async-start | bytes 3932160 | tf_op jit(solution)/shard_map/all_to_all | solution.py:843
  211.3 30.0 %collective-permute-start.15 = (s32[2,160]{1,0:T(2,128)S(1)}, s32[2,160]{1,0:T(2,128)S(1)}, u32[]{:S(2)}, u32[]{:S(2)}) collective-permute-start(s32[2,160]{1,0:T(2,128)S(1)} %bitcast.150), channel_id=1, source_target_pairs={{0,3},{1,2},{2,1},{3,0},{4,7},{5,6},{6,5},{7,4},{8,11},{9,10},{10,... | collective-permute-start | bytes 3848 | tf_op jit(solution)/shard_map/ppermute | solution.py:786
  242.9 55.3 %all-to-all-start.4 = ((bf16[8,160,768]{2,1,0:T(8,128)(2,1)}), bf16[8,160,768]{2,1,0:T(8,128)(2,1)S(1)}, u32[]{:S(2)}, u32[]{:S(2)}) async-start(bf16[8,160,768]{2,1,0:T(8,128)(2,1)} %bitcast.21), calls=%async_computation.4 | async-start | bytes 3932160 | tf_op jit(solution)/shard_map/all_to_all | solution.py:843
  246.5 113.0 %reduce-scatter.3.cloned.1.call-start = ((), (), s32[]{:S(2)}) async-start(), calls=%async_computation.18 | async-start | bytes 5898240 | tf_op jit(solution)/shard_map/reduce_scatter | solution.py:944
  300.8 58.7 %all-to-all-start.6 = ((bf16[8,160,768]{2,1,0:T(8,128)(2,1)}), bf16[8,160,768]{2,1,0:T(8,128)(2,1)S(1)}, u32[]{:S(2)}, u32[]{:S(2)}) async-start(bf16[8,160,768]{2,1,0:T(8,128)(2,1)} %bitcast.137), calls=%async_computation.6 | async-start | bytes 3932160 | tf_op jit(solution)/shard_map/all_to_all | solution.py:843
  360.7 49.0 %all-to-all-start.7 = ((bf16[8,160,768]{2,1,0:T(8,128)(2,1)}), bf16[8,160,768]{2,1,0:T(8,128)(2,1)}, u32[]{:S(2)}, u32[]{:S(2)}) async-start(bf16[8,160,768]{2,1,0:T(8,128)(2,1)} %bitcast.136), calls=%async_computation.8 | async-start | bytes 3932160 | tf_op jit(solution)/shard_map/all_to_all | solution.py:843
  366.6 130.4 %reduce-scatter.5.cloned.1.call-start = ((), (), s32[]{:S(2)}) async-start(), calls=%async_computation.19 | async-start | bytes 5898240 | tf_op jit(solution)/shard_map/reduce_scatter | solution.py:953
  370.5 34.8 %collective-permute-start.21 = (bf16[192,3072]{1,0:T(8,128)(2,1)S(1)}, bf16[192,3072]{1,0:T(8,128)(2,1)}, u32[]{:S(2)}, u32[]{:S(2)}) collective-permute-start(bf16[192,3072]{1,0:T(8,128)(2,1)S(1)} %add_convert_fusion.1), channel_id=1, source_target_pairs={{0,16},{8,24},{16,0},{24,8},{1,17},{9,25},{17,1},{25,9},{2,18},{10... | collective-permute-start | bytes 3538952 | tf_op jit(solution)/shard_map/ppermute | solution.py:786
  421.3 61.4 %all-to-all-start.8 = ((bf16[8,160,768]{2,1,0:T(8,128)(2,1)}), bf16[8,160,768]{2,1,0:T(8,128)(2,1)S(1)}, u32[]{:S(2)}, u32[]{:S(2)}) async-start(bf16[8,160,768]{2,1,0:T(8,128)(2,1)} %bitcast.132), calls=%async_computation.9 | async-start | bytes 3932160 | tf_op jit(solution)/shard_map/all_to_all | solution.py:843
  484.3 54.1 %all-to-all-start.9 = ((bf16[8,160,768]{2,1,0:T(8,128)(2,1)}), bf16[8,160,768]{2,1,0:T(8,128)(2,1)}, u32[]{:S(2)}, u32[]{:S(2)}) async-start(bf16[8,160,768]{2,1,0:T(8,128)(2,1)} %bitcast.128), calls=%async_computation.10 | async-start | bytes 3932160 | tf_op jit(solution)/shard_map/all_to_all | solution.py:843
  493.5 33.4 %collective-permute-start.31 = (bf16[192,3072]{1,0:T(8,128)(2,1)S(1)}, bf16[192,3072]{1,0:T(8,128)(2,1)S(1)}, u32[]{:S(2)}, u32[]{:S(2)}) collective-permute-start(bf16[192,3072]{1,0:T(8,128)(2,1)S(1)} %add_convert_fusion), channel_id=1, source_target_pairs={{0,16},{8,24},{16,0},{24,8},{1,17},{9,25},{17,1},{25,9},{2,18},{10... | collective-permute-start | bytes 3538952 | tf_op jit(solution)/shard_map/ppermute | solution.py:786
  497.1 30.5 %collective-permute-start.30 = (bf16[192,768]{1,0:T(8,128)(2,1)S(1)}, bf16[192,768]{1,0:T(8,128)(2,1)S(1)}, u32[]{:S(2)}, u32[]{:S(2)}) collective-permute-start(bf16[192,768]{1,0:T(8,128)(2,1)S(1)} %add_convert_fusion.3), channel_id=1, source_target_pairs={{0,16},{8,24},{16,0},{24,8},{1,17},{9,25},{17,1},{25,9},{2,18},{10... | collective-permute-start | bytes 884744 | tf_op jit(solution)/shard_map/ppermute | solution.py:786
  540.8 39.3 %all-to-all-start.10 = ((bf16[32,78,192]{2,1,0:T(8,128)(2,1)}), bf16[32,78,192]{2,1,0:T(8,128)(2,1)S(1)}, u32[]{:S(2)}, u32[]{:S(2)}) async-start(bf16[32,78,192]{2,1,0:T(8,128)(2,1)} %reshape.224), calls=%async_computation.12 | async-start | bytes 2621440 | tf_op jit(solution)/shard_map/all_to_all | solution.py:976
  546.9 55.9 %collective-permute-start.35 = (bf16[192,3072]{1,0:T(8,128)(2,1)}, bf16[192,3072]{1,0:T(8,128)(2,1)}, u32[]{:S(2)}, u32[]{:S(2)}) collective-permute-start(bf16[192,3072]{1,0:T(8,128)(2,1)} %get-tuple-element.375), channel_id=1, source_target_pairs={{0,8},{8,0},{16,24},{24,16},{1,9},{9,1},{17,25},{25,17},{2,10},{10... | collective-permute-start | bytes 3538952 | tf_op jit(solution)/shard_map/ppermute | solution.py:786
  547.3 48.0 %collective-permute-start.32 = (bf16[576,640]{1,0:T(8,128)(2,1)}, bf16[576,640]{1,0:T(8,128)(2,1)S(1)}, u32[]{:S(2)}, u32[]{:S(2)}) collective-permute-start(bf16[576,640]{1,0:T(8,128)(2,1)} %get-tuple-element.355), channel_id=1, source_target_pairs={{0,16},{8,24},{16,0},{24,8},{1,17},{9,25},{17,1},{25,9},{2,18},{10... | collective-permute-start | bytes 2211848 | tf_op jit(solution)/shard_map/ppermute | solution.py:786
  548.9 46.4 %collective-permute-start.33 = (bf16[576,640]{1,0:T(8,128)(2,1)}, bf16[576,640]{1,0:T(8,128)(2,1)S(1)}, u32[]{:S(2)}, u32[]{:S(2)}) collective-permute-start(bf16[576,640]{1,0:T(8,128)(2,1)} %get-tuple-element.356), channel_id=1, source_target_pairs={{0,8},{8,0},{16,24},{24,16},{1,9},{9,1},{17,25},{25,17},{2,10},{10... | collective-permute-start | bytes 2211848 | tf_op jit(solution)/shard_map/ppermute | solution.py:786
  549.0 46.3 %collective-permute-start.34 = (bf16[576,640]{1,0:T(8,128)(2,1)}, bf16[576,640]{1,0:T(8,128)(2,1)}, u32[]{:S(2)}, u32[]{:S(2)}) collective-permute-start(bf16[576,640]{1,0:T(8,128)(2,1)} %get-tuple-element.357), channel_id=1, source_target_pairs={{0,24},{8,16},{16,8},{24,0},{1,25},{9,17},{17,9},{25,1},{2,26},{10... | collective-permute-start | bytes 2211848 | tf_op jit(solution)/shard_map/ppermute | solution.py:786
  597.5 42.5 %all-to-all-start.12 = ((bf16[8,408,192]{1,2,0:T(8,128)(2,1)}), bf16[8,408,192]{1,2,0:T(8,128)(2,1)S(1)}, u32[]{:S(2)}, u32[]{:S(2)}) async-start(bf16[8,408,192]{1,2,0:T(8,128)(2,1)} %broadcast_in_dim.87), calls=%async_computation.14 | async-start | bytes 3145728 | tf_op jit(solution)/shard_map/all_to_all | solution.py:1023
  (82 other events, 985.5 us)
Sparse Core Ops, SparseCore 0:
  71.5 69.4 all-gather.3
  150.4 64.6 all-gather.7
  216.7 30.7 all-gather.5
  298.3 48.7 reduce-scatter.2
  370.4 54.8 reduce-scatter.4

commit v3 on v2

--- a/solution.py
+++ b/solution.py
@@ -536,19 +536,20 @@
 NOTES = 16
 
 
-def send_kernel(code, value, *outs):
-    blocks, count = outs[0].shape[:2]
-    slot = lax.broadcasted_iota(jnp.int32, (count, value.shape[0]), 0)
-    for block in range(blocks):
-        for number, out in enumerate(outs):
-            here = slot + ((number // 2 * blocks + block) * 2 + number % 2) * count
-            pick = ((here == code[0:1, :]) | (here == code[1:2, :])).astype(bfloat)
-            out[block] = dot(pick, value[...]).astype(bfloat)
-
-
-def send_rows(code, value, blocks, slot_rows):
-    shape = (blocks, slot_rows // 2, value.shape[1])
-    return once(send_kernel, "send_rows", (code, value), [(shape, bfloat)] * 4)
+def send_kernel(place, value, *outs):
+    begin = 0
+    for out in outs:
+        count = out.shape[0]
+        here = lax.broadcasted_iota(jnp.int32, (count, value.shape[0]), 0) + begin
+        pick = ((here == place[0:1, :]) | (here == place[1:2, :])).astype(bfloat)
+        out[...] = dot(pick, value[...]).astype(bfloat)
+        begin += count
+
+
+def send_rows(place, value, blocks, counts):
+    shapes = [((blocks * count, value.shape[1]), bfloat) for count in counts]
+    found = once(send_kernel, "send_rows", (place, value), shapes)
+    return [part.reshape(blocks, count, -1) for part, count in zip(found, counts)]
 
 
 def send_noted_kernel(part, notes, out):
@@ -610,31 +611,36 @@
     return once(finish_kernel, "finish", (z0, z1, code, y), [(y.shape, bfloat)])[0]
 
 
-def unpack_kernel(value, wq, wk, wv, gain, q_out, k_out, v_out, other_out, gain_out):
-    lanes, _, part = value.shape
+def unpack_kernel(value, wq, wk, wv, gain, q_out, k_out, v_out, router_out, norm_out, rel_out, gain_out):
+    blocks, lanes, count, part = value.shape
     heads = part // HEAD_DIM
     mark = 3 * part
     others = None
     for lane in range(lanes):
-        whole = value[lane, :mark, :].astype(single).T
+        rows = jnp.concatenate([value[block, lane] for block in range(blocks)], axis=0)
+        whole = rows[:mark, :].astype(single).T
         for head in range(heads):
             at = slice((lane * heads + head) * HEAD_DIM, (lane * heads + head + 1) * HEAD_DIM)
             for number, ref in enumerate((q_out, k_out, v_out)):
                 begin = (3 * head + number) * HEAD_DIM
                 ref[:, at] = whole[:, begin : begin + HEAD_DIM]
-        term = value[lane, mark + 16 : mark + 32 + other_out.shape[0] - 16, :].astype(single)
+        term = rows[mark : mark + 32 + router_out.shape[1], :].astype(single)
+        rel_out[lane : lane + 1, :] = term[0:1, :]
         others = term if others is None else others + term
-    other_out[...] = others
+    norm_out[...] = others[16:17, :]
+    router_out[...] = others[32:, :].T
     total = None
     for ref, weight in ((q_out, wq), (k_out, wk), (v_out, wv)):
         term = jnp.sum(ref[...] * weight[...].astype(single), axis=1, keepdims=True)
         total = term if total is None else total + term
-    gain_out[...] = total / gain[...].astype(single)
-
-
-def unpack(value, wq, wk, wv, gain, heads, experts):
+    total = jnp.broadcast_to(total / gain[...].astype(single), (part, 128))
+    gain_out[...] = total.T[0:1, :]
+
+
+def unpack(value, wq, wk, wv, gain, experts):
     part, width = wq.shape
-    outputs = [((part, width), single)] * 3 + [((16 + experts, part), single), ((part, 1), single)]
+    outputs = [((part, width), single)] * 3
+    outputs += [((part, experts), single), ((1, part), single), ((value.shape[1], part), single), ((1, part), single)]
     return once(unpack_kernel, "unpack", (value, wq, wk, wv, gain), outputs)
 
 
@@ -838,6 +844,16 @@
     code = (pair_routes % local) * slots + (pair_routes // local) * slot_rows + local_rank
     code_t = code.reshape(top_count, rows)
     code = code_t.T
+    third, half = slot_rows * 3 // 10, slot_rows // 2
+    second = slot_rows - third
+    counts = (third, second - third, third + half, slot_rows - half)
+    held = ((0, 0, third, 0, 0), (0, third, second, 1, 0), (0, second, slot_rows, 2, 0), (1, 0, half, 2, third))
+    send_place = jnp.zeros_like(local_rank)
+    for owner, lowest, highest, number, skip in held + ((1, half, slot_rows, 3, 0),):
+        inside = (pair_routes % local == owner) & (local_rank >= lowest) & (local_rank < highest)
+        row = blocks * sum(counts[:number]) + (pair_routes // local) * counts[number] + skip
+        send_place = send_place + jnp.where(inside, row + local_rank - lowest, 0)
+    send_place = send_place.reshape(top_count, rows)
 
     def exchange(value):
         return lax.all_to_all(
@@ -862,15 +878,16 @@
     low = low - base + WINDOW
     need = (jnp.max(low.reshape(-1, QB), axis=1) > jnp.arange(total // QB) * QB).astype(jnp.int32)
     low = low.reshape(1, total)
-    packed = pack(order, w_query, w_key, w_value, w_router.T, gains)
-    far, near, code_t, low, need, vecs, code, packed = tie(far, near, code_t, low, need, vecs, code, packed)
-    packed = trade(packed)
-    both = swap(far, "head", 1)
-    cot_parts = list(send_rows(code_t, cotangent, blocks, slot_rows))
+    packed = trade(pack(order, w_query, w_key, w_value, w_router.T, gains))
+    cot_parts = send_rows(send_place, cotangent, blocks, counts)
     spread_out = lambda value: lax.all_to_all(value, "seq", split_axis=0, concat_axis=0, tiled=True)
     cots = [spread_out(cot_parts[0])]
-    packed, both, w_second, w_out, cots[0], cot_parts = tie(packed, both, w_second, w_out, cots[0], cot_parts)
+    far, near, packed, cots, cot_parts, low, need, vecs, code = tie(
+        far, near, packed, cots, cot_parts, low, need, vecs, code
+    )
+    both = swap(far, "head", 1)
     cots.append(spread_out(cot_parts[1]))
+    both, w_second, w_out = tie(both, w_second, w_out)
 
     out_far = swap(w_out, "head", 2)
     out_near = swap(w_out, "head", 1)
@@ -889,13 +906,12 @@
     ot, out_far, out_near = tie(ot, out_far, out_near)
     w_outs = (w_out, out_far, out_near, swap(out_far, "head", 1))
     ots = trade(ot)
-    ots, w_first, cots[2], cot_parts[3] = tie(ots, w_first, cots[2], cot_parts[3])
+    ots, w_first, cots[2] = tie(ots, w_first, cots[2])
     noted = spread_out(send_noted(cot_parts[3], gains[2:3].astype(bfloat)))
     first_full = lax.all_gather(w_first, "head", axis=1, tiled=True)
 
     y, *sends = middle(ots, w_outs, x, gain_two, code_t, slots)
     sends[0], noted = tie(sends[0], noted)
-    cots.append(noted[:, NOTES:, :])
 
     tallies = noted[:, 0, :].reshape(blocks * lanes, part).astype(jnp.int32)
     ahead = (tallies[:, experts : experts + 1] < block_rank[None, :]).astype(jnp.int32)
@@ -907,7 +923,8 @@
         + jnp.where(slot_ids == code_t[1:2], jnp.where(kept[1:2], route_t[0:1] + 1, 0), 0),
         axis=1,
     )
-    cot_slots = [jnp.concatenate([cots[2 * i], cots[2 * i + 1]], axis=1).reshape(slots, width) for i in range(local)]
+    cot_slots = [[cots[0], cots[1], cots[2][:, :third]], [cots[2][:, third:], noted[:, NOTES:, :]]]
+    cot_slots = [jnp.concatenate(value, axis=1).reshape(slots, width) for value in cot_slots]
     backs = [dot(cot_slots[0], second_full[0], NT).astype(bfloat)]
     other, backs[0] = tie(other, backs[0])
     other = other.reshape(local, blocks, slot_rows)
@@ -964,11 +981,10 @@
         returns[0], returns[1], code, y, gain_two, cotangent, w_outs, ots
     )
     douts, outw = trade(douts[:lanes]), douts[lanes:]
+    outw_cross, outw_direct = near_parts(outw)
     dy, z0 = tie(dy, z0)
     z_back = [exchange(z0)]
-    douts, outw, cross1, direct1 = tie(douts, outw, cross1, direct1)
-    outw_cross, outw_direct = near_parts(outw)
-    across1 = swap(add(first_parts1[1], cross1, bfloat), "head", 2)
+    douts, outw_cross, outw_direct, cross1, direct1 = tie(douts, outw_cross, outw_direct, cross1, direct1)
 
     def sum_blocks(value):
         count, last = value.shape[1:]
@@ -980,8 +996,15 @@
         0, early, (0, heads), order, need, low, qt, kvp, kv, vecs, lse_early, douts
     )
     behind = lax.ppermute(behind, "seq", [(i + 1, i) for i in range(blocks - 1)])
-    dq_early, outw_cross, outw_direct, second1 = tie(dq_early, outw_cross, outw_direct, second1)
+    dq_early, second1 = tie(dq_early, second1)
     outw_across = swap(add(outw[1], outw_cross, bfloat), "head", 2)
+    hops = [1 << bit for bit in range(blocks.bit_length() - 1)]
+
+    def hop(value, masks):
+        for mask in masks:
+            value = add(value, swap(value, "seq", mask), bfloat)
+        return value
+
     cut = heads - 1
 
     def later_part(span):
@@ -990,13 +1013,17 @@
         )
 
     dq_last, dkv_last, sums_last = later_part((cut, heads - cut))
-    dkv_last, z_back[0], z1, behind = tie(dkv_last, z_back[0], z1, behind)
+    dkv_last, z_back[0], z1, behind, outw_across, cross1 = tie(
+        dkv_last, z_back[0], z1, behind, outw_across, cross1
+    )
+    across1 = swap(add(first_parts1[1], cross1, bfloat), "head", 2)
+    grad_outw = add(add(outw[0], outw_direct), outw_across, bfloat)
+    grad_outw = hop(grad_outw, hops[:-2])
     z_back.append(exchange(z1))
     ds_early, dkv_last = tie(ds_early, dkv_last)
     dq_first, dkv_first, sums_first = later_part((0, cut))
-    dq_first, outw_across, across1 = tie(dq_first, outw_across, across1)
-    grad_outw = add(add(outw[0], outw_direct), outw_across, bfloat)
-    grad_outw = spread_out(grad_outw.reshape(blocks, -1, part))
+    dq_first, grad_outw, across1 = tie(dq_first, grad_outw, across1)
+    grad_outw = hop(grad_outw, hops[-2:-1])
     *parts, grad_part = settle(
         order,
         dq_early,
@@ -1011,25 +1038,21 @@
     )
     pieces = trade(parts)
     first1 = add(add(first_parts1[0], direct1), across1)
-    output = finish(z_back[0], z_back[1], code, y).reshape(hidden_in.shape)
-
     grad_part, z_back[1] = tie(grad_part, z_back[1])
     value = sum_blocks(grad_part)
-    value, dy, pieces, grad_outw = tie(value, dy, pieces, grad_outw)
-    grad_hidden = tail(order, pieces, w_rows_full, x, gain_one, dy).reshape(hidden_in.shape)
-    grad_outw = jnp.sum(grad_outw.astype(single), axis=0).astype(bfloat)
+    output = finish(z_back[0], z_back[1], code, y).reshape(hidden_in.shape)
+    value, grad_outw, pieces[1], pieces[2], output = tie(value, grad_outw, pieces[1], pieces[2], output)
+    grad_outw = hop(grad_outw, hops[-1:])
     count = value.shape[1]
-    value = jnp.concatenate([value.reshape(-1, part), grad_outw], axis=0)
     value = lax.all_to_all(
         jnp.broadcast_to(value[None], (blocks,) + value.shape), "seq", split_axis=0, concat_axis=0, tiled=True
     )
-    grad_outw = value[:, lanes * count :, :].reshape(part, width)
-    value = value[:, : lanes * count, :].reshape(blocks, lanes, count, part)
-    value = value.transpose(1, 0, 2, 3).reshape(lanes, -1, part)
-    mark = 3 * part
-    grad_rel = value[:, mark, : heads * BUCKETS].astype(single)
-    grad_rel = lax.dynamic_index_in_dim(grad_rel, lane, 0, keepdims=False)
-    *grads, others, grad_norm1 = unpack(value, w_query, w_key, w_value, norm1_gain.reshape(part, 1), heads, experts)
+    grad_hidden = tail(order, pieces, w_rows_full, x, gain_one, dy).reshape(hidden_in.shape)
+    value, grad_hidden = tie(value, grad_hidden)
+    if count % 16:
+        value = value.transpose(1, 0, 2, 3).reshape(1, lanes, -1, part)
+    *grads, grad_router, grad_norm2, rels, grad_norm1 = unpack(value, w_query, w_key, w_value, norm1_gain.reshape(part, 1), experts)
+    grad_rel = lax.dynamic_index_in_dim(rels, lane, 0, keepdims=False)[: heads * BUCKETS]
     return (
         output,
         grad_hidden,
@@ -1039,8 +1062,8 @@
         grads[2],
         grad_outw.astype(single),
         grad_rel,
-        others[0],
-        others[16:].T,
+        grad_norm2.reshape(part),
+        grad_router,
         jnp.stack([first0, first1]),
         jnp.stack([second0, second1]).astype(single),
     )

time: 674 us -> 638 us (0.947)
  waiting for transfers between devices: 165 us -> 151 us
  local copies, waits for them, and re-layouts: 41.7 us -> 32 us
    ppermute x34 -> x37, waiting for transfers between devices: 82.8 us -> 114 us  [swap(): lax.ppermute(value, axis, [(i, i ^ mask) for i in range(lax.axis_size(axi...]
    all_to_all x1, waiting for transfers between devices: 28.4 us -> 0.01 us  [sum_blocks(): lax.all_to_all(value, ('head', 'seq'), split_axis=0, concat_axis=0, tiled...]
    all_to_all x5 -> x4, waiting for transfers between devices: 32.5 us -> 21.2 us  [per_device(): lax.all_to_all(value, 'seq', split_axis=0, concat_axis=0, tiled=True)]
    all_to_all x5 -> x4, starting transfers between devices: 28 us -> 20.6 us  [per_device(): lax.all_to_all(value, 'seq', split_axis=0, concat_axis=0, tiled=True)]
    ppermute x34 -> x37, starting transfers between devices: 33.6 us -> 38.9 us  [swap(): lax.ppermute(value, axis, [(i, i ^ mask) for i in range(lax.axis_size(axi...]
    unnamed x112 -> x120, local copies, waits for them, and re-layouts: 11.9 us -> 14.1 us
  transfers between devices with their start and end apart: 54 -> 56, of which waited for: 21 -> 21; matrix products, arithmetic and copies ran while one was open for 10% -> 10% of each run, Pallas kernels for 40% -> 43%
where the time goes in v3:
time: 638 us; the launch traced here: 631 us
  Pallas kernels  275 us (43%)
  waiting for transfers between devices  151 us (24%)
  starting transfers between devices  107 us (17%)
  local copies, waits for them, and re-layouts  32 us (5%)
  other arithmetic  25.6 us (4%)
  matrix products  22.2 us (3%)
  between operations  17.1 us (3%)
    ppermute x37, waiting for transfers between devices, swap(): lax.ppermute(value, axis, [(i, i ^ mask) for i in range(lax.axis_size(axi...  114 us
    pallas_call x2, Pallas kernels, expert(): pl.pallas_call(expert_kernel, grid=(inner // block,), in_specs=[SMEM, who...  104 us
    pallas_call x10, Pallas kernels, once(): pl.pallas_call(kernel, grid=(1,), in_specs=[SMEM if value.ndim == 1 else...  71.7 us
    pallas_call x3, Pallas kernels, attention_backward(): pl.pallas_call(kernel, grid=(steps,), in_specs=specs, out_specs=out_specs...  66.6 us
    ppermute x37, starting transfers between devices, swap(): lax.ppermute(value, axis, [(i, i ^ mask) for i in range(lax.axis_size(axi...  38.9 us
    pallas_call x2, Pallas kernels, attention_forward(): pl.pallas_call(functools.partial(forward_kernel, first), grid=(steps,), i...  33.6 us
    all_to_all x6, starting transfers between devices, exchange(): lax.all_to_all(value.reshape(blocks, slot_rows, -1), 'seq', split_axis=0,...  30.1 us
    dot_general x3, matrix products, dot(): lax.dot_general(a, b, (dims, ((), ())), preferred_element_type=single)  22.2 us
  transfers between devices with their start and end apart: 56, of which 21 were waited for; matrix products, arithmetic and copies ran while one was open for 10% of the time, Pallas kernels for 43%

profile of v3, /device:TPU:0, one launch (start us, length us, event | category | flops | bytes accessed | tf_op | source)
XLA Modules:
  0.0 630.6 jit_solution(8076991175388356441)
XLA Ops:
  58.7 11.3 %project.1 = (bf16[4,640,768]{2,1,0:T(8,128)(2,1)}, bf16[192,2560]{1,0:T(8,128)(2,1)}, bf16[3,2560,128]{2,1,0:T(8,128)(2,1)}, bf16[3,1024,128]{2,1,0:T(8,128)(2,...) custom-call(s32[4]{0:T(128)} %pad_add_fusion.order, bf16[640,768]{1,0:T(8,128)(2,1)} %bitcast.142, ...), custom_call_target="tpu_custom_call" | custom-call | flops 1000 | bytes 1000 | tf_op jit(solution)/shard_map/project/pallas_call | solution.py:46
  73.9 19.3 %attend.2 = (bf16[192,640]{1,0:T(8,128)(2,1)}, bf16[192,640]{1,0:T(8,128)(2,1)}, bf16[192,640]{1,0:T(8,128)(2,1)}, bf16[192,640]{1,0:T(8,128)(2,1)}, f32[6,8,256]{2,1,0:T(8,128)}) custom-call(s32[4]{0:T(128)} %pad_add_fusion.order, s32[10]{0:T(128)} %compare_convert_fusion.1.need, s32[1,2560]{1,0:T(1,128)} %reshape.216.low, ...), custom_call_target="tpu_custom_call" | custom-call | flops 1000 | bytes 1000 | tf_op jit(solution)/shard_map/attend/pallas_call | solution.py:286
  100.2 14.3 %attend.3 = (bf16[192,640]{1,0:T(8,128)(2,1)}, bf16[192,640]{1,0:T(8,128)(2,1)}, bf16[192,640]{1,0:T(8,128)(2,1)}, bf16[192,640]{1,0:T(8,128)(2,1)}, f32[4,8,256]{2,1,0:T(8,128)}) custom-call(s32[4]{0:T(128)} %pad_add_fusion.order, s32[10]{0:T(128)} %compare_convert_fusion.1.need, s32[1,2560]{1,0:T(1,128)} %reshape.216.low, ...), custom_call_target="tpu_custom_call" | custom-call | flops 1000 | bytes 1000 | tf_op jit(solution)/shard_map/attend/pallas_call | solution.py:286
  117.7 9.8 %collective-permute-done.9.o1 = bf16[192,640]{1,0:T(8,128)(2,1)S(1)} collective-permute-done((bf16[192,640]{1,0:T(8,128)(2,1)}, bf16[192,640]{1,0:T(8,128)(2,1)S(1)}, u32[]{:S(2)}, u32[]{:S(2)}) %collective-permute-start.9) | collective-permute-done | bytes 245792 | tf_op jit(solution)/shard_map/ppermute | solution.py:792
  146.5 8.8 %middle.1 = (f32[640,768]{1,0:T(8,128)}, bf16[1280,768]{1,0:T(8,128)(2,1)}, bf16[1280,768]{1,0:T(8,128)(2,1)}) custom-call(bf16[192,640]{1,0:T(8,128)(2,1)} %get-tuple-element.235.o0, bf16[192,640]{1,0:T(8,128)(2,1)} %copy-done.29, bf16[192,640]{1,0:T(8,128)(2,1)} %copy-done.30, bf16[192,640]{1,0:T(8,128)(2,1)} %collective-permute-done.11.o3, ...), custom_call_target="tpu_custom_call" | custom-call | flops 1000 | bytes 1000 | tf_op jit(solution)/shard_map/middle/pallas_call | solution.py:46
  155.3 17.0 %all-to-all-done.3 = bf16[8,96,768]{2,1,0:T(8,128)(2,1)S(1)} async-done(((bf16[8,96,768]{2,1,0:T(8,128)(2,1)}), bf16[8,96,768]{2,1,0:T(8,128)(2,1)S(1)}, u32[]{:S(2)}, u32[]{:S(2)}) %all-to-all-start.3) | async-done | bytes 1179680 | tf_op jit(solution)/shard_map/all_to_all | solution.py:883
  181.9 11.2 %convolution_convert_fusion.1.da = bf16[1280,3072]{1,0:T(8,128)(2,1)} fusion(bf16[1280,768]{1,0:T(8,128)(2,1)} %bitcast.158, bf16[2,3072,768]{2,1,0:T(8,128)(2,1)} %all-gather.4.cloned.1.call-done.w2), kind=kOutput, calls=%fused_computation.1 | convolution fusion | flops 6043729920 | bytes 14548992 | tf_op jit(solution)/shard_map/dot_general | solution.py:28
  214.5 10.8 %convolution_convert_fusion.da = bf16[1280,3072]{1,0:T(8,128)(2,1)} fusion(bf16[1280,768]{1,0:T(8,128)(2,1)S(1)} %bitcast.156, bf16[2,3072,768]{2,1,0:T(8,128)(2,1)} %all-gather.4.cloned.1.call-done.w2), kind=kOutput, calls=%fused_computation | convolution fusion | flops 6043729920 | bytes 14548992 | tf_op jit(solution)/shard_map/dot_general | solution.py:28
  230.8 51.3 %expert.2 = (bf16[192,3072]{1,0:T(8,128)(2,1)}, bf16[192,3072]{1,0:T(8,128)(2,1)}, bf16[192,3072]{1,0:T(8,128)(2,1)}, bf16[192,3072]{1,0:T(8,128)(2,1)}, bf16[30...) custom-call(s32[2]{0:T(128)} %get-tuple-element.438.mine, ...), custom_call_target="tpu_custom_call" | custom-call | flops 60397977600 | bytes 50331648 | tf_op jit(solution)/shard_map/expert/pallas_call | solution.py:744
  284.8 6.2 all-to-all-start.6
  290.9 52.3 %expert.3 = (bf16[192,3072]{1,0:T(8,128)(2,1)}, bf16[192,3072]{1,0:T(8,128)(2,1)}, bf16[192,3072]{1,0:T(8,128)(2,1)}, bf16[192,3072]{1,0:T(8,128)(2,1)}, bf16[30...) custom-call(s32[2]{0:T(128)} %get-tuple-element.437.mine, ...), custom_call_target="tpu_custom_call" | custom-call | flops 60397977600 | bytes 50331648 | tf_op jit(solution)/shard_map/expert/pallas_call | solution.py:744
  355.1 34.2 %collective-permute-done.21 = bf16[192,3072]{1,0:T(8,128)(2,1)} collective-permute-done((bf16[192,3072]{1,0:T(8,128)(2,1)S(1)}, bf16[192,3072]{1,0:T(8,128)(2,1)}, u32[]{:S(2)}, u32[]{:S(2)}) %collective-permute-start.21) | collective-permute-done | bytes 1179680 | tf_op jit(solution)/shard_map/ppermute | solution.py:792
  393.9 11.5 %return_rows.1 = (f32[640,768]{1,0:T(8,128)}, f32[1,768]{1,0:T(1,128)}, bf16[192,640]{1,0:T(8,128)(2,1)}, bf16[192,640]{1,0:T(8,128)(2,1)}, bf16[192,640]{1,0:T(...) custom-call(bf16[1280,768]{1,0:T(8,128)(2,1)} %bitcast.146, ...), custom_call_target="tpu_custom_call" | custom-call | flops 1000 | bytes 1000 | tf_op jit(solution)/shard_map/return_rows/pallas_call | solution.py:46
  424.3 21.6 %attend_back.3 = (bf16[192,1024]{1,0:T(8,128)(2,1)}, bf16[3,128,1024]{2,1,0:T(8,128)(2,1)}, f32[3,128,1024]{2,1,0:T(8,128)}, f32[3,1280,256]{2,1,0:T(8,128)}) custom-call(s32[5]{0:T(128)} %concatenate.40.order, s32[10]{0:T(128)} %compare_convert_fusion.1.need, s32[1,2560]{1,0:T(1,128)} %reshape.216.low, bf16[192,2560]{1,0:T(8,128)(2,1)} %get-tuple-element.209.qt, ...), custom_call_target="tpu_custom_call" | custom-call | flops 1000 | bytes 1000 | tf_op jit(solution)/shard_map/attend_back/pallas_call | solution.py:427
  449.0 16.0 %attend_back.4 = (bf16[64,1536]{1,0:T(8,128)(2,1)}, f32[1,128,2560]{2,1,0:T(8,128)}, f32[1,8,512]{2,1,0:T(8,128)}) custom-call(s32[5]{0:T(128)} %concatenate.49.order, s32[10]{0:T(128)} %compare_convert_fusion.1.need, s32[1,2560]{1,0:T(1,128)} %reshape.216.low, bf16[192,2560]{1,0:T(8,128)(2,1)} %get-tuple-element.209.qt, ...), custom_call_target="tpu_custom_call" | custom-call | flops 1000 | bytes 1000 | tf_op jit(solution)/shard_map/attend_back/pallas_call | solution.py:427
  469.7 6.0 all-to-all-start.9
  481.5 29.0 %attend_back.5 = (bf16[128,1536]{1,0:T(8,128)(2,1)}, f32[2,128,2560]{2,1,0:T(8,128)}, f32[2,8,512]{2,1,0:T(8,128)}) custom-call(s32[5]{0:T(128)} %concatenate.40.order, s32[10]{0:T(128)} %compare_convert_fusion.1.need, s32[1,2560]{1,0:T(1,128)} %reshape.216.low, bf16[192,2560]{1,0:T(8,128)(2,1)} %get-tuple-element.209.qt, ...), custom_call_target="tpu_custom_call" | custom-call | flops 1000 | bytes 1000 | tf_op jit(solution)/shard_map/attend_back/pallas_call | solution.py:427
  510.6 11.1 %settle.1 = (bf16[576,640]{1,0:T(8,128)(2,1)}, bf16[576,640]{1,0:T(8,128)(2,1)}, bf16[576,640]{1,0:T(8,128)(2,1)}, bf16[576,640]{1,0:T(8,128)(2,1)}, bf16[4,624,192]{2,1,0:T(8,128)(2,1)}) custom-call(s32[4]{0:T(128)} %pad_add_fusion.order, bf16[192,1024]{1,0:T(8,128)(2,1)} %get-tuple-element.306.dq0, bf16[128,1536]{1,0:T(8,128)(2,1)} %get-tuple-element.327.dq1, ...), custom_call_target="tpu_custom_call" | custom-call | flops 1000 | bytes 1000 | tf_op jit(solution)/shard_map/settle/pallas_call | solution.py:46
  532.4 23.9 %collective-permute-done.33 = bf16[192,768]{1,0:T(8,128)(2,1)} collective-permute-done((bf16[192,768]{1,0:T(8,128)(2,1)S(1)}, bf16[192,768]{1,0:T(8,128)(2,1)}, u32[]{:S(2)}, u32[]{:S(2)}) %collective-permute-start.33) | collective-permute-done | bytes 294944 | tf_op jit(solution)/shard_map/ppermute | solution.py:792
  557.3 6.6 %finish.1 = bf16[640,768]{1,0:T(8,128)(2,1)} custom-call(bf16[1280,768]{1,0:T(8,128)(2,1)} %bitcast.145, bf16[1280,768]{1,0:T(8,128)(2,1)} %bitcast.53.z1, s32[640,2]{1,0:T(8,128)} %bitcast.148, f32[640,768]{1,0:T(8,128)} %get-tuple-element.291.y), custom_call_target="tpu_custom_call" | custom-call | flops 1000 | bytes 1000 | tf_op jit(solution)/shard_map/finish/pallas_call | solution.py:46
  566.8 7.1 %all-to-all-start.11 = ((bf16[8,4,78,192]{3,1,2,0:T(4,128)(2,1)}), bf16[8,4,78,192]{3,1,2,0:T(4,128)(2,1)S(1)}, u32[]{:S(2)}, u32[]{:S(2)}) async-start(bf16[8,4,78,192]{3,1,2,0:T(4,128)(2,1)} %broadcast_in_dim.93), calls=%async_computation.13 | async-start | bytes 2555904 | tf_op jit(solution)/shard_map/all_to_all | solution.py:1047
  585.5 9.5 %collective-permute-done.36.refs_3_ = bf16[576,640]{1,0:T(8,128)(2,1)S(1)} collective-permute-done((bf16[576,640]{1,0:T(8,128)(2,1)S(1)}, bf16[576,640]{1,0:T(8,128)(2,1)S(1)}, u32[]{:S(2)}, u32[]{:S(2)}) %collective-permute-start.36) | collective-permute-done | bytes 737312 | tf_op jit(solution)/shard_map/ppermute | solution.py:792
  595.9 8.7 %tail.1 = f32[640,768]{1,0:T(8,128)} custom-call(s32[4]{0:T(128)} %pad_add_fusion.order, bf16[576,640]{1,0:T(8,128)(2,1)} %get-tuple-element.348.refs_0_, bf16[576,640]{1,0:T(8,128)(2,1)} %copy-done.32, bf16[576,640]{1,0:T(8,128)(2,1)} %copy-done.33, bf16[576,640]{1,0:T(8,128)(2,1)} %copy-done.34, bf16[2304,768]{1,0:T(8,128)(2,1)} %all-gather.6.cloned.1.call-done.refs_4_, ...), custom_call_target="tpu_custom_call" | custom-call | flops 1000 | bytes 1000 | tf_op jit(solution)/shard_map/tail/pallas_call | solution.py:46
  604.6 7.6 %all-to-all-done.11 = bf16[8,4,78,192]{3,1,2,0:T(4,128)(2,1)S(1)} async-done(((bf16[8,4,78,192]{3,1,2,0:T(4,128)(2,1)}), bf16[8,4,78,192]{3,1,2,0:T(4,128)(2,1)S(1)}, u32[]{:S(2)}, u32[]{:S(2)}) %all-to-all-start.11) | async-done | bytes 958496 | tf_op jit(solution)/shard_map/all_to_all | solution.py:1047
  (325 shorter events, 208.4 us)
Async XLA Ops:
  7.2 41.8 %collective-permute-start = (bf16[640,768]{1,0:T(8,128)(2,1)}, bf16[640,768]{1,0:T(8,128)(2,1)}, u32[]{:S(2)}, u32[]{:S(2)}) collective-permute-start(bf16[640,768]{1,0:T(8,128)(2,1)} %bitcast.140), channel_id=1, source_target_pairs={{0,16},{8,24},{16,0},{24,8},{1,17},{9,25},{17,1},{25,9},{2,18},{10... | collective-permute-start | bytes 2949128 | tf_op jit(solution)/shard_map/ppermute | solution.py:792
  10.2 38.8 %collective-permute-start.1 = (bf16[640,768]{1,0:T(8,128)(2,1)}, bf16[640,768]{1,0:T(8,128)(2,1)}, u32[]{:S(2)}, u32[]{:S(2)}) collective-permute-start(bf16[640,768]{1,0:T(8,128)(2,1)} %bitcast.141), channel_id=1, source_target_pairs={{0,8},{8,0},{16,24},{24,16},{1,9},{9,1},{17,25},{25,17},{2,10},{10... | collective-permute-start | bytes 2949128 | tf_op jit(solution)/shard_map/ppermute | solution.py:792
  27.3 154.6 %all-gather.4.cloned.1.call-start = ((), (), s32[]{:S(2)}) async-start(), calls=%async_computation.14 | async-start | bytes 11796480 | tf_op jit(solution)/shard_map/all_gather | solution.py:894
  52.7 40.5 %all-to-all-start.1 = ((bf16[8,64,768]{2,1,0:T(8,128)(2,1)}), bf16[8,64,768]{2,1,0:T(8,128)(2,1)S(1)}, u32[]{:S(2)}, u32[]{:S(2)}) async-start(bf16[8,64,768]{2,1,0:T(8,128)(2,1)} %bitcast.15), calls=%async_computation.1 | async-start | bytes 1572864 | tf_op jit(solution)/shard_map/all_to_all | solution.py:883
  94.1 42.0 %all-to-all-start.2 = ((bf16[8,128,768]{2,1,0:T(8,128)(2,1)}), bf16[8,128,768]{2,1,0:T(8,128)(2,1)S(1)}, u32[]{:S(2)}, u32[]{:S(2)}) async-start(bf16[8,128,768]{2,1,0:T(8,128)(2,1)} %bitcast.163), calls=%async_computation.2 | async-start | bytes 3145728 | tf_op jit(solution)/shard_map/all_to_all | solution.py:883
  99.4 131.4 %all-gather.8.cloned.1.call-start = ((), (), s32[]{:S(2)}) async-start(), calls=%async_computation.16 | async-start | bytes 11796480 | tf_op jit(solution)/shard_map/all_gather | solution.py:911
  139.9 32.4 %all-to-all-start.3 = ((bf16[8,96,768]{2,1,0:T(8,128)(2,1)}), bf16[8,96,768]{2,1,0:T(8,128)(2,1)S(1)}, u32[]{:S(2)}, u32[]{:S(2)}) async-start(bf16[8,96,768]{2,1,0:T(8,128)(2,1)} %send_noted.1), calls=%async_computation.3 | async-start | bytes 2359296 | tf_op jit(solution)/shard_map/all_to_all | solution.py:883
  143.5 138.6 %all-gather.6.cloned.1.call-start = ((), (), s32[]{:S(2)}) async-start(), calls=%async_computation.15 | async-start | bytes 4423680 | tf_op jit(solution)/shard_map/all_gather | solution.py:897
  173.8 53.1 %all-to-all-start.5 = ((bf16[8,160,768]{2,1,0:T(8,128)(2,1)}), bf16[8,160,768]{2,1,0:T(8,128)(2,1)}, u32[]{:S(2)}, u32[]{:S(2)}) async-start(bf16[8,160,768]{2,1,0:T(8,128)(2,1)} %bitcast.155), calls=%async_computation.5 | async-start | bytes 3932160 | tf_op jit(solution)/shard_map/all_to_all | solution.py:859
  226.9 55.2 %all-to-all-start.4 = ((bf16[8,160,768]{2,1,0:T(8,128)(2,1)}), bf16[8,160,768]{2,1,0:T(8,128)(2,1)S(1)}, u32[]{:S(2)}, u32[]{:S(2)}) async-start(bf16[8,160,768]{2,1,0:T(8,128)(2,1)} %bitcast.25), calls=%async_computation.4 | async-start | bytes 3932160 | tf_op jit(solution)/shard_map/all_to_all | solution.py:859
  230.5 112.7 %reduce-scatter.3.cloned.1.call-start = ((), (), s32[]{:S(2)}) async-start(), calls=%async_computation.17 | async-start | bytes 5898240 | tf_op jit(solution)/shard_map/reduce_scatter | solution.py:961
  284.8 58.4 %all-to-all-start.6 = ((bf16[8,160,768]{2,1,0:T(8,128)(2,1)}), bf16[8,160,768]{2,1,0:T(8,128)(2,1)S(1)}, u32[]{:S(2)}, u32[]{:S(2)}) async-start(bf16[8,160,768]{2,1,0:T(8,128)(2,1)} %bitcast.162), calls=%async_computation.6 | async-start | bytes 3932160 | tf_op jit(solution)/shard_map/all_to_all | solution.py:859
  344.5 49.5 %all-to-all-start.7 = ((bf16[8,160,768]{2,1,0:T(8,128)(2,1)}), bf16[8,160,768]{2,1,0:T(8,128)(2,1)}, u32[]{:S(2)}, u32[]{:S(2)}) async-start(bf16[8,160,768]{2,1,0:T(8,128)(2,1)} %bitcast.161), calls=%async_computation.8 | async-start | bytes 3932160 | tf_op jit(solution)/shard_map/all_to_all | solution.py:859
  350.3 160.3 %reduce-scatter.5.cloned.1.call-start = ((), (), s32[]{:S(2)}) async-start(), calls=%async_computation.18 | async-start | bytes 5898240 | tf_op jit(solution)/shard_map/reduce_scatter | solution.py:970
  354.2 35.1 %collective-permute-start.21 = (bf16[192,3072]{1,0:T(8,128)(2,1)S(1)}, bf16[192,3072]{1,0:T(8,128)(2,1)}, u32[]{:S(2)}, u32[]{:S(2)}) collective-permute-start(bf16[192,3072]{1,0:T(8,128)(2,1)S(1)} %add_convert_fusion.1), channel_id=1, source_target_pairs={{0,16},{8,24},{16,0},{24,8},{1,17},{9,25},{17,1},{25,9},{2,18},{10... | collective-permute-start | bytes 3538952 | tf_op jit(solution)/shard_map/ppermute | solution.py:792
  405.5 62.7 %all-to-all-start.8 = ((bf16[8,160,768]{2,1,0:T(8,128)(2,1)}), bf16[8,160,768]{2,1,0:T(8,128)(2,1)S(1)}, u32[]{:S(2)}, u32[]{:S(2)}) async-start(bf16[8,160,768]{2,1,0:T(8,128)(2,1)} %bitcast.154), calls=%async_computation.10 | async-start | bytes 3932160 | tf_op jit(solution)/shard_map/all_to_all | solution.py:859
  469.7 52.1 %all-to-all-start.9 = ((bf16[8,160,768]{2,1,0:T(8,128)(2,1)}), bf16[8,160,768]{2,1,0:T(8,128)(2,1)}, u32[]{:S(2)}, u32[]{:S(2)}) async-start(bf16[8,160,768]{2,1,0:T(8,128)(2,1)} %bitcast.153), calls=%async_computation.11 | async-start | bytes 3932160 | tf_op jit(solution)/shard_map/all_to_all | solution.py:859
  477.5 33.1 %collective-permute-start.32 = (bf16[192,3072]{1,0:T(8,128)(2,1)S(1)}, bf16[192,3072]{1,0:T(8,128)(2,1)S(1)}, u32[]{:S(2)}, u32[]{:S(2)}) collective-permute-start(bf16[192,3072]{1,0:T(8,128)(2,1)S(1)} %add_convert_fusion), channel_id=1, source_target_pairs={{0,16},{8,24},{16,0},{24,8},{1,17},{9,25},{17,1},{25,9},{2,18},{10... | collective-permute-start | bytes 3538952 | tf_op jit(solution)/shard_map/ppermute | solution.py:792
  524.1 39.8 %all-to-all-start.10 = ((bf16[32,78,192]{2,1,0:T(8,128)(2,1)}), bf16[32,78,192]{2,1,0:T(8,128)(2,1)S(1)}, u32[]{:S(2)}, u32[]{:S(2)}) async-start(bf16[32,78,192]{2,1,0:T(8,128)(2,1)} %reshape.234), calls=%async_computation.12 | async-start | bytes 2621440 | tf_op jit(solution)/shard_map/all_to_all | solution.py:992
  528.2 45.7 %collective-permute-start.38 = (bf16[192,3072]{1,0:T(8,128)(2,1)}, bf16[192,3072]{1,0:T(8,128)(2,1)}, u32[]{:S(2)}, u32[]{:S(2)}) collective-permute-start(bf16[192,3072]{1,0:T(8,128)(2,1)} %get-tuple-element.365), channel_id=1, source_target_pairs={{0,8},{8,0},{16,24},{24,16},{1,9},{9,1},{17,25},{25,17},{2,10},{10... | collective-permute-start | bytes 3538952 | tf_op jit(solution)/shard_map/ppermute | solution.py:792
  528.5 35.7 %collective-permute-start.34 = (bf16[576,640]{1,0:T(8,128)(2,1)}, bf16[576,640]{1,0:T(8,128)(2,1)S(1)}, u32[]{:S(2)}, u32[]{:S(2)}) collective-permute-start(bf16[576,640]{1,0:T(8,128)(2,1)} %get-tuple-element.342), channel_id=1, source_target_pairs={{0,16},{8,24},{16,0},{24,8},{1,17},{9,25},{17,1},{25,9},{2,18},{10... | collective-permute-start | bytes 2211848 | tf_op jit(solution)/shard_map/ppermute | solution.py:792
  530.2 34.0 %collective-permute-start.35 = (bf16[576,640]{1,0:T(8,128)(2,1)}, bf16[576,640]{1,0:T(8,128)(2,1)S(1)}, u32[]{:S(2)}, u32[]{:S(2)}) collective-permute-start(bf16[576,640]{1,0:T(8,128)(2,1)} %get-tuple-element.343), channel_id=1, source_target_pairs={{0,8},{8,0},{16,24},{24,16},{1,9},{9,1},{17,25},{25,17},{2,10},{10... | collective-permute-start | bytes 2211848 | tf_op jit(solution)/shard_map/ppermute | solution.py:792
  566.8 45.5 %all-to-all-start.11 = ((bf16[8,4,78,192]{3,1,2,0:T(4,128)(2,1)}), bf16[8,4,78,192]{3,1,2,0:T(4,128)(2,1)S(1)}, u32[]{:S(2)}, u32[]{:S(2)}) async-start(bf16[8,4,78,192]{3,1,2,0:T(4,128)(2,1)} %broadcast_in_dim.93), calls=%async_computation.13 | async-start | bytes 2555904 | tf_op jit(solution)/shard_map/all_to_all | solution.py:1047
  577.4 39.6 %collective-permute-start.37 = (bf16[192,768]{1,0:T(8,128)(2,1)S(1)}, bf16[192,768]{1,0:T(8,128)(2,1)S(1)}, u32[]{:S(2)}, u32[]{:S(2)}) collective-permute-start(bf16[192,768]{1,0:T(8,128)(2,1)S(1)} %add_convert_fusion.3), channel_id=1, source_target_pairs={{0,4},{1,5},{2,6},{3,7},{4,0},{5,1},{6,2},{7,3},{8,12},{9,13},{10,... | collective-permute-start | bytes 884744 | tf_op jit(solution)/shard_map/ppermute | solution.py:792
  (90 other events, 1062.6 us)
Sparse Core Ops, SparseCore 0:
  52.8 74.3 all-gather.3
  136.3 62.3 all-gather.7
  200.3 30.7 all-gather.5
  282.3 48.2 reduce-scatter.2
  354.1 54.8 reduce-scatter.4

commit v4 on v3

--- a/solution.py
+++ b/solution.py
@@ -671,7 +671,7 @@
 
 
 def expert_kernel(
-    mine, xs, router, other, w1, w2, da, cot, g10, g11, g12, g13, g2, dx_out, z_out, m_out, total, result, dgate, gate, act_all, du_all, xst, dzt
+    mine, xs, router, other, w1, da, cot, g10, g11, g12, g13, g2, dx_out, a_out, m_out, total, dgate, gate, act_all, du_all, xst, dzt
 ):
     step = pl.program_id(0)
     rows = xs.shape[0]
@@ -691,7 +691,6 @@
         gate[...] = jnp.broadcast_to(value, gate.shape)
         dgate[...] = jnp.zeros_like(dgate)
         total[...] = jnp.zeros_like(total)
-        result[...] = jnp.zeros_like(result)
         for begin in range(0, rows, ROW_BLOCK):
             at = slice(begin, begin + ROW_BLOCK)
             xst[:, at] = xs[at, :].T
@@ -712,9 +711,9 @@
             part = part + product[:, col : col + 128]
         dgate[at, :] += part
         act_all[at, :] = act.astype(bfloat)
+        a_out[at, :] = (act * gate[at, 0:1]).astype(bfloat)
         du_all[at, :] = (gate[at, 0:1] * back * slope).astype(bfloat)
     total[...] += dot(du_all[...], w1[...], NT)
-    result[...] += dot(act_all[...], w2[...])
     grad = dot(xst[...], du_all[...]).astype(bfloat)
     part = g10.shape[0]
 
@@ -732,10 +731,9 @@
         m = (weight * (own.astype(single) - rest.astype(single))).astype(bfloat)
         m_out[...] = dot(m, xs[...], TN)
         dx_out[...] = (total[...] + dot(m, router[...])).astype(bfloat)
-        z_out[...] = (result[...] * value).astype(bfloat)
-
-
-def expert(mine, xs, router, other, w1, w2, da, cot, local):
+
+
+def expert(mine, xs, router, other, w1, da, cot, local):
     rows, width = xs.shape
     inner = w1.shape[2]
     experts = router.shape[0]
@@ -750,7 +748,6 @@
             whole((experts, width)),
             whole((rows, 1)),
             pl.BlockSpec((None, width, block), lambda f: (local, 0, f)),
-            pl.BlockSpec((None, block, width), lambda f: (local, f, 0)),
             pl.BlockSpec((rows, block), lambda f: (0, f)),
             whole((rows, width)),
         ],
@@ -758,18 +755,17 @@
             *[pl.BlockSpec((width // len(MASKS), block), lambda f: (0, f))] * len(MASKS),
             pl.BlockSpec((block, width), lambda f: (f, 0)),
             whole((rows, width)),
-            whole((rows, width)),
+            pl.BlockSpec((rows, block), lambda f: (0, f)),
             whole((experts, width)),
         ],
         out_shape=[
             *[jax.ShapeDtypeStruct((width // len(MASKS), inner), bfloat)] * len(MASKS),
             jax.ShapeDtypeStruct((inner, width), bfloat),
             jax.ShapeDtypeStruct((rows, width), bfloat),
-            jax.ShapeDtypeStruct((rows, width), bfloat),
+            jax.ShapeDtypeStruct((rows, inner), bfloat),
             jax.ShapeDtypeStruct((experts, width), single),
         ],
         scratch_shapes=[
-            pltpu.VMEM((rows, width), single),
             pltpu.VMEM((rows, width), single),
             pltpu.VMEM((rows, 128), single),
             pltpu.VMEM((rows, 128), single),
@@ -781,7 +777,7 @@
         compiler_params=params(60, 1),
         cost_estimate=cost(20 * rows * width * inner, 8 * rows * inner + 8 * width * inner, rows * inner),
         name="expert",
-    )(mine, xs, router, other, w1, w2, da, cot)
+    )(mine, xs, router, other, w1, da, cot)
 
 
 def tie(*values):
@@ -844,12 +840,11 @@
     code = (pair_routes % local) * slots + (pair_routes // local) * slot_rows + local_rank
     code_t = code.reshape(top_count, rows)
     code = code_t.T
-    third, half = slot_rows * 3 // 10, slot_rows // 2
-    second = slot_rows - third
-    counts = (third, second - third, third + half, slot_rows - half)
-    held = ((0, 0, third, 0, 0), (0, third, second, 1, 0), (0, second, slot_rows, 2, 0), (1, 0, half, 2, third))
+    one, two, three = slot_rows * 3 // 10, slot_rows * 7 // 10, slot_rows // 2
+    counts = (one, two - one, slot_rows - two + three, slot_rows - three)
+    held = ((0, 0, one, 0, 0), (0, one, two, 1, 0), (0, two, slot_rows, 2, 0), (1, 0, three, 2, slot_rows - two))
     send_place = jnp.zeros_like(local_rank)
-    for owner, lowest, highest, number, skip in held + ((1, half, slot_rows, 3, 0),):
+    for owner, lowest, highest, number, skip in held + ((1, three, slot_rows, 3, 0),):
         inside = (pair_routes % local == owner) & (local_rank >= lowest) & (local_rank < highest)
         row = blocks * sum(counts[:number]) + (pair_routes // local) * counts[number] + skip
         send_place = send_place + jnp.where(inside, row + local_rank - lowest, 0)
@@ -923,7 +918,8 @@
         + jnp.where(slot_ids == code_t[1:2], jnp.where(kept[1:2], route_t[0:1] + 1, 0), 0),
         axis=1,
     )
-    cot_slots = [[cots[0], cots[1], cots[2][:, :third]], [cots[2][:, third:], noted[:, NOTES:, :]]]
+    last = slot_rows - two
+    cot_slots = [[cots[0], cots[1], cots[2][:, :last]], [cots[2][:, last:], noted[:, NOTES:, :]]]
     cot_slots = [jnp.concatenate(value, axis=1).reshape(slots, width) for value in cot_slots]
     backs = [dot(cot_slots[0], second_full[0], NT).astype(bfloat)]
     other, backs[0] = tie(other, backs[0])
@@ -948,18 +944,17 @@
             router_t,
             other[number],
             first_full,
-            second_full,
             backs[number],
             cot_slots[number],
             number,
         )
 
-    received[1], w_rows_full, (*first_parts0, second0, dx0, z0, router0) = tie(
+    received[1], w_rows_full, (*first_parts0, second0, dx0, act0, router0) = tie(
         received[1], w_rows_full, run_expert(0)
     )
     returns = [exchange(dx0)]
     second0 = lax.psum_scatter(second0, "head", scatter_dimension=0, tiled=True)
-    returns[0], second0, (*first_parts1, second1, dx1, z1, router1) = tie(returns[0], second0, run_expert(1))
+    returns[0], second0, (*first_parts1, second1, dx1, act1, router1) = tie(returns[0], second0, run_expert(1))
     def near_parts(parts):
         return swap(parts[3], "head", 1), swap(parts[2], "head", 1)
 
@@ -971,11 +966,13 @@
 
     cross0, direct0 = near_parts(first_parts0)
     returns.append(exchange(dx1))
-    across0 = swap(add(first_parts0[1], cross0, bfloat), "head", 2)
+    away0, act0, act1 = tie(add(first_parts0[1], cross0, bfloat), act0, act1)
+    across0 = swap(away0, "head", 2)
     cross1, direct1 = near_parts(first_parts1)
     second1 = scatter(second1)
 
-    returns[1], across0 = tie(returns[1], across0)
+    z0, z1 = (dot(act, second_full[i]).astype(bfloat) for i, act in enumerate((act0, act1)))
+    returns[1], across0, z0, z1 = tie(returns[1], across0, z0, z1)
     first0 = add(add(first_parts0[0], direct0), across0)
     dy, gain_terms, *douts = return_rows(
         returns[0], returns[1], code, y, gain_two, cotangent, w_outs, ots
@@ -1041,14 +1038,14 @@
     grad_part, z_back[1] = tie(grad_part, z_back[1])
     value = sum_blocks(grad_part)
     output = finish(z_back[0], z_back[1], code, y).reshape(hidden_in.shape)
-    value, grad_outw, pieces[1], pieces[2], output = tie(value, grad_outw, pieces[1], pieces[2], output)
+    value, grad_outw, pieces[1], pieces[2] = tie(value, grad_outw, pieces[1], pieces[2])
     grad_outw = hop(grad_outw, hops[-1:])
     count = value.shape[1]
     value = lax.all_to_all(
         jnp.broadcast_to(value[None], (blocks,) + value.shape), "seq", split_axis=0, concat_axis=0, tiled=True
     )
     grad_hidden = tail(order, pieces, w_rows_full, x, gain_one, dy).reshape(hidden_in.shape)
-    value, grad_hidden = tie(value, grad_hidden)
+    value, grad_hidden, output = tie(value, grad_hidden, output)
     if count % 16:
         value = value.transpose(1, 0, 2, 3).reshape(1, lanes, -1, part)
     *grads, grad_router, grad_norm2, rels, grad_norm1 = unpack(value, w_query, w_key, w_value, norm1_gain.reshape(part, 1), experts)

time: 638 us -> 628 us (0.984)
  matrix products: 22.2 us -> 45.2 us
  waiting for transfers between devices: 151 us -> 130 us
  Pallas kernels: 275 us -> 265 us
    ppermute x37, waiting for transfers between devices: 114 us -> 78.7 us  [swap(): lax.ppermute(value, axis, [(i, i ^ mask) for i in range(lax.axis_size(axi...]
    dot_general x3 -> x5, matrix products: 22.2 us -> 45.2 us  [dot(): lax.dot_general(a, b, (dims, ((), ())), preferred_element_type=single)]
    pallas_call x2, Pallas kernels: 104 us -> 93.3 us  [expert(): pl.pallas_call(expert_kernel, grid=(inner // block,), in_specs=[SMEM, who...]
    all_to_all x6, waiting for transfers between devices: 4.62 us -> 14.2 us  [exchange(): lax.all_to_all(value.reshape(blocks, slot_rows, -1), 'seq', split_axis=0,...]
    unnamed x120 -> x110, local copies, waits for them, and re-layouts: 14.1 us -> 10.7 us
  transfers between devices with their start and end apart: 56 -> 56, of which waited for: 21 -> 21; matrix products, arithmetic and copies ran while one was open for 10% -> 14% of each run, Pallas kernels for 43% -> 42%
where the time goes in v4:
time: 628 us; the launch traced here: 621 us
  Pallas kernels  265 us (42%)
  waiting for transfers between devices  130 us (21%)
  starting transfers between devices  105 us (17%)
  matrix products  45.2 us (7%)
  other arithmetic  28.8 us (5%)
  local copies, waits for them, and re-layouts  28.7 us (5%)
  between operations  17.3 us (3%)
    pallas_call x2, Pallas kernels, expert(): pl.pallas_call(expert_kernel, grid=(inner // block,), in_specs=[SMEM, who...  93.3 us
    ppermute x37, waiting for transfers between devices, swap(): lax.ppermute(value, axis, [(i, i ^ mask) for i in range(lax.axis_size(axi...  78.7 us
    pallas_call x10, Pallas kernels, once(): pl.pallas_call(kernel, grid=(1,), in_specs=[SMEM if value.ndim == 1 else...  71.6 us
    pallas_call x3, Pallas kernels, attention_backward(): pl.pallas_call(kernel, grid=(steps,), in_specs=specs, out_specs=out_specs...  66.6 us
    dot_general x5, matrix products, dot(): lax.dot_general(a, b, (dims, ((), ())), preferred_element_type=single)  45.2 us
    ppermute x37, starting transfers between devices, swap(): lax.ppermute(value, axis, [(i, i ^ mask) for i in range(lax.axis_size(axi...  38.5 us
    pallas_call x2, Pallas kernels, attention_forward(): pl.pallas_call(functools.partial(forward_kernel, first), grid=(steps,), i...  33.6 us
    all_to_all x6, starting transfers between devices, exchange(): lax.all_to_all(value.reshape(blocks, slot_rows, -1), 'seq', split_axis=0,...  30.8 us
  transfers between devices with their start and end apart: 56, of which 21 were waited for; matrix products, arithmetic and copies ran while one was open for 14% of the time, Pallas kernels for 42%

profile of v4, /device:TPU:0, one launch (start us, length us, event | category | flops | bytes accessed | tf_op | source)
XLA Modules:
  0.0 621.1 jit_solution(4343462941072848603)
XLA Ops:
  52.7 6.2 all-to-all-start.1
  58.9 11.3 %project.1 = (bf16[4,640,768]{2,1,0:T(8,128)(2,1)}, bf16[192,2560]{1,0:T(8,128)(2,1)}, bf16[3,2560,128]{2,1,0:T(8,128)(2,1)}, bf16[3,1024,128]{2,1,0:T(8,128)(2,...) custom-call(s32[4]{0:T(128)} %pad_add_fusion.order, bf16[640,768]{1,0:T(8,128)(2,1)} %bitcast.150, ...), custom_call_target="tpu_custom_call" | custom-call | flops 1000 | bytes 1000 | tf_op jit(solution)/shard_map/project/pallas_call | solution.py:46
  74.2 19.3 %attend.2 = (bf16[192,640]{1,0:T(8,128)(2,1)}, bf16[192,640]{1,0:T(8,128)(2,1)}, bf16[192,640]{1,0:T(8,128)(2,1)}, bf16[192,640]{1,0:T(8,128)(2,1)}, f32[6,8,256]{2,1,0:T(8,128)}) custom-call(s32[4]{0:T(128)} %pad_add_fusion.order, s32[10]{0:T(128)} %compare_convert_fusion.1.need, s32[1,2560]{1,0:T(1,128)} %reshape.216.low, ...), custom_call_target="tpu_custom_call" | custom-call | flops 1000 | bytes 1000 | tf_op jit(solution)/shard_map/attend/pallas_call | solution.py:286
  100.3 14.3 %attend.3 = (bf16[192,640]{1,0:T(8,128)(2,1)}, bf16[192,640]{1,0:T(8,128)(2,1)}, bf16[192,640]{1,0:T(8,128)(2,1)}, bf16[192,640]{1,0:T(8,128)(2,1)}, f32[4,8,256]{2,1,0:T(8,128)}) custom-call(s32[4]{0:T(128)} %pad_add_fusion.order, s32[10]{0:T(128)} %compare_convert_fusion.1.need, s32[1,2560]{1,0:T(1,128)} %reshape.216.low, ...), custom_call_target="tpu_custom_call" | custom-call | flops 1000 | bytes 1000 | tf_op jit(solution)/shard_map/attend/pallas_call | solution.py:286
  117.7 9.8 %collective-permute-done.9.o1 = bf16[192,640]{1,0:T(8,128)(2,1)S(1)} collective-permute-done((bf16[192,640]{1,0:T(8,128)(2,1)}, bf16[192,640]{1,0:T(8,128)(2,1)S(1)}, u32[]{:S(2)}, u32[]{:S(2)}) %collective-permute-start.9) | collective-permute-done | bytes 245792 | tf_op jit(solution)/shard_map/ppermute | solution.py:788
  146.7 8.8 %middle.1 = (f32[640,768]{1,0:T(8,128)}, bf16[1280,768]{1,0:T(8,128)(2,1)}, bf16[1280,768]{1,0:T(8,128)(2,1)}) custom-call(bf16[192,640]{1,0:T(8,128)(2,1)} %get-tuple-element.240.o0, bf16[192,640]{1,0:T(8,128)(2,1)} %copy-done.30, bf16[192,640]{1,0:T(8,128)(2,1)} %copy-done.31, bf16[192,640]{1,0:T(8,128)(2,1)} %collective-permute-done.11.o3, ...), custom_call_target="tpu_custom_call" | custom-call | flops 1000 | bytes 1000 | tf_op jit(solution)/shard_map/middle/pallas_call | solution.py:46
  155.6 17.0 %all-to-all-done.3 = bf16[8,96,768]{2,1,0:T(8,128)(2,1)S(1)} async-done(((bf16[8,96,768]{2,1,0:T(8,128)(2,1)}), bf16[8,96,768]{2,1,0:T(8,128)(2,1)S(1)}, u32[]{:S(2)}, u32[]{:S(2)}) %all-to-all-start.3) | async-done | bytes 1179680 | tf_op jit(solution)/shard_map/all_to_all | solution.py:878
  182.2 11.2 %convolution_convert_fusion.1.da = bf16[1280,3072]{1,0:T(8,128)(2,1)} fusion(bf16[1280,768]{1,0:T(8,128)(2,1)} %bitcast.165, bf16[2,3072,768]{2,1,0:T(8,128)(2,1)} %all-gather.4.cloned.1.call-done), kind=kOutput, calls=%fused_computation.1 | convolution fusion | flops 6043729920 | bytes 14548992 | tf_op jit(solution)/shard_map/dot_general | solution.py:28
  214.8 10.8 %convolution_convert_fusion.da = bf16[1280,3072]{1,0:T(8,128)(2,1)} fusion(bf16[1280,768]{1,0:T(8,128)(2,1)S(1)} %bitcast.163, bf16[2,3072,768]{2,1,0:T(8,128)(2,1)} %all-gather.4.cloned.1.call-done), kind=kOutput, calls=%fused_computation | convolution fusion | flops 6043729920 | bytes 14548992 | tf_op jit(solution)/shard_map/dot_general | solution.py:28
  231.3 46.2 %expert.2 = (bf16[192,3072]{1,0:T(8,128)(2,1)}, bf16[192,3072]{1,0:T(8,128)(2,1)}, bf16[192,3072]{1,0:T(8,128)(2,1)}, bf16[192,3072]{1,0:T(8,128)(2,1)}, bf16[30...) custom-call(s32[2]{0:T(128)} %get-tuple-element.448.mine, ...), custom_call_target="tpu_custom_call" | custom-call | flops 60397977600 | bytes 50331648 | tf_op jit(solution)/shard_map/expert/pallas_call | solution.py:742
  286.3 47.1 %expert.3 = (bf16[192,3072]{1,0:T(8,128)(2,1)}, bf16[192,3072]{1,0:T(8,128)(2,1)}, bf16[192,3072]{1,0:T(8,128)(2,1)}, bf16[192,3072]{1,0:T(8,128)(2,1)}, bf16[30...) custom-call(s32[2]{0:T(128)} %get-tuple-element.447.mine, ...), custom_call_target="tpu_custom_call" | custom-call | flops 60397977600 | bytes 50331648 | tf_op jit(solution)/shard_map/expert/pallas_call | solution.py:742
  343.4 10.9 %fusion.3 = bf16[1280,768]{1,0:T(8,128)(2,1)} fusion(bf16[1280,3072]{1,0:T(8,128)(2,1)} %get-tuple-element.297, bf16[2,3072,768]{2,1,0:T(8,128)(2,1)} %all-gather.4.cloned.1.call-done), kind=kOutput, calls=%fused_computation.12 | convolution fusion | flops 6040780800 | bytes 14548992 | tf_op jit(solution)/shard_map/dot_general | solution.py:28
  354.4 12.1 %fusion.2 = bf16[1280,768]{1,0:T(8,128)(2,1)} fusion(bf16[1280,3072]{1,0:T(8,128)(2,1)} %get-tuple-element.298, bf16[2,3072,768]{2,1,0:T(8,128)(2,1)} %all-gather.4.cloned.1.call-done), kind=kOutput, calls=%fused_computation.11 | convolution fusion | flops 6040780800 | bytes 14548992 | tf_op jit(solution)/shard_map/dot_general | solution.py:28
  366.5 7.7 %collective-permute-done.21 = bf16[192,3072]{1,0:T(8,128)(2,1)} collective-permute-done((bf16[192,3072]{1,0:T(8,128)(2,1)S(1)}, bf16[192,3072]{1,0:T(8,128)(2,1)}, u32[]{:S(2)}, u32[]{:S(2)}) %collective-permute-start.21) | collective-permute-done | bytes 1179680 | tf_op jit(solution)/shard_map/ppermute | solution.py:788
  374.2 14.2 %all-to-all-done.7 = bf16[8,160,768]{2,1,0:T(8,128)(2,1)} async-done(((bf16[8,160,768]{2,1,0:T(8,128)(2,1)}), bf16[8,160,768]{2,1,0:T(8,128)(2,1)}, u32[]{:S(2)}, u32[]{:S(2)}) %all-to-all-start.7) | async-done | bytes 1966112 | tf_op jit(solution)/shard_map/all_to_all | solution.py:854
  388.4 11.5 %return_rows.1 = (f32[640,768]{1,0:T(8,128)}, f32[1,768]{1,0:T(1,128)}, bf16[192,640]{1,0:T(8,128)(2,1)}, bf16[192,640]{1,0:T(8,128)(2,1)}, bf16[192,640]{1,0:T(...) custom-call(bf16[1280,768]{1,0:T(8,128)(2,1)} %bitcast.154, ...), custom_call_target="tpu_custom_call" | custom-call | flops 1000 | bytes 1000 | tf_op jit(solution)/shard_map/return_rows/pallas_call | solution.py:46
  419.0 21.6 %attend_back.3 = (bf16[192,1024]{1,0:T(8,128)(2,1)}, bf16[3,128,1024]{2,1,0:T(8,128)(2,1)}, f32[3,128,1024]{2,1,0:T(8,128)}, f32[3,1280,256]{2,1,0:T(8,128)}) custom-call(s32[5]{0:T(128)} %concatenate.40.order, s32[10]{0:T(128)} %compare_convert_fusion.1.need, s32[1,2560]{1,0:T(1,128)} %reshape.216.low, bf16[192,2560]{1,0:T(8,128)(2,1)} %get-tuple-element.214.qt, ...), custom_call_target="tpu_custom_call" | custom-call | flops 1000 | bytes 1000 | tf_op jit(solution)/shard_map/attend_back/pallas_call | solution.py:427
  443.7 16.0 %attend_back.4 = (bf16[64,1536]{1,0:T(8,128)(2,1)}, f32[1,128,2560]{2,1,0:T(8,128)}, f32[1,8,512]{2,1,0:T(8,128)}) custom-call(s32[5]{0:T(128)} %concatenate.49.order, s32[10]{0:T(128)} %compare_convert_fusion.1.need, s32[1,2560]{1,0:T(1,128)} %reshape.216.low, bf16[192,2560]{1,0:T(8,128)(2,1)} %get-tuple-element.214.qt, ...), custom_call_target="tpu_custom_call" | custom-call | flops 1000 | bytes 1000 | tf_op jit(solution)/shard_map/attend_back/pallas_call | solution.py:427
  477.1 29.0 %attend_back.5 = (bf16[128,1536]{1,0:T(8,128)(2,1)}, f32[2,128,2560]{2,1,0:T(8,128)}, f32[2,8,512]{2,1,0:T(8,128)}) custom-call(s32[5]{0:T(128)} %concatenate.40.order, s32[10]{0:T(128)} %compare_convert_fusion.1.need, s32[1,2560]{1,0:T(1,128)} %reshape.216.low, bf16[192,2560]{1,0:T(8,128)(2,1)} %get-tuple-element.214.qt, ...), custom_call_target="tpu_custom_call" | custom-call | flops 1000 | bytes 1000 | tf_op jit(solution)/shard_map/attend_back/pallas_call | solution.py:427
  506.2 11.1 %settle.1 = (bf16[576,640]{1,0:T(8,128)(2,1)}, bf16[576,640]{1,0:T(8,128)(2,1)}, bf16[576,640]{1,0:T(8,128)(2,1)}, bf16[576,640]{1,0:T(8,128)(2,1)}, bf16[4,624,192]{2,1,0:T(8,128)(2,1)}) custom-call(s32[4]{0:T(128)} %pad_add_fusion.order, bf16[192,1024]{1,0:T(8,128)(2,1)} %get-tuple-element.316.dq0, bf16[128,1536]{1,0:T(8,128)(2,1)} %get-tuple-element.337.dq1, ...), custom_call_target="tpu_custom_call" | custom-call | flops 1000 | bytes 1000 | tf_op jit(solution)/shard_map/settle/pallas_call | solution.py:46
  527.8 23.9 %collective-permute-done.33 = bf16[192,768]{1,0:T(8,128)(2,1)S(1)} collective-permute-done((bf16[192,768]{1,0:T(8,128)(2,1)S(1)}, bf16[192,768]{1,0:T(8,128)(2,1)S(1)}, u32[]{:S(2)}, u32[]{:S(2)}) %collective-permute-start.33) | collective-permute-done | bytes 294944 | tf_op jit(solution)/shard_map/ppermute | solution.py:788
  575.1 6.6 %finish.1 = bf16[640,768]{1,0:T(8,128)(2,1)} custom-call(bf16[1280,768]{1,0:T(8,128)(2,1)} %bitcast.153, bf16[1280,768]{1,0:T(8,128)(2,1)} %bitcast.53.z1, s32[640,2]{1,0:T(8,128)} %bitcast.156, f32[640,768]{1,0:T(8,128)} %get-tuple-element.301.y), custom_call_target="tpu_custom_call" | custom-call | flops 1000 | bytes 1000 | tf_op jit(solution)/shard_map/finish/pallas_call | solution.py:46
  585.9 8.7 %tail.1 = f32[640,768]{1,0:T(8,128)} custom-call(s32[4]{0:T(128)} %pad_add_fusion.order, bf16[576,640]{1,0:T(8,128)(2,1)} %get-tuple-element.355.refs_0_, bf16[576,640]{1,0:T(8,128)(2,1)} %collective-permute-done.34.refs_1_, bf16[576,640]{1,0:T(8,128)(2,1)} %collective-permute-done.35.refs_2_, bf16[576,640]{1,0:T(8,128)(2,1)} %copy-done.32, ...), custom_call_target="tpu_custom_call" | custom-call | flops 1000 | bytes 1000 | tf_op jit(solution)/shard_map/tail/pallas_call | solution.py:46
  594.6 7.4 %all-to-all-done.11 = bf16[8,4,78,192]{3,1,2,0:T(4,128)(2,1)S(1)} async-done(((bf16[8,4,78,192]{3,1,2,0:T(4,128)(2,1)}), bf16[8,4,78,192]{3,1,2,0:T(4,128)(2,1)S(1)}, u32[]{:S(2)}, u32[]{:S(2)}) %all-to-all-start.11) | async-done | bytes 958496 | tf_op jit(solution)/shard_map/all_to_all | solution.py:1044
  (317 shorter events, 220.9 us)
Async XLA Ops:
  7.2 41.8 %collective-permute-start = (bf16[640,768]{1,0:T(8,128)(2,1)}, bf16[640,768]{1,0:T(8,128)(2,1)}, u32[]{:S(2)}, u32[]{:S(2)}) collective-permute-start(bf16[640,768]{1,0:T(8,128)(2,1)} %bitcast.148), channel_id=1, source_target_pairs={{0,16},{8,24},{16,0},{24,8},{1,17},{9,25},{17,1},{25,9},{2,18},{10... | collective-permute-start | bytes 2949128 | tf_op jit(solution)/shard_map/ppermute | solution.py:788
  10.2 38.8 %collective-permute-start.1 = (bf16[640,768]{1,0:T(8,128)(2,1)}, bf16[640,768]{1,0:T(8,128)(2,1)}, u32[]{:S(2)}, u32[]{:S(2)}) collective-permute-start(bf16[640,768]{1,0:T(8,128)(2,1)} %bitcast.149), channel_id=1, source_target_pairs={{0,8},{8,0},{16,24},{24,16},{1,9},{9,1},{17,25},{25,17},{2,10},{10... | collective-permute-start | bytes 2949128 | tf_op jit(solution)/shard_map/ppermute | solution.py:788
  27.3 154.8 %all-gather.4.cloned.1.call-start = ((), (), s32[]{:S(2)}) async-start(), calls=%async_computation.14 | async-start | bytes 11796480 | tf_op jit(solution)/shard_map/all_gather | solution.py:889
  52.7 40.8 %all-to-all-start.1 = ((bf16[8,64,768]{2,1,0:T(8,128)(2,1)}), bf16[8,64,768]{2,1,0:T(8,128)(2,1)S(1)}, u32[]{:S(2)}, u32[]{:S(2)}) async-start(bf16[8,64,768]{2,1,0:T(8,128)(2,1)} %bitcast.15), calls=%async_computation.1 | async-start | bytes 1572864 | tf_op jit(solution)/shard_map/all_to_all | solution.py:878
  94.4 41.9 %all-to-all-start.2 = ((bf16[8,128,768]{2,1,0:T(8,128)(2,1)}), bf16[8,128,768]{2,1,0:T(8,128)(2,1)S(1)}, u32[]{:S(2)}, u32[]{:S(2)}) async-start(bf16[8,128,768]{2,1,0:T(8,128)(2,1)} %bitcast.171), calls=%async_computation.2 | async-start | bytes 3145728 | tf_op jit(solution)/shard_map/all_to_all | solution.py:878
  99.6 131.6 %all-gather.8.cloned.1.call-start = ((), (), s32[]{:S(2)}) async-start(), calls=%async_computation.16 | async-start | bytes 11796480 | tf_op jit(solution)/shard_map/all_gather | solution.py:906
  140.2 32.4 %all-to-all-start.3 = ((bf16[8,96,768]{2,1,0:T(8,128)(2,1)}), bf16[8,96,768]{2,1,0:T(8,128)(2,1)S(1)}, u32[]{:S(2)}, u32[]{:S(2)}) async-start(bf16[8,96,768]{2,1,0:T(8,128)(2,1)} %send_noted.1), calls=%async_computation.3 | async-start | bytes 2359296 | tf_op jit(solution)/shard_map/all_to_all | solution.py:878
  143.8 133.7 %all-gather.6.cloned.1.call-start = ((), (), s32[]{:S(2)}) async-start(), calls=%async_computation.15 | async-start | bytes 4423680 | tf_op jit(solution)/shard_map/all_gather | solution.py:892
  174.0 53.1 %all-to-all-start.5 = ((bf16[8,160,768]{2,1,0:T(8,128)(2,1)}), bf16[8,160,768]{2,1,0:T(8,128)(2,1)}, u32[]{:S(2)}, u32[]{:S(2)}) async-start(bf16[8,160,768]{2,1,0:T(8,128)(2,1)} %bitcast.162), calls=%async_computation.5 | async-start | bytes 3932160 | tf_op jit(solution)/shard_map/all_to_all | solution.py:854
  227.2 50.3 %all-to-all-start.4 = ((bf16[8,160,768]{2,1,0:T(8,128)(2,1)}), bf16[8,160,768]{2,1,0:T(8,128)(2,1)S(1)}, u32[]{:S(2)}, u32[]{:S(2)}) async-start(bf16[8,160,768]{2,1,0:T(8,128)(2,1)} %bitcast.25), calls=%async_computation.4 | async-start | bytes 3932160 | tf_op jit(solution)/shard_map/all_to_all | solution.py:854
  230.8 105.4 %reduce-scatter.3.cloned.1.call-start = ((), (), s32[]{:S(2)}) async-start(), calls=%async_computation.17 | async-start | bytes 5898240 | tf_op jit(solution)/shard_map/reduce_scatter | solution.py:956
  280.1 56.0 %all-to-all-start.6 = ((bf16[8,160,768]{2,1,0:T(8,128)(2,1)}), bf16[8,160,768]{2,1,0:T(8,128)(2,1)S(1)}, u32[]{:S(2)}, u32[]{:S(2)}) async-start(bf16[8,160,768]{2,1,0:T(8,128)(2,1)} %bitcast.169), calls=%async_computation.6 | async-start | bytes 3932160 | tf_op jit(solution)/shard_map/all_to_all | solution.py:854
  286.2 47.2 %collective-permute-start.20 = (bf16[192,3072]{1,0:T(8,128)(2,1)}, bf16[192,3072]{1,0:T(8,128)(2,1)}, u32[]{:S(2)}, u32[]{:S(2)}) collective-permute-start(bf16[192,3072]{1,0:T(8,128)(2,1)} %get-tuple-element.293), channel_id=1, source_target_pairs={{0,8},{8,0},{16,24},{24,16},{1,9},{9,1},{17,25},{25,17},{2,10},{10... | collective-permute-start | bytes 3538952 | tf_op jit(solution)/shard_map/ppermute | solution.py:788
  336.2 52.2 %all-to-all-start.7 = ((bf16[8,160,768]{2,1,0:T(8,128)(2,1)}), bf16[8,160,768]{2,1,0:T(8,128)(2,1)}, u32[]{:S(2)}, u32[]{:S(2)}) async-start(bf16[8,160,768]{2,1,0:T(8,128)(2,1)} %bitcast.170), calls=%async_computation.8 | async-start | bytes 3932160 | tf_op jit(solution)/shard_map/all_to_all | solution.py:854
  342.3 163.9 %reduce-scatter.5.cloned.1.call-start = ((), (), s32[]{:S(2)}) async-start(), calls=%async_computation.18 | async-start | bytes 5898240 | tf_op jit(solution)/shard_map/reduce_scatter | solution.py:965
  399.9 63.3 %all-to-all-start.8 = ((bf16[8,160,768]{2,1,0:T(8,128)(2,1)}), bf16[8,160,768]{2,1,0:T(8,128)(2,1)S(1)}, u32[]{:S(2)}, u32[]{:S(2)}) async-start(bf16[8,160,768]{2,1,0:T(8,128)(2,1)} %bitcast.167), calls=%async_computation.10 | async-start | bytes 3932160 | tf_op jit(solution)/shard_map/all_to_all | solution.py:854
  463.2 54.1 %all-to-all-start.9 = ((bf16[8,160,768]{2,1,0:T(8,128)(2,1)}), bf16[8,160,768]{2,1,0:T(8,128)(2,1)}, u32[]{:S(2)}, u32[]{:S(2)}) async-start(bf16[8,160,768]{2,1,0:T(8,128)(2,1)} %bitcast.161), calls=%async_computation.11 | async-start | bytes 3932160 | tf_op jit(solution)/shard_map/all_to_all | solution.py:854
  472.1 34.1 %collective-permute-start.32 = (bf16[192,3072]{1,0:T(8,128)(2,1)}, bf16[192,3072]{1,0:T(8,128)(2,1)S(1)}, u32[]{:S(2)}, u32[]{:S(2)}) collective-permute-start(bf16[192,3072]{1,0:T(8,128)(2,1)} %add_convert_fusion), channel_id=1, source_target_pairs={{0,16},{8,24},{16,0},{24,8},{1,17},{9,25},{17,1},{25,9},{2,18},{10... | collective-permute-start | bytes 3538952 | tf_op jit(solution)/shard_map/ppermute | solution.py:788
  474.0 32.1 %collective-permute-start.31 = (bf16[192,768]{1,0:T(8,128)(2,1)S(1)}, bf16[192,768]{1,0:T(8,128)(2,1)S(1)}, u32[]{:S(2)}, u32[]{:S(2)}) collective-permute-start(bf16[192,768]{1,0:T(8,128)(2,1)S(1)} %add_convert_fusion.5), channel_id=1, source_target_pairs={{0,1},{1,0},{2,3},{3,2},{4,5},{5,4},{6,7},{7,6},{8,9},{9,8},{10,11... | collective-permute-start | bytes 884744 | tf_op jit(solution)/shard_map/ppermute | solution.py:788
  519.7 37.1 %all-to-all-start.10 = ((bf16[32,78,192]{2,1,0:T(8,128)(2,1)}), bf16[32,78,192]{2,1,0:T(8,128)(2,1)S(1)}, u32[]{:S(2)}, u32[]{:S(2)}) async-start(bf16[32,78,192]{2,1,0:T(8,128)(2,1)} %reshape.234), calls=%async_computation.12 | async-start | bytes 2621440 | tf_op jit(solution)/shard_map/all_to_all | solution.py:989
  523.6 40.1 %collective-permute-start.38 = (bf16[192,3072]{1,0:T(8,128)(2,1)}, bf16[192,3072]{1,0:T(8,128)(2,1)}, u32[]{:S(2)}, u32[]{:S(2)}) collective-permute-start(bf16[192,3072]{1,0:T(8,128)(2,1)} %get-tuple-element.375), channel_id=1, source_target_pairs={{0,8},{8,0},{16,24},{24,16},{1,9},{9,1},{17,25},{25,17},{2,10},{10... | collective-permute-start | bytes 3538952 | tf_op jit(solution)/shard_map/ppermute | solution.py:788
  523.9 33.1 %collective-permute-start.34 = (bf16[576,640]{1,0:T(8,128)(2,1)}, bf16[576,640]{1,0:T(8,128)(2,1)}, u32[]{:S(2)}, u32[]{:S(2)}) collective-permute-start(bf16[576,640]{1,0:T(8,128)(2,1)} %get-tuple-element.352), channel_id=1, source_target_pairs={{0,16},{8,24},{16,0},{24,8},{1,17},{9,25},{17,1},{25,9},{2,18},{10... | collective-permute-start | bytes 2211848 | tf_op jit(solution)/shard_map/ppermute | solution.py:788
  558.5 43.5 %all-to-all-start.11 = ((bf16[8,4,78,192]{3,1,2,0:T(4,128)(2,1)}), bf16[8,4,78,192]{3,1,2,0:T(4,128)(2,1)S(1)}, u32[]{:S(2)}, u32[]{:S(2)}) async-start(bf16[8,4,78,192]{3,1,2,0:T(4,128)(2,1)} %broadcast_in_dim.93), calls=%async_computation.13 | async-start | bytes 2555904 | tf_op jit(solution)/shard_map/all_to_all | solution.py:1044
  566.9 40.2 %collective-permute-start.37 = (bf16[192,768]{1,0:T(8,128)(2,1)S(1)}, bf16[192,768]{1,0:T(8,128)(2,1)S(1)}, u32[]{:S(2)}, u32[]{:S(2)}) collective-permute-start(bf16[192,768]{1,0:T(8,128)(2,1)S(1)} %add_convert_fusion.3), channel_id=1, source_target_pairs={{0,4},{1,5},{2,6},{3,7},{4,0},{5,1},{6,2},{7,3},{8,12},{9,13},{10,... | collective-permute-start | bytes 884744 | tf_op jit(solution)/shard_map/ppermute | solution.py:788
  (85 other events, 1182.8 us)
Sparse Core Ops, SparseCore 0:
  52.8 74.2 all-gather.3
  136.5 62.3 all-gather.7
  200.5 30.7 all-gather.5
  277.7 49.5 reduce-scatter.2
  346.1 51.1 reduce-scatter.4

commit v5 on v4

--- a/solution.py
+++ b/solution.py
@@ -482,30 +482,33 @@
     found.append(jnp.zeros((1, part - BUCKETS * heads), single))
     rel = jnp.broadcast_to(jnp.concatenate(found, axis=1), (16, part))
     router = (router0[...] + router1[...]).astype(bfloat)
+    chunk = grad.shape[1]
+    blocks = grad.shape[0] // len(outs)
     for lane in range(len(outs)):
         columns = slice(lane * part, (lane + 1) * part)
-        grad[lane, :count, :] = total[:, columns]
         mine = jnp.where(order[0] == lane, 1.0, 0.0)
-        grad[lane, count : count + 16, :] = (rel * mine).astype(bfloat)
         terms = jnp.broadcast_to(gain_terms[:, columns], (16, part))
-        grad[lane, count + 16 : count + 32, :] = terms.astype(bfloat)
-        begin = count + 32 + router.shape[0]
-        grad[lane, count + 32 : begin, :] = router[:, columns]
-        if begin < grad.shape[1]:
-            grad[lane, begin:, :] = jnp.zeros((grad.shape[1] - begin, part), bfloat)
-
-
-def settle(order, dq0, late, behind, normed, sums, hot, gain_terms, routers, multiple):
+        rows_out = [total[:, columns], (rel * mine).astype(bfloat), terms.astype(bfloat), router[:, columns]]
+        left = blocks * chunk - sum(value.shape[0] for value in rows_out)
+        if left:
+            rows_out.append(jnp.zeros((left, part), bfloat))
+        rows_out = jnp.concatenate(rows_out, axis=0)
+        for block in range(blocks):
+            grad[lane * blocks + block] = rows_out[block * chunk : (block + 1) * chunk, :]
+
+
+def settle(order, dq0, late, behind, normed, sums, hot, gain_terms, routers, blocks):
     lanes, rows, width = normed.shape
     tall = 3 * width // lanes
     count = tall + 32 + routers[0].shape[0]
-    count = -(-count // multiple) * multiple
+    count = -(-count // max(16, blocks)) * max(16, blocks)
+    cut = blocks if count // blocks % 16 == 0 else 1
     (dq1, dkv1), (dq2, dkv2) = late
     return once(
         settle_kernel,
         "settle",
         (order, dq0, dq1, dq2, dkv1, dkv2, behind, normed, *sums, hot, gain_terms, *routers),
-        [((tall, rows), bfloat)] * lanes + [((lanes, count, width // lanes), bfloat)],
+        [((tall, rows), bfloat)] * lanes + [((lanes * cut, count // cut, width // lanes), bfloat)],
     )
 
 
@@ -895,14 +898,15 @@
     early = WINDOW // QB
     later = total // QB - early
     *ot, lse_later = attention_forward(early, later, order, need, low, qt, None, kv, vecs, lanes)
-    ot, kvp, cots[1], cot_parts[2] = tie(ot, kvp, cots[1], cot_parts[2])
+    noted = send_noted(cot_parts[3], gains[2:3].astype(bfloat))
+    ot, kvp, cots[1], cot_parts[2], noted = tie(ot, kvp, cots[1], cot_parts[2], noted)
     cots.append(spread_out(cot_parts[2]))
     *ot, lse_early = attention_forward(0, early, order, need, low, qt, kvp, kv, vecs, lanes, ot)
     ot, out_far, out_near = tie(ot, out_far, out_near)
     w_outs = (w_out, out_far, out_near, swap(out_far, "head", 1))
     ots = trade(ot)
     ots, w_first, cots[2] = tie(ots, w_first, cots[2])
-    noted = spread_out(send_noted(cot_parts[3], gains[2:3].astype(bfloat)))
+    noted = spread_out(noted)
     first_full = lax.all_gather(w_first, "head", axis=1, tiled=True)
 
     y, *sends = middle(ots, w_outs, x, gain_two, code_t, slots)
@@ -972,7 +976,8 @@
     second1 = scatter(second1)
 
     z0, z1 = (dot(act, second_full[i]).astype(bfloat) for i, act in enumerate((act0, act1)))
-    returns[1], across0, z0, z1 = tie(returns[1], across0, z0, z1)
+    away1 = add(first_parts1[1], cross1, bfloat)
+    returns[1], across0, z0, z1, away1 = tie(returns[1], across0, z0, z1, away1)
     first0 = add(add(first_parts0[0], direct0), across0)
     dy, gain_terms, *douts = return_rows(
         returns[0], returns[1], code, y, gain_two, cotangent, w_outs, ots
@@ -981,11 +986,11 @@
     outw_cross, outw_direct = near_parts(outw)
     dy, z0 = tie(dy, z0)
     z_back = [exchange(z0)]
-    douts, outw_cross, outw_direct, cross1, direct1 = tie(douts, outw_cross, outw_direct, cross1, direct1)
+    douts, outw_cross, outw_direct = tie(douts, outw_cross, outw_direct)
 
     def sum_blocks(value):
-        count, last = value.shape[1:]
-        value = value.reshape(lanes * blocks, count // blocks, last)
+        last = value.shape[-1]
+        value = value.reshape(lanes * blocks, -1, last)
         value = lax.all_to_all(value, ("head", "seq"), split_axis=0, concat_axis=0, tiled=True)
         return jnp.sum(value.reshape(lanes, blocks, -1, last).astype(single), axis=1).astype(bfloat)
 
@@ -1010,10 +1015,10 @@
         )
 
     dq_last, dkv_last, sums_last = later_part((cut, heads - cut))
-    dkv_last, z_back[0], z1, behind, outw_across, cross1 = tie(
-        dkv_last, z_back[0], z1, behind, outw_across, cross1
-    )
-    across1 = swap(add(first_parts1[1], cross1, bfloat), "head", 2)
+    dkv_last, z_back[0], z1, behind, outw_across, away1 = tie(
+        dkv_last, z_back[0], z1, behind, outw_across, away1
+    )
+    across1 = swap(away1, "head", 2)
     grad_outw = add(add(outw[0], outw_direct), outw_across, bfloat)
     grad_outw = hop(grad_outw, hops[:-2])
     z_back.append(exchange(z1))
@@ -1031,7 +1036,7 @@
         jnp.asarray(hot, single),
         gain_terms,
         (router0, router1),
-        max(16, blocks),
+        blocks,
     )
     pieces = trade(parts)
     first1 = add(add(first_parts1[0], direct1), across1)

time: 628 us -> 624 us (level)
    ppermute x37, waiting for transfers between devices: 78.7 us -> 70.8 us  [swap(): lax.ppermute(value, axis, [(i, i ^ mask) for i in range(lax.axis_size(axi...]
  transfers between devices with their start and end apart: 56 -> 56, of which waited for: 21 -> 20; matrix products, arithmetic and copies ran while one was open for 14% -> 15% of each run, Pallas kernels for 42% -> 42%
where the time goes in v5:
time: 624 us; the launch traced here: 617 us
  Pallas kernels  265 us (42%)
  waiting for transfers between devices  126 us (20%)
  starting transfers between devices  105 us (17%)
  matrix products  45.3 us (7%)
  other arithmetic  30.6 us (5%)
  local copies, waits for them, and re-layouts  27.3 us (4%)
  between operations  17.2 us (3%)
    pallas_call x2, Pallas kernels, expert(): pl.pallas_call(expert_kernel, grid=(inner // block,), in_specs=[SMEM, who...  93.2 us
    pallas_call x10, Pallas kernels, once(): pl.pallas_call(kernel, grid=(1,), in_specs=[SMEM if value.ndim == 1 else...  71.6 us
    ppermute x37, waiting for transfers between devices, swap(): lax.ppermute(value, axis, [(i, i ^ mask) for i in range(lax.axis_size(axi...  70.8 us
    pallas_call x3, Pallas kernels, attention_backward(): pl.pallas_call(kernel, grid=(steps,), in_specs=specs, out_specs=out_specs...  66.6 us
    dot_general x5, matrix products, dot(): lax.dot_general(a, b, (dims, ((), ())), preferred_element_type=single)  45.3 us
    ppermute x37, starting transfers between devices, swap(): lax.ppermute(value, axis, [(i, i ^ mask) for i in range(lax.axis_size(axi...  38.8 us
    pallas_call x2, Pallas kernels, attention_forward(): pl.pallas_call(functools.partial(forward_kernel, first), grid=(steps,), i...  33.7 us
    all_to_all x6, starting transfers between devices, exchange(): lax.all_to_all(value.reshape(blocks, slot_rows, -1), 'seq', split_axis=0,...  32.1 us
  transfers between devices with their start and end apart: 56, of which 20 were waited for; matrix products, arithmetic and copies ran while one was open for 15% of the time, Pallas kernels for 42%

profile of v5, /device:TPU:0, one launch (start us, length us, event | category | flops | bytes accessed | tf_op | source)
XLA Modules:
  0.0 616.6 jit_solution(2737313533339436934)
XLA Ops:
  58.7 11.2 %project.1 = (bf16[4,640,768]{2,1,0:T(8,128)(2,1)}, bf16[192,2560]{1,0:T(8,128)(2,1)}, bf16[3,2560,128]{2,1,0:T(8,128)(2,1)}, bf16[3,1024,128]{2,1,0:T(8,128)(2,...) custom-call(s32[4]{0:T(128)} %pad_add_fusion.order, bf16[640,768]{1,0:T(8,128)(2,1)} %bitcast.150, ...), custom_call_target="tpu_custom_call" | custom-call | flops 1000 | bytes 1000 | tf_op jit(solution)/shard_map/project/pallas_call | solution.py:46
  77.5 19.3 %attend.2 = (bf16[192,640]{1,0:T(8,128)(2,1)}, bf16[192,640]{1,0:T(8,128)(2,1)}, bf16[192,640]{1,0:T(8,128)(2,1)}, bf16[192,640]{1,0:T(8,128)(2,1)}, f32[6,8,256]{2,1,0:T(8,128)}) custom-call(s32[4]{0:T(128)} %pad_add_fusion.order, s32[10]{0:T(128)} %compare_convert_fusion.1.need, s32[1,2560]{1,0:T(1,128)} %reshape.216.low, ...), custom_call_target="tpu_custom_call" | custom-call | flops 1000 | bytes 1000 | tf_op jit(solution)/shard_map/attend/pallas_call | solution.py:286
  103.2 14.4 %attend.3 = (bf16[192,640]{1,0:T(8,128)(2,1)}, bf16[192,640]{1,0:T(8,128)(2,1)}, bf16[192,640]{1,0:T(8,128)(2,1)}, bf16[192,640]{1,0:T(8,128)(2,1)}, f32[4,8,256]{2,1,0:T(8,128)}) custom-call(s32[4]{0:T(128)} %pad_add_fusion.order, s32[10]{0:T(128)} %compare_convert_fusion.1.need, s32[1,2560]{1,0:T(1,128)} %reshape.216.low, ...), custom_call_target="tpu_custom_call" | custom-call | flops 1000 | bytes 1000 | tf_op jit(solution)/shard_map/attend/pallas_call | solution.py:286
  120.5 7.0 %collective-permute-done.9.o1 = bf16[192,640]{1,0:T(8,128)(2,1)S(1)} collective-permute-done((bf16[192,640]{1,0:T(8,128)(2,1)}, bf16[192,640]{1,0:T(8,128)(2,1)S(1)}, u32[]{:S(2)}, u32[]{:S(2)}) %collective-permute-start.9) | collective-permute-done | bytes 245792 | tf_op jit(solution)/shard_map/ppermute | solution.py:791
  132.0 6.8 %all-to-all-done.2 = bf16[8,128,768]{2,1,0:T(8,128)(2,1)S(1)} async-done(((bf16[8,128,768]{2,1,0:T(8,128)(2,1)}), bf16[8,128,768]{2,1,0:T(8,128)(2,1)S(1)}, u32[]{:S(2)}, u32[]{:S(2)}) %all-to-all-start.2) | async-done | bytes 1572896 | tf_op jit(solution)/shard_map/all_to_all | solution.py:881
  145.4 9.1 %middle.1 = (f32[640,768]{1,0:T(8,128)}, bf16[1280,768]{1,0:T(8,128)(2,1)}, bf16[1280,768]{1,0:T(8,128)(2,1)}) custom-call(bf16[192,640]{1,0:T(8,128)(2,1)} %get-tuple-element.242.o0, bf16[192,640]{1,0:T(8,128)(2,1)} %copy-done.26, bf16[192,640]{1,0:T(8,128)(2,1)} %copy-done.27, bf16[192,640]{1,0:T(8,128)(2,1)} %collective-permute-done.11.o3, ...), custom_call_target="tpu_custom_call" | custom-call | flops 1000 | bytes 1000 | tf_op jit(solution)/shard_map/middle/pallas_call | solution.py:46
  154.5 16.7 %all-to-all-done.3 = bf16[8,96,768]{2,1,0:T(8,128)(2,1)S(1)} async-done(((bf16[8,96,768]{2,1,0:T(8,128)(2,1)}), bf16[8,96,768]{2,1,0:T(8,128)(2,1)S(1)}, u32[]{:S(2)}, u32[]{:S(2)}) %all-to-all-start.3) | async-done | bytes 1179680 | tf_op jit(solution)/shard_map/all_to_all | solution.py:881
  180.9 11.3 %convolution_convert_fusion.1.da = bf16[1280,3072]{1,0:T(8,128)(2,1)} fusion(bf16[1280,768]{1,0:T(8,128)(2,1)} %bitcast.165, bf16[2,3072,768]{2,1,0:T(8,128)(2,1)} %all-gather.4.cloned.1.call-done), kind=kOutput, calls=%fused_computation.1 | convolution fusion | flops 6043729920 | bytes 14548992 | tf_op jit(solution)/shard_map/dot_general | solution.py:28
  213.4 10.7 %convolution_convert_fusion.da = bf16[1280,3072]{1,0:T(8,128)(2,1)} fusion(bf16[1280,768]{1,0:T(8,128)(2,1)S(1)} %bitcast.163, bf16[2,3072,768]{2,1,0:T(8,128)(2,1)} %all-gather.4.cloned.1.call-done), kind=kOutput, calls=%fused_computation | convolution fusion | flops 6043729920 | bytes 14548992 | tf_op jit(solution)/shard_map/dot_general | solution.py:28
  229.7 46.3 %expert.2 = (bf16[192,3072]{1,0:T(8,128)(2,1)}, bf16[192,3072]{1,0:T(8,128)(2,1)}, bf16[192,3072]{1,0:T(8,128)(2,1)}, bf16[192,3072]{1,0:T(8,128)(2,1)}, bf16[30...) custom-call(s32[2]{0:T(128)} %get-tuple-element.448.mine, ...), custom_call_target="tpu_custom_call" | custom-call | flops 60397977600 | bytes 50331648 | tf_op jit(solution)/shard_map/expert/pallas_call | solution.py:745
  285.1 46.9 %expert.3 = (bf16[192,3072]{1,0:T(8,128)(2,1)}, bf16[192,3072]{1,0:T(8,128)(2,1)}, bf16[192,3072]{1,0:T(8,128)(2,1)}, bf16[192,3072]{1,0:T(8,128)(2,1)}, bf16[30...) custom-call(s32[2]{0:T(128)} %get-tuple-element.447.mine, ...), custom_call_target="tpu_custom_call" | custom-call | flops 60397977600 | bytes 50331648 | tf_op jit(solution)/shard_map/expert/pallas_call | solution.py:745
  342.0 10.9 %fusion.3 = bf16[1280,768]{1,0:T(8,128)(2,1)} fusion(bf16[1280,3072]{1,0:T(8,128)(2,1)} %get-tuple-element.298, bf16[2,3072,768]{2,1,0:T(8,128)(2,1)} %all-gather.4.cloned.1.call-done), kind=kOutput, calls=%fused_computation.12 | convolution fusion | flops 6040780800 | bytes 14548992 | tf_op jit(solution)/shard_map/dot_general | solution.py:28
  353.0 12.2 %fusion.2 = bf16[1280,768]{1,0:T(8,128)(2,1)} fusion(bf16[1280,3072]{1,0:T(8,128)(2,1)} %get-tuple-element.299, bf16[2,3072,768]{2,1,0:T(8,128)(2,1)} %all-gather.4.cloned.1.call-done), kind=kOutput, calls=%fused_computation.11 | convolution fusion | flops 6040780800 | bytes 14548992 | tf_op jit(solution)/shard_map/dot_general | solution.py:28
  372.7 14.3 %all-to-all-done.7 = bf16[8,160,768]{2,1,0:T(8,128)(2,1)} async-done(((bf16[8,160,768]{2,1,0:T(8,128)(2,1)}), bf16[8,160,768]{2,1,0:T(8,128)(2,1)}, u32[]{:S(2)}, u32[]{:S(2)}) %all-to-all-start.7) | async-done | bytes 1966112 | tf_op jit(solution)/shard_map/all_to_all | solution.py:857
  387.0 11.5 %return_rows.1 = (f32[640,768]{1,0:T(8,128)}, f32[1,768]{1,0:T(1,128)}, bf16[192,640]{1,0:T(8,128)(2,1)}, bf16[192,640]{1,0:T(8,128)(2,1)}, bf16[192,640]{1,0:T(...) custom-call(bf16[1280,768]{1,0:T(8,128)(2,1)} %bitcast.154, ...), custom_call_target="tpu_custom_call" | custom-call | flops 1000 | bytes 1000 | tf_op jit(solution)/shard_map/return_rows/pallas_call | solution.py:46
  416.5 21.6 %attend_back.3 = (bf16[192,1024]{1,0:T(8,128)(2,1)}, bf16[3,128,1024]{2,1,0:T(8,128)(2,1)}, f32[3,128,1024]{2,1,0:T(8,128)}, f32[3,1280,256]{2,1,0:T(8,128)}) custom-call(s32[5]{0:T(128)} %concatenate.40.order, s32[10]{0:T(128)} %compare_convert_fusion.1.need, s32[1,2560]{1,0:T(1,128)} %reshape.216.low, bf16[192,2560]{1,0:T(8,128)(2,1)} %get-tuple-element.214.qt, ...), custom_call_target="tpu_custom_call" | custom-call | flops 1000 | bytes 1000 | tf_op jit(solution)/shard_map/attend_back/pallas_call | solution.py:427
  440.9 16.0 %attend_back.4 = (bf16[64,1536]{1,0:T(8,128)(2,1)}, f32[1,128,2560]{2,1,0:T(8,128)}, f32[1,8,512]{2,1,0:T(8,128)}) custom-call(s32[5]{0:T(128)} %concatenate.49.order, s32[10]{0:T(128)} %compare_convert_fusion.1.need, s32[1,2560]{1,0:T(1,128)} %reshape.216.low, bf16[192,2560]{1,0:T(8,128)(2,1)} %get-tuple-element.214.qt, ...), custom_call_target="tpu_custom_call" | custom-call | flops 1000 | bytes 1000 | tf_op jit(solution)/shard_map/attend_back/pallas_call | solution.py:427
  460.7 7.2 %all-to-all-start.9 = ((bf16[8,160,768]{2,1,0:T(8,128)(2,1)}), bf16[8,160,768]{2,1,0:T(8,128)(2,1)}, u32[]{:S(2)}, u32[]{:S(2)}) async-start(bf16[8,160,768]{2,1,0:T(8,128)(2,1)} %bitcast.162), calls=%async_computation.11 | async-start | bytes 3932160 | tf_op jit(solution)/shard_map/all_to_all | solution.py:857
  473.0 28.9 %attend_back.5 = (bf16[128,1536]{1,0:T(8,128)(2,1)}, f32[2,128,2560]{2,1,0:T(8,128)}, f32[2,8,512]{2,1,0:T(8,128)}) custom-call(s32[5]{0:T(128)} %concatenate.40.order, s32[10]{0:T(128)} %compare_convert_fusion.1.need, s32[1,2560]{1,0:T(1,128)} %reshape.216.low, bf16[192,2560]{1,0:T(8,128)(2,1)} %get-tuple-element.214.qt, ...), custom_call_target="tpu_custom_call" | custom-call | flops 1000 | bytes 1000 | tf_op jit(solution)/shard_map/attend_back/pallas_call | solution.py:427
  502.0 10.9 %settle.1 = (bf16[576,640]{1,0:T(8,128)(2,1)}, bf16[576,640]{1,0:T(8,128)(2,1)}, bf16[576,640]{1,0:T(8,128)(2,1)}, bf16[576,640]{1,0:T(8,128)(2,1)}, bf16[4,624,192]{2,1,0:T(8,128)(2,1)}) custom-call(s32[4]{0:T(128)} %pad_add_fusion.order, bf16[192,1024]{1,0:T(8,128)(2,1)} %get-tuple-element.317.dq0, bf16[128,1536]{1,0:T(8,128)(2,1)} %get-tuple-element.337.dq1, ...), custom_call_target="tpu_custom_call" | custom-call | flops 1000 | bytes 1000 | tf_op jit(solution)/shard_map/settle/pallas_call | solution.py:46
  523.6 23.7 %collective-permute-done.32 = bf16[192,768]{1,0:T(8,128)(2,1)S(1)} collective-permute-done((bf16[192,768]{1,0:T(8,128)(2,1)S(1)}, bf16[192,768]{1,0:T(8,128)(2,1)S(1)}, u32[]{:S(2)}, u32[]{:S(2)}) %collective-permute-start.32) | collective-permute-done | bytes 294944 | tf_op jit(solution)/shard_map/ppermute | solution.py:791
  572.0 6.6 %finish.1 = bf16[640,768]{1,0:T(8,128)(2,1)} custom-call(bf16[1280,768]{1,0:T(8,128)(2,1)} %bitcast.153, bf16[1280,768]{1,0:T(8,128)(2,1)} %bitcast.53.z1, s32[640,2]{1,0:T(8,128)} %bitcast.156, f32[640,768]{1,0:T(8,128)} %get-tuple-element.304.y), custom_call_target="tpu_custom_call" | custom-call | flops 1000 | bytes 1000 | tf_op jit(solution)/shard_map/finish/pallas_call | solution.py:46
  581.4 8.7 %tail.1 = f32[640,768]{1,0:T(8,128)} custom-call(s32[4]{0:T(128)} %pad_add_fusion.order, bf16[576,640]{1,0:T(8,128)(2,1)} %get-tuple-element.355.refs_0_, bf16[576,640]{1,0:T(8,128)(2,1)} %collective-permute-done.33.refs_1_, bf16[576,640]{1,0:T(8,128)(2,1)} %collective-permute-done.34.refs_2_, bf16[576,640]{1,0:T(8,128)(2,1)} %copy-done.28, ...), custom_call_target="tpu_custom_call" | custom-call | flops 1000 | bytes 1000 | tf_op jit(solution)/shard_map/tail/pallas_call | solution.py:46
  590.1 7.5 %all-to-all-done.11 = bf16[8,4,78,192]{3,1,2,0:T(4,128)(2,1)S(1)} async-done(((bf16[8,4,78,192]{3,1,2,0:T(4,128)(2,1)}), bf16[8,4,78,192]{3,1,2,0:T(4,128)(2,1)S(1)}, u32[]{:S(2)}, u32[]{:S(2)}) %all-to-all-start.11) | async-done | bytes 958496 | tf_op jit(solution)/shard_map/all_to_all | solution.py:1049
  (307 shorter events, 219.4 us)
Async XLA Ops:
  7.2 41.9 %collective-permute-start = (bf16[640,768]{1,0:T(8,128)(2,1)}, bf16[640,768]{1,0:T(8,128)(2,1)}, u32[]{:S(2)}, u32[]{:S(2)}) collective-permute-start(bf16[640,768]{1,0:T(8,128)(2,1)} %bitcast.148), channel_id=1, source_target_pairs={{0,16},{8,24},{16,0},{24,8},{1,17},{9,25},{17,1},{25,9},{2,18},{10... | collective-permute-start | bytes 2949128 | tf_op jit(solution)/shard_map/ppermute | solution.py:791
  10.2 38.8 %collective-permute-start.1 = (bf16[640,768]{1,0:T(8,128)(2,1)}, bf16[640,768]{1,0:T(8,128)(2,1)}, u32[]{:S(2)}, u32[]{:S(2)}) collective-permute-start(bf16[640,768]{1,0:T(8,128)(2,1)} %bitcast.149), channel_id=1, source_target_pairs={{0,8},{8,0},{16,24},{24,16},{1,9},{9,1},{17,25},{25,17},{2,10},{10... | collective-permute-start | bytes 2949128 | tf_op jit(solution)/shard_map/ppermute | solution.py:791
  27.3 153.6 %all-gather.4.cloned.1.call-start = ((), (), s32[]{:S(2)}) async-start(), calls=%async_computation.14 | async-start | bytes 11796480 | tf_op jit(solution)/shard_map/all_gather | solution.py:892
  52.7 44.1 %all-to-all-start.1 = ((bf16[8,64,768]{2,1,0:T(8,128)(2,1)}), bf16[8,64,768]{2,1,0:T(8,128)(2,1)S(1)}, u32[]{:S(2)}, u32[]{:S(2)}) async-start(bf16[8,64,768]{2,1,0:T(8,128)(2,1)} %bitcast.15), calls=%async_computation.1 | async-start | bytes 1572864 | tf_op jit(solution)/shard_map/all_to_all | solution.py:881
  97.8 41.1 %all-to-all-start.2 = ((bf16[8,128,768]{2,1,0:T(8,128)(2,1)}), bf16[8,128,768]{2,1,0:T(8,128)(2,1)S(1)}, u32[]{:S(2)}, u32[]{:S(2)}) async-start(bf16[8,128,768]{2,1,0:T(8,128)(2,1)} %bitcast.171), calls=%async_computation.2 | async-start | bytes 3145728 | tf_op jit(solution)/shard_map/all_to_all | solution.py:881
  102.1 127.5 %all-gather.8.cloned.1.call-start = ((), (), s32[]{:S(2)}) async-start(), calls=%async_computation.16 | async-start | bytes 11796480 | tf_op jit(solution)/shard_map/all_gather | solution.py:910
  138.9 32.4 %all-to-all-start.3 = ((bf16[8,96,768]{2,1,0:T(8,128)(2,1)}), bf16[8,96,768]{2,1,0:T(8,128)(2,1)S(1)}, u32[]{:S(2)}, u32[]{:S(2)}) async-start(bf16[8,96,768]{2,1,0:T(8,128)(2,1)} %send_noted.1), calls=%async_computation.3 | async-start | bytes 2359296 | tf_op jit(solution)/shard_map/all_to_all | solution.py:881
  142.5 133.5 %all-gather.6.cloned.1.call-start = ((), (), s32[]{:S(2)}) async-start(), calls=%async_computation.15 | async-start | bytes 4423680 | tf_op jit(solution)/shard_map/all_gather | solution.py:895
  172.8 53.0 %all-to-all-start.5 = ((bf16[8,160,768]{2,1,0:T(8,128)(2,1)}), bf16[8,160,768]{2,1,0:T(8,128)(2,1)}, u32[]{:S(2)}, u32[]{:S(2)}) async-start(bf16[8,160,768]{2,1,0:T(8,128)(2,1)} %bitcast.161), calls=%async_computation.5 | async-start | bytes 3932160 | tf_op jit(solution)/shard_map/all_to_all | solution.py:857
  225.8 50.2 %all-to-all-start.4 = ((bf16[8,160,768]{2,1,0:T(8,128)(2,1)}), bf16[8,160,768]{2,1,0:T(8,128)(2,1)S(1)}, u32[]{:S(2)}, u32[]{:S(2)}) async-start(bf16[8,160,768]{2,1,0:T(8,128)(2,1)} %bitcast.25), calls=%async_computation.4 | async-start | bytes 3932160 | tf_op jit(solution)/shard_map/all_to_all | solution.py:857
  229.4 105.4 %reduce-scatter.3.cloned.1.call-start = ((), (), s32[]{:S(2)}) async-start(), calls=%async_computation.17 | async-start | bytes 5898240 | tf_op jit(solution)/shard_map/reduce_scatter | solution.py:960
  278.6 56.1 %all-to-all-start.6 = ((bf16[8,160,768]{2,1,0:T(8,128)(2,1)}), bf16[8,160,768]{2,1,0:T(8,128)(2,1)S(1)}, u32[]{:S(2)}, u32[]{:S(2)}) async-start(bf16[8,160,768]{2,1,0:T(8,128)(2,1)} %bitcast.170), calls=%async_computation.6 | async-start | bytes 3932160 | tf_op jit(solution)/shard_map/all_to_all | solution.py:857
  285.0 47.0 %collective-permute-start.20 = (bf16[192,3072]{1,0:T(8,128)(2,1)}, bf16[192,3072]{1,0:T(8,128)(2,1)}, u32[]{:S(2)}, u32[]{:S(2)}) collective-permute-start(bf16[192,3072]{1,0:T(8,128)(2,1)} %get-tuple-element.294), channel_id=1, source_target_pairs={{0,8},{8,0},{16,24},{24,16},{1,9},{9,1},{17,25},{25,17},{2,10},{10... | collective-permute-start | bytes 3538952 | tf_op jit(solution)/shard_map/ppermute | solution.py:791
  334.8 52.2 %all-to-all-start.7 = ((bf16[8,160,768]{2,1,0:T(8,128)(2,1)}), bf16[8,160,768]{2,1,0:T(8,128)(2,1)}, u32[]{:S(2)}, u32[]{:S(2)}) async-start(bf16[8,160,768]{2,1,0:T(8,128)(2,1)} %bitcast.169), calls=%async_computation.8 | async-start | bytes 3932160 | tf_op jit(solution)/shard_map/all_to_all | solution.py:857
  341.0 161.0 %reduce-scatter.5.cloned.1.call-start = ((), (), s32[]{:S(2)}) async-start(), calls=%async_computation.18 | async-start | bytes 5898240 | tf_op jit(solution)/shard_map/reduce_scatter | solution.py:969
  398.6 62.2 %all-to-all-start.8 = ((bf16[8,160,768]{2,1,0:T(8,128)(2,1)}), bf16[8,160,768]{2,1,0:T(8,128)(2,1)S(1)}, u32[]{:S(2)}, u32[]{:S(2)}) async-start(bf16[8,160,768]{2,1,0:T(8,128)(2,1)} %bitcast.167), calls=%async_computation.10 | async-start | bytes 3932160 | tf_op jit(solution)/shard_map/all_to_all | solution.py:857
  460.7 53.0 %all-to-all-start.9 = ((bf16[8,160,768]{2,1,0:T(8,128)(2,1)}), bf16[8,160,768]{2,1,0:T(8,128)(2,1)}, u32[]{:S(2)}, u32[]{:S(2)}) async-start(bf16[8,160,768]{2,1,0:T(8,128)(2,1)} %bitcast.162), calls=%async_computation.11 | async-start | bytes 3932160 | tf_op jit(solution)/shard_map/all_to_all | solution.py:857
  468.0 34.0 %collective-permute-start.31 = (bf16[192,3072]{1,0:T(8,128)(2,1)S(1)}, bf16[192,3072]{1,0:T(8,128)(2,1)}, u32[]{:S(2)}, u32[]{:S(2)}) collective-permute-start(bf16[192,3072]{1,0:T(8,128)(2,1)S(1)} %copy-done.19), channel_id=1, source_target_pairs={{0,16},{8,24},{16,0},{24,8},{1,17},{9,25},{17,1},{25,9},{2,18},{10... | collective-permute-start | bytes 3538952 | tf_op jit(solution)/shard_map/ppermute | solution.py:791
  516.1 36.3 %all-to-all-start.10 = ((bf16[32,78,192]{2,1,0:T(8,128)(2,1)}), bf16[32,78,192]{2,1,0:T(8,128)(2,1)S(1)}, u32[]{:S(2)}, u32[]{:S(2)}) async-start(bf16[32,78,192]{2,1,0:T(8,128)(2,1)} %reshape.234), calls=%async_computation.12 | async-start | bytes 2621440 | tf_op jit(solution)/shard_map/all_to_all | solution.py:994
  519.2 40.1 %collective-permute-start.37 = (bf16[192,3072]{1,0:T(8,128)(2,1)}, bf16[192,3072]{1,0:T(8,128)(2,1)}, u32[]{:S(2)}, u32[]{:S(2)}) collective-permute-start(bf16[192,3072]{1,0:T(8,128)(2,1)} %get-tuple-element.375), channel_id=1, source_target_pairs={{0,8},{8,0},{16,24},{24,16},{1,9},{9,1},{17,25},{25,17},{2,10},{10... | collective-permute-start | bytes 3538952 | tf_op jit(solution)/shard_map/ppermute | solution.py:791
  519.5 33.1 %collective-permute-start.33 = (bf16[576,640]{1,0:T(8,128)(2,1)}, bf16[576,640]{1,0:T(8,128)(2,1)}, u32[]{:S(2)}, u32[]{:S(2)}) collective-permute-start(bf16[576,640]{1,0:T(8,128)(2,1)} %get-tuple-element.352), channel_id=1, source_target_pairs={{0,16},{8,24},{16,0},{24,8},{1,17},{9,25},{17,1},{25,9},{2,18},{10... | collective-permute-start | bytes 2211848 | tf_op jit(solution)/shard_map/ppermute | solution.py:791
  523.5 38.2 %collective-permute-start.38 = (bf16[192,3072]{1,0:T(8,128)(2,1)}, bf16[192,3072]{1,0:T(8,128)(2,1)}, u32[]{:S(2)}, u32[]{:S(2)}) collective-permute-start(bf16[192,3072]{1,0:T(8,128)(2,1)} %get-tuple-element.378), channel_id=1, source_target_pairs={{0,8},{8,0},{16,24},{24,16},{1,9},{9,1},{17,25},{25,17},{2,10},{10... | collective-permute-start | bytes 3538952 | tf_op jit(solution)/shard_map/ppermute | solution.py:791
  554.1 43.5 %all-to-all-start.11 = ((bf16[8,4,78,192]{3,1,2,0:T(4,128)(2,1)}), bf16[8,4,78,192]{3,1,2,0:T(4,128)(2,1)S(1)}, u32[]{:S(2)}, u32[]{:S(2)}) async-start(bf16[8,4,78,192]{3,1,2,0:T(4,128)(2,1)} %broadcast_in_dim.93), calls=%async_computation.13 | async-start | bytes 2555904 | tf_op jit(solution)/shard_map/all_to_all | solution.py:1049
  563.8 38.8 %collective-permute-start.36 = (bf16[192,768]{1,0:T(8,128)(2,1)S(1)}, bf16[192,768]{1,0:T(8,128)(2,1)S(1)}, u32[]{:S(2)}, u32[]{:S(2)}) collective-permute-start(bf16[192,768]{1,0:T(8,128)(2,1)S(1)} %add_convert_fusion.3), channel_id=1, source_target_pairs={{0,4},{1,5},{2,6},{3,7},{4,0},{5,1},{6,2},{7,3},{8,12},{9,13},{10,... | collective-permute-start | bytes 884744 | tf_op jit(solution)/shard_map/ppermute | solution.py:791
  (80 other events, 1227.9 us)
Sparse Core Ops, SparseCore 0:
  52.8 71.4 all-gather.3
  139.0 62.3 all-gather.7
  202.9 30.8 all-gather.5
  276.2 49.4 reduce-scatter.2
  344.8 51.1 reduce-scatter.4

commit v6 on v5

--- a/solution.py
+++ b/solution.py
@@ -843,7 +843,7 @@
     code = (pair_routes % local) * slots + (pair_routes // local) * slot_rows + local_rank
     code_t = code.reshape(top_count, rows)
     code = code_t.T
-    one, two, three = slot_rows * 3 // 10, slot_rows * 7 // 10, slot_rows // 2
+    one, two, three = slot_rows * 3 // 10, slot_rows * 8 // 10, slot_rows // 2
     counts = (one, two - one, slot_rows - two + three, slot_rows - three)
     held = ((0, 0, one, 0, 0), (0, one, two, 1, 0), (0, two, slot_rows, 2, 0), (1, 0, three, 2, slot_rows - two))
     send_place = jnp.zeros_like(local_rank)

time: 624 us -> 621 us (level)
  transfers between devices with their start and end apart: 56 -> 56, of which waited for: 20 -> 20; matrix products, arithmetic and copies ran while one was open for 15% -> 15% of each run, Pallas kernels for 42% -> 43%
where the time goes in v6:
time: 621 us; the launch traced here: 613 us
  Pallas kernels  265 us (43%)
  waiting for transfers between devices  122 us (20%)
  starting transfers between devices  107 us (17%)
  matrix products  45.2 us (7%)
  other arithmetic  30.5 us (5%)
  local copies, waits for them, and re-layouts  26.6 us (4%)
  between operations  17 us (3%)
    pallas_call x2, Pallas kernels, expert(): pl.pallas_call(expert_kernel, grid=(inner // block,), in_specs=[SMEM, who...  93.4 us
    pallas_call x10, Pallas kernels, once(): pl.pallas_call(kernel, grid=(1,), in_specs=[SMEM if value.ndim == 1 else...  71.5 us
    ppermute x37, waiting for transfers between devices, swap(): lax.ppermute(value, axis, [(i, i ^ mask) for i in range(lax.axis_size(axi...  70.4 us
    pallas_call x3, Pallas kernels, attention_backward(): pl.pallas_call(kernel, grid=(steps,), in_specs=specs, out_specs=out_specs...  66.7 us
    dot_general x5, matrix products, dot(): lax.dot_general(a, b, (dims, ((), ())), preferred_element_type=single)  45.2 us
    ppermute x37, starting transfers between devices, swap(): lax.ppermute(value, axis, [(i, i ^ mask) for i in range(lax.axis_size(axi...  39.3 us
    pallas_call x2, Pallas kernels, attention_forward(): pl.pallas_call(functools.partial(forward_kernel, first), grid=(steps,), i...  33.7 us
    all_to_all x6, starting transfers between devices, exchange(): lax.all_to_all(value.reshape(blocks, slot_rows, -1), 'seq', split_axis=0,...  31.8 us
  transfers between devices with their start and end apart: 56, of which 20 were waited for; matrix products, arithmetic and copies ran while one was open for 15% of the time, Pallas kernels for 43%

profile of v6, /device:TPU:0, one launch (start us, length us, event | category | flops | bytes accessed | tf_op | source)
XLA Modules:
  0.0 613.3 jit_solution(3608054400358473197)
XLA Ops:
  58.2 11.2 %project.1 = (bf16[4,640,768]{2,1,0:T(8,128)(2,1)}, bf16[192,2560]{1,0:T(8,128)(2,1)}, bf16[3,2560,128]{2,1,0:T(8,128)(2,1)}, bf16[3,1024,128]{2,1,0:T(8,128)(2,...) custom-call(s32[4]{0:T(128)} %pad_add_fusion.order, bf16[640,768]{1,0:T(8,128)(2,1)} %bitcast.150, ...), custom_call_target="tpu_custom_call" | custom-call | flops 1000 | bytes 1000 | tf_op jit(solution)/shard_map/project/pallas_call | solution.py:46
  77.1 19.4 %attend.2 = (bf16[192,640]{1,0:T(8,128)(2,1)}, bf16[192,640]{1,0:T(8,128)(2,1)}, bf16[192,640]{1,0:T(8,128)(2,1)}, bf16[192,640]{1,0:T(8,128)(2,1)}, f32[6,8,256]{2,1,0:T(8,128)}) custom-call(s32[4]{0:T(128)} %pad_add_fusion.order, s32[10]{0:T(128)} %compare_convert_fusion.1.need, s32[1,2560]{1,0:T(1,128)} %reshape.216.low, ...), custom_call_target="tpu_custom_call" | custom-call | flops 1000 | bytes 1000 | tf_op jit(solution)/shard_map/attend/pallas_call | solution.py:286
  103.5 14.3 %attend.3 = (bf16[192,640]{1,0:T(8,128)(2,1)}, bf16[192,640]{1,0:T(8,128)(2,1)}, bf16[192,640]{1,0:T(8,128)(2,1)}, bf16[192,640]{1,0:T(8,128)(2,1)}, f32[4,8,256]{2,1,0:T(8,128)}) custom-call(s32[4]{0:T(128)} %pad_add_fusion.order, s32[10]{0:T(128)} %compare_convert_fusion.1.need, s32[1,2560]{1,0:T(1,128)} %reshape.216.low, ...), custom_call_target="tpu_custom_call" | custom-call | flops 1000 | bytes 1000 | tf_op jit(solution)/shard_map/attend/pallas_call | solution.py:286
  120.9 6.9 %collective-permute-done.9.o1 = bf16[192,640]{1,0:T(8,128)(2,1)S(1)} collective-permute-done((bf16[192,640]{1,0:T(8,128)(2,1)}, bf16[192,640]{1,0:T(8,128)(2,1)S(1)}, u32[]{:S(2)}, u32[]{:S(2)}) %collective-permute-start.9) | collective-permute-done | bytes 245792 | tf_op jit(solution)/shard_map/ppermute | solution.py:791
  143.0 9.0 %middle.1 = (f32[640,768]{1,0:T(8,128)}, bf16[1280,768]{1,0:T(8,128)(2,1)}, bf16[1280,768]{1,0:T(8,128)(2,1)}) custom-call(bf16[192,640]{1,0:T(8,128)(2,1)} %get-tuple-element.242.o0, bf16[192,640]{1,0:T(8,128)(2,1)} %copy-done.28, bf16[192,640]{1,0:T(8,128)(2,1)} %copy-done.29, bf16[192,640]{1,0:T(8,128)(2,1)} %copy-done.30, bf16[192,768]{1,0:T(8,128)(2,1)} %w0.1, ...), custom_call_target="tpu_custom_call" | custom-call | flops 1000 | bytes 1000 | tf_op jit(solution)/shard_map/middle/pallas_call | solution.py:46
  152.1 16.1 %all-to-all-done.3 = bf16[8,96,768]{2,1,0:T(8,128)(2,1)S(1)} async-done(((bf16[8,96,768]{2,1,0:T(8,128)(2,1)}), bf16[8,96,768]{2,1,0:T(8,128)(2,1)S(1)}, u32[]{:S(2)}, u32[]{:S(2)}) %all-to-all-start.3) | async-done | bytes 1179680 | tf_op jit(solution)/shard_map/all_to_all | solution.py:881
  177.8 11.3 %convolution_convert_fusion.1.da = bf16[1280,3072]{1,0:T(8,128)(2,1)} fusion(bf16[1280,768]{1,0:T(8,128)(2,1)} %bitcast.165, bf16[2,3072,768]{2,1,0:T(8,128)(2,1)} %all-gather.4.cloned.1.call-done), kind=kOutput, calls=%fused_computation.1 | convolution fusion | flops 6043729920 | bytes 14548992 | tf_op jit(solution)/shard_map/dot_general | solution.py:28
  210.4 10.8 %convolution_convert_fusion.da = bf16[1280,3072]{1,0:T(8,128)(2,1)} fusion(bf16[1280,768]{1,0:T(8,128)(2,1)S(1)} %bitcast.163, bf16[2,3072,768]{2,1,0:T(8,128)(2,1)} %all-gather.4.cloned.1.call-done), kind=kOutput, calls=%fused_computation | convolution fusion | flops 6043729920 | bytes 14548992 | tf_op jit(solution)/shard_map/dot_general | solution.py:28
  226.8 46.3 %expert.2 = (bf16[192,3072]{1,0:T(8,128)(2,1)}, bf16[192,3072]{1,0:T(8,128)(2,1)}, bf16[192,3072]{1,0:T(8,128)(2,1)}, bf16[192,3072]{1,0:T(8,128)(2,1)}, bf16[30...) custom-call(s32[2]{0:T(128)} %get-tuple-element.448.mine, ...), custom_call_target="tpu_custom_call" | custom-call | flops 60397977600 | bytes 50331648 | tf_op jit(solution)/shard_map/expert/pallas_call | solution.py:745
  281.9 47.1 %expert.3 = (bf16[192,3072]{1,0:T(8,128)(2,1)}, bf16[192,3072]{1,0:T(8,128)(2,1)}, bf16[192,3072]{1,0:T(8,128)(2,1)}, bf16[192,3072]{1,0:T(8,128)(2,1)}, bf16[30...) custom-call(s32[2]{0:T(128)} %get-tuple-element.447.mine, ...), custom_call_target="tpu_custom_call" | custom-call | flops 60397977600 | bytes 50331648 | tf_op jit(solution)/shard_map/expert/pallas_call | solution.py:745
  339.3 10.9 %fusion.3 = bf16[1280,768]{1,0:T(8,128)(2,1)} fusion(bf16[1280,3072]{1,0:T(8,128)(2,1)} %get-tuple-element.298, bf16[2,3072,768]{2,1,0:T(8,128)(2,1)} %all-gather.4.cloned.1.call-done), kind=kOutput, calls=%fused_computation.12 | convolution fusion | flops 6040780800 | bytes 14548992 | tf_op jit(solution)/shard_map/dot_general | solution.py:28
  350.2 12.1 %fusion.2 = bf16[1280,768]{1,0:T(8,128)(2,1)} fusion(bf16[1280,3072]{1,0:T(8,128)(2,1)} %get-tuple-element.299, bf16[2,3072,768]{2,1,0:T(8,128)(2,1)} %all-gather.4.cloned.1.call-done), kind=kOutput, calls=%fused_computation.11 | convolution fusion | flops 6040780800 | bytes 14548992 | tf_op jit(solution)/shard_map/dot_general | solution.py:28
  370.1 13.9 %all-to-all-done.7 = bf16[8,160,768]{2,1,0:T(8,128)(2,1)} async-done(((bf16[8,160,768]{2,1,0:T(8,128)(2,1)}), bf16[8,160,768]{2,1,0:T(8,128)(2,1)}, u32[]{:S(2)}, u32[]{:S(2)}) %all-to-all-start.7) | async-done | bytes 1966112 | tf_op jit(solution)/shard_map/all_to_all | solution.py:857
  384.0 11.5 %return_rows.1 = (f32[640,768]{1,0:T(8,128)}, f32[1,768]{1,0:T(1,128)}, bf16[192,640]{1,0:T(8,128)(2,1)}, bf16[192,640]{1,0:T(8,128)(2,1)}, bf16[192,640]{1,0:T(...) custom-call(bf16[1280,768]{1,0:T(8,128)(2,1)} %bitcast.154, ...), custom_call_target="tpu_custom_call" | custom-call | flops 1000 | bytes 1000 | tf_op jit(solution)/shard_map/return_rows/pallas_call | solution.py:46
  402.7 6.3 %collective-permute-done.23.d1 = bf16[192,640]{1,0:T(8,128)(2,1)S(1)} collective-permute-done((bf16[192,640]{1,0:T(8,128)(2,1)}, bf16[192,640]{1,0:T(8,128)(2,1)S(1)}, u32[]{:S(2)}, u32[]{:S(2)}) %collective-permute-start.23) | collective-permute-done | bytes 245792 | tf_op jit(solution)/shard_map/ppermute | solution.py:791
  413.2 21.6 %attend_back.3 = (bf16[192,1024]{1,0:T(8,128)(2,1)}, bf16[3,128,1024]{2,1,0:T(8,128)(2,1)}, f32[3,128,1024]{2,1,0:T(8,128)}, f32[3,1280,256]{2,1,0:T(8,128)}) custom-call(s32[5]{0:T(128)} %concatenate.40.order, s32[10]{0:T(128)} %compare_convert_fusion.1.need, s32[1,2560]{1,0:T(1,128)} %reshape.216.low, bf16[192,2560]{1,0:T(8,128)(2,1)} %get-tuple-element.214.qt, ...), custom_call_target="tpu_custom_call" | custom-call | flops 1000 | bytes 1000 | tf_op jit(solution)/shard_map/attend_back/pallas_call | solution.py:427
  437.8 16.0 %attend_back.4 = (bf16[64,1536]{1,0:T(8,128)(2,1)}, f32[1,128,2560]{2,1,0:T(8,128)}, f32[1,8,512]{2,1,0:T(8,128)}) custom-call(s32[5]{0:T(128)} %concatenate.49.order, s32[10]{0:T(128)} %compare_convert_fusion.1.need, s32[1,2560]{1,0:T(1,128)} %reshape.216.low, bf16[192,2560]{1,0:T(8,128)(2,1)} %get-tuple-element.214.qt, ...), custom_call_target="tpu_custom_call" | custom-call | flops 1000 | bytes 1000 | tf_op jit(solution)/shard_map/attend_back/pallas_call | solution.py:427
  457.3 7.3 %all-to-all-start.9 = ((bf16[8,160,768]{2,1,0:T(8,128)(2,1)}), bf16[8,160,768]{2,1,0:T(8,128)(2,1)}, u32[]{:S(2)}, u32[]{:S(2)}) async-start(bf16[8,160,768]{2,1,0:T(8,128)(2,1)} %bitcast.162), calls=%async_computation.11 | async-start | bytes 3932160 | tf_op jit(solution)/shard_map/all_to_all | solution.py:857
  469.8 29.0 %attend_back.5 = (bf16[128,1536]{1,0:T(8,128)(2,1)}, f32[2,128,2560]{2,1,0:T(8,128)}, f32[2,8,512]{2,1,0:T(8,128)}) custom-call(s32[5]{0:T(128)} %concatenate.40.order, s32[10]{0:T(128)} %compare_convert_fusion.1.need, s32[1,2560]{1,0:T(1,128)} %reshape.216.low, bf16[192,2560]{1,0:T(8,128)(2,1)} %get-tuple-element.214.qt, ...), custom_call_target="tpu_custom_call" | custom-call | flops 1000 | bytes 1000 | tf_op jit(solution)/shard_map/attend_back/pallas_call | solution.py:427
  499.0 10.9 %settle.1 = (bf16[576,640]{1,0:T(8,128)(2,1)}, bf16[576,640]{1,0:T(8,128)(2,1)}, bf16[576,640]{1,0:T(8,128)(2,1)}, bf16[576,640]{1,0:T(8,128)(2,1)}, bf16[4,624,192]{2,1,0:T(8,128)(2,1)}) custom-call(s32[4]{0:T(128)} %pad_add_fusion.order, bf16[192,1024]{1,0:T(8,128)(2,1)} %get-tuple-element.317.dq0, bf16[128,1536]{1,0:T(8,128)(2,1)} %get-tuple-element.337.dq1, ...), custom_call_target="tpu_custom_call" | custom-call | flops 1000 | bytes 1000 | tf_op jit(solution)/shard_map/settle/pallas_call | solution.py:46
  520.6 23.7 %collective-permute-done.32 = bf16[192,768]{1,0:T(8,128)(2,1)S(1)} collective-permute-done((bf16[192,768]{1,0:T(8,128)(2,1)S(1)}, bf16[192,768]{1,0:T(8,128)(2,1)S(1)}, u32[]{:S(2)}, u32[]{:S(2)}) %collective-permute-start.32) | collective-permute-done | bytes 294944 | tf_op jit(solution)/shard_map/ppermute | solution.py:791
  568.9 6.6 %finish.1 = bf16[640,768]{1,0:T(8,128)(2,1)} custom-call(bf16[1280,768]{1,0:T(8,128)(2,1)} %bitcast.153, bf16[1280,768]{1,0:T(8,128)(2,1)} %bitcast.53.z1, s32[640,2]{1,0:T(8,128)} %bitcast.156, f32[640,768]{1,0:T(8,128)} %get-tuple-element.304.y), custom_call_target="tpu_custom_call" | custom-call | flops 1000 | bytes 1000 | tf_op jit(solution)/shard_map/finish/pallas_call | solution.py:46
  578.3 8.7 %tail.1 = f32[640,768]{1,0:T(8,128)} custom-call(s32[4]{0:T(128)} %pad_add_fusion.order, bf16[576,640]{1,0:T(8,128)(2,1)} %get-tuple-element.355.refs_0_, bf16[576,640]{1,0:T(8,128)(2,1)} %collective-permute-done.33.refs_1_, bf16[576,640]{1,0:T(8,128)(2,1)} %collective-permute-done.34.refs_2_, bf16[576,640]{1,0:T(8,128)(2,1)} %copy-done.31, ...), custom_call_target="tpu_custom_call" | custom-call | flops 1000 | bytes 1000 | tf_op jit(solution)/shard_map/tail/pallas_call | solution.py:46
  587.0 7.5 %all-to-all-done.11 = bf16[8,4,78,192]{3,1,2,0:T(4,128)(2,1)S(1)} async-done(((bf16[8,4,78,192]{3,1,2,0:T(4,128)(2,1)}), bf16[8,4,78,192]{3,1,2,0:T(4,128)(2,1)S(1)}, u32[]{:S(2)}, u32[]{:S(2)}) %all-to-all-start.11) | async-done | bytes 958496 | tf_op jit(solution)/shard_map/all_to_all | solution.py:1049
  (313 shorter events, 217.7 us)
Async XLA Ops:
  7.2 41.7 %collective-permute-start = (bf16[640,768]{1,0:T(8,128)(2,1)}, bf16[640,768]{1,0:T(8,128)(2,1)}, u32[]{:S(2)}, u32[]{:S(2)}) collective-permute-start(bf16[640,768]{1,0:T(8,128)(2,1)} %bitcast.148), channel_id=1, source_target_pairs={{0,16},{8,24},{16,0},{24,8},{1,17},{9,25},{17,1},{25,9},{2,18},{10... | collective-permute-start | bytes 2949128 | tf_op jit(solution)/shard_map/ppermute | solution.py:791
  10.2 38.7 %collective-permute-start.1 = (bf16[640,768]{1,0:T(8,128)(2,1)}, bf16[640,768]{1,0:T(8,128)(2,1)}, u32[]{:S(2)}, u32[]{:S(2)}) collective-permute-start(bf16[640,768]{1,0:T(8,128)(2,1)} %bitcast.149), channel_id=1, source_target_pairs={{0,8},{8,0},{16,24},{24,16},{1,9},{9,1},{17,25},{25,17},{2,10},{10... | collective-permute-start | bytes 2949128 | tf_op jit(solution)/shard_map/ppermute | solution.py:791
  27.3 150.6 %all-gather.4.cloned.1.call-start = ((), (), s32[]{:S(2)}) async-start(), calls=%async_computation.14 | async-start | bytes 11796480 | tf_op jit(solution)/shard_map/all_gather | solution.py:892
  52.0 44.5 %all-to-all-start.1 = ((bf16[8,80,768]{2,1,0:T(8,128)(2,1)}), bf16[8,80,768]{2,1,0:T(8,128)(2,1)S(1)}, u32[]{:S(2)}, u32[]{:S(2)}) async-start(bf16[8,80,768]{2,1,0:T(8,128)(2,1)} %bitcast.15), calls=%async_computation.1 | async-start | bytes 1966080 | tf_op jit(solution)/shard_map/all_to_all | solution.py:881
  97.4 38.2 %all-to-all-start.2 = ((bf16[8,112,768]{2,1,0:T(8,128)(2,1)}), bf16[8,112,768]{2,1,0:T(8,128)(2,1)S(1)}, u32[]{:S(2)}, u32[]{:S(2)}) async-start(bf16[8,112,768]{2,1,0:T(8,128)(2,1)} %bitcast.171), calls=%async_computation.2 | async-start | bytes 2752512 | tf_op jit(solution)/shard_map/all_to_all | solution.py:881
  102.7 124.1 %all-gather.8.cloned.1.call-start = ((), (), s32[]{:S(2)}) async-start(), calls=%async_computation.16 | async-start | bytes 11796480 | tf_op jit(solution)/shard_map/all_gather | solution.py:910
  135.7 32.5 %all-to-all-start.3 = ((bf16[8,96,768]{2,1,0:T(8,128)(2,1)}), bf16[8,96,768]{2,1,0:T(8,128)(2,1)S(1)}, u32[]{:S(2)}, u32[]{:S(2)}) async-start(bf16[8,96,768]{2,1,0:T(8,128)(2,1)} %send_noted.1), calls=%async_computation.3 | async-start | bytes 2359296 | tf_op jit(solution)/shard_map/all_to_all | solution.py:881
  139.4 133.8 %all-gather.6.cloned.1.call-start = ((), (), s32[]{:S(2)}) async-start(), calls=%async_computation.15 | async-start | bytes 4423680 | tf_op jit(solution)/shard_map/all_gather | solution.py:895
  169.7 53.0 %all-to-all-start.5 = ((bf16[8,160,768]{2,1,0:T(8,128)(2,1)}), bf16[8,160,768]{2,1,0:T(8,128)(2,1)}, u32[]{:S(2)}, u32[]{:S(2)}) async-start(bf16[8,160,768]{2,1,0:T(8,128)(2,1)} %bitcast.161), calls=%async_computation.5 | async-start | bytes 3932160 | tf_op jit(solution)/shard_map/all_to_all | solution.py:857
  222.7 50.4 %all-to-all-start.4 = ((bf16[8,160,768]{2,1,0:T(8,128)(2,1)}), bf16[8,160,768]{2,1,0:T(8,128)(2,1)S(1)}, u32[]{:S(2)}, u32[]{:S(2)}) async-start(bf16[8,160,768]{2,1,0:T(8,128)(2,1)} %bitcast.25), calls=%async_computation.4 | async-start | bytes 3932160 | tf_op jit(solution)/shard_map/all_to_all | solution.py:857
  226.3 105.5 %reduce-scatter.3.cloned.1.call-start = ((), (), s32[]{:S(2)}) async-start(), calls=%async_computation.17 | async-start | bytes 5898240 | tf_op jit(solution)/shard_map/reduce_scatter | solution.py:960
  275.7 56.0 %all-to-all-start.6 = ((bf16[8,160,768]{2,1,0:T(8,128)(2,1)}), bf16[8,160,768]{2,1,0:T(8,128)(2,1)S(1)}, u32[]{:S(2)}, u32[]{:S(2)}) async-start(bf16[8,160,768]{2,1,0:T(8,128)(2,1)} %bitcast.170), calls=%async_computation.6 | async-start | bytes 3932160 | tf_op jit(solution)/shard_map/all_to_all | solution.py:857
  281.8 47.2 %collective-permute-start.20 = (bf16[192,3072]{1,0:T(8,128)(2,1)}, bf16[192,3072]{1,0:T(8,128)(2,1)}, u32[]{:S(2)}, u32[]{:S(2)}) collective-permute-start(bf16[192,3072]{1,0:T(8,128)(2,1)} %get-tuple-element.294), channel_id=1, source_target_pairs={{0,8},{8,0},{16,24},{24,16},{1,9},{9,1},{17,25},{25,17},{2,10},{10... | collective-permute-start | bytes 3538952 | tf_op jit(solution)/shard_map/ppermute | solution.py:791
  331.8 52.2 %all-to-all-start.7 = ((bf16[8,160,768]{2,1,0:T(8,128)(2,1)}), bf16[8,160,768]{2,1,0:T(8,128)(2,1)}, u32[]{:S(2)}, u32[]{:S(2)}) async-start(bf16[8,160,768]{2,1,0:T(8,128)(2,1)} %bitcast.169), calls=%async_computation.8 | async-start | bytes 3932160 | tf_op jit(solution)/shard_map/all_to_all | solution.py:857
  337.9 161.1 %reduce-scatter.5.cloned.1.call-start = ((), (), s32[]{:S(2)}) async-start(), calls=%async_computation.18 | async-start | bytes 5898240 | tf_op jit(solution)/shard_map/reduce_scatter | solution.py:969
  395.5 61.8 %all-to-all-start.8 = ((bf16[8,160,768]{2,1,0:T(8,128)(2,1)}), bf16[8,160,768]{2,1,0:T(8,128)(2,1)S(1)}, u32[]{:S(2)}, u32[]{:S(2)}) async-start(bf16[8,160,768]{2,1,0:T(8,128)(2,1)} %bitcast.167), calls=%async_computation.10 | async-start | bytes 3932160 | tf_op jit(solution)/shard_map/all_to_all | solution.py:857
  457.3 53.1 %all-to-all-start.9 = ((bf16[8,160,768]{2,1,0:T(8,128)(2,1)}), bf16[8,160,768]{2,1,0:T(8,128)(2,1)}, u32[]{:S(2)}, u32[]{:S(2)}) async-start(bf16[8,160,768]{2,1,0:T(8,128)(2,1)} %bitcast.162), calls=%async_computation.11 | async-start | bytes 3932160 | tf_op jit(solution)/shard_map/all_to_all | solution.py:857
  464.7 34.3 %collective-permute-start.31 = (bf16[192,3072]{1,0:T(8,128)(2,1)S(1)}, bf16[192,3072]{1,0:T(8,128)(2,1)}, u32[]{:S(2)}, u32[]{:S(2)}) collective-permute-start(bf16[192,3072]{1,0:T(8,128)(2,1)S(1)} %copy-done.21), channel_id=1, source_target_pairs={{0,16},{8,24},{16,0},{24,8},{1,17},{9,25},{17,1},{25,9},{2,18},{10... | collective-permute-start | bytes 3538952 | tf_op jit(solution)/shard_map/ppermute | solution.py:791
  512.8 36.6 %all-to-all-start.10 = ((bf16[32,78,192]{2,1,0:T(8,128)(2,1)}), bf16[32,78,192]{2,1,0:T(8,128)(2,1)S(1)}, u32[]{:S(2)}, u32[]{:S(2)}) async-start(bf16[32,78,192]{2,1,0:T(8,128)(2,1)} %reshape.234), calls=%async_computation.12 | async-start | bytes 2621440 | tf_op jit(solution)/shard_map/all_to_all | solution.py:994
  516.2 40.0 %collective-permute-start.37 = (bf16[192,3072]{1,0:T(8,128)(2,1)}, bf16[192,3072]{1,0:T(8,128)(2,1)}, u32[]{:S(2)}, u32[]{:S(2)}) collective-permute-start(bf16[192,3072]{1,0:T(8,128)(2,1)} %get-tuple-element.375), channel_id=1, source_target_pairs={{0,8},{8,0},{16,24},{24,16},{1,9},{9,1},{17,25},{25,17},{2,10},{10... | collective-permute-start | bytes 3538952 | tf_op jit(solution)/shard_map/ppermute | solution.py:791
  516.5 33.1 %collective-permute-start.33 = (bf16[576,640]{1,0:T(8,128)(2,1)}, bf16[576,640]{1,0:T(8,128)(2,1)}, u32[]{:S(2)}, u32[]{:S(2)}) collective-permute-start(bf16[576,640]{1,0:T(8,128)(2,1)} %get-tuple-element.352), channel_id=1, source_target_pairs={{0,16},{8,24},{16,0},{24,8},{1,17},{9,25},{17,1},{25,9},{2,18},{10... | collective-permute-start | bytes 2211848 | tf_op jit(solution)/shard_map/ppermute | solution.py:791
  520.4 38.1 %collective-permute-start.38 = (bf16[192,3072]{1,0:T(8,128)(2,1)}, bf16[192,3072]{1,0:T(8,128)(2,1)}, u32[]{:S(2)}, u32[]{:S(2)}) collective-permute-start(bf16[192,3072]{1,0:T(8,128)(2,1)} %get-tuple-element.378), channel_id=1, source_target_pairs={{0,8},{8,0},{16,24},{24,16},{1,9},{9,1},{17,25},{25,17},{2,10},{10... | collective-permute-start | bytes 3538952 | tf_op jit(solution)/shard_map/ppermute | solution.py:791
  551.1 43.4 %all-to-all-start.11 = ((bf16[8,4,78,192]{3,1,2,0:T(4,128)(2,1)}), bf16[8,4,78,192]{3,1,2,0:T(4,128)(2,1)S(1)}, u32[]{:S(2)}, u32[]{:S(2)}) async-start(bf16[8,4,78,192]{3,1,2,0:T(4,128)(2,1)} %broadcast_in_dim.93), calls=%async_computation.13 | async-start | bytes 2555904 | tf_op jit(solution)/shard_map/all_to_all | solution.py:1049
  560.7 38.8 %collective-permute-start.36 = (bf16[192,768]{1,0:T(8,128)(2,1)S(1)}, bf16[192,768]{1,0:T(8,128)(2,1)S(1)}, u32[]{:S(2)}, u32[]{:S(2)}) collective-permute-start(bf16[192,768]{1,0:T(8,128)(2,1)S(1)} %add_convert_fusion.3), channel_id=1, source_target_pairs={{0,4},{1,5},{2,6},{3,7},{4,0},{5,1},{6,2},{7,3},{8,12},{9,13},{10,... | collective-permute-start | bytes 884744 | tf_op jit(solution)/shard_map/ppermute | solution.py:791
  (83 other events, 1252.3 us)
Sparse Core Ops, SparseCore 0:
  52.1 70.7 all-gather.3
  135.8 62.3 all-gather.7
  199.8 30.7 all-gather.5
  273.3 49.4 reduce-scatter.2
  341.7 51.3 reduce-scatter.4
